TPU v7x, 128 devices: a whole 4x4x4 slice. The times are simulated.
128 devices in a mesh: src: 4 (over y), gz: 32 (over x, z, core).
Axes of the slice: x: 4, y: 4, z: 4, core: 2. Of those that a mesh axis runs over, the one named last changes fastest.
Arguments:
- fields_e: float32 [4, 3, 8, 256, 4096], P('src', None, None, None, 'gz'), may hold values from -12 to 12
- fields_h: float32 [4, 3, 8, 256, 4096], P('src', None, None, None, 'gz'), may hold values from -0.0007324219 to 0.0007324219
- cot_e: float32 [4, 3, 8, 256, 4096], P('src', None, None, None, 'gz'), may hold values from -6 to 6
- cot_h: float32 [4, 3, 8, 256, 4096], P('src', None, None, None, 'gz'), may hold values from -6 to 6
- labels: int32 [8, 256, 4096], P(None, None, 'gz'), may hold values from 0 to 3
- region_eps: float32 [4], replicated, may hold values from 1 to 12
- angle_index: int32 [4], P('src'), may hold values from 0 to 7
- profiles: float32 [8, 2, 8, 256], replicated, may hold values from -6 to 6
- zsheet: float32 [4096], P('gz'), may hold values from -0.0007324219 to 0.0007324219
- layer_term: float32 [4096], P('gz'), as said below
- block_inverse: float32 [4096, 128], P('gz'), as said below
Outputs:
- e_new: float32 [4, 3, 8, 256, 4096], P('src', None, None, None, 'gz')
- h_new: float32 [4, 3, 8, 256, 4096], P('src', None, None, None, 'gz')
- eps_grad: float32 [8, 256, 4096], P(None, None, 'gz')
Inputs may be any that keep to these rules, and one draw needn't show every extreme that they name: `layer_term`: each value is between 1 / (256 * 128^2) and 8 / (256 * 128^2). `block_inverse`: each block of 128 rows is symmetric with positive entries; with the couplings of the steps the matrix M is symmetric positive definite.
All inputs are finite; a program needn't handle non-finite values.
Results may differ from a plain program's by a relative error of at most 0.0003.
Values sent between devices are 32-bit elements; how exact they have to be, the bound alone decides.
No kernel may reach another device: no remote copies, remote signals or barrier semaphores. Data moves between devices by JAX's collectives and lax.ppermute only.
A program may use at most 128 MiB of HBM per device.

v0:
```python
import jax
import jax.numpy as jnp
from jax import lax
from jax.sharding import PartitionSpec as P

REGIONS = 4
ANGLES = 8


HIGH = lax.Precision.HIGHEST


def prefix(x, axis, combine, identity, reverse):
    peers, here = (lax.axis_size(axis), lax.axis_index(axis))
    everything = jax.tree.map(lambda part: lax.all_gather(part, axis), x)
    start = jax.tree.map(
        lambda part, zero: jnp.broadcast_to(jnp.asarray(zero, part.dtype), part.shape), x, identity
    )

    def step(k, before):
        at = peers - 1 - k if reverse else k
        reached = at > here if reverse else at < here
        new = combine(before, jax.tree.map(lambda part: part[at], everything))
        return jax.tree.map(lambda a, b: jnp.where(reached, a, b), new, before)

    return lax.fori_loop(0, peers, step, start)


def shifted(block, axis, distance):
    devices = range(lax.axis_size(axis))
    route = [(i - distance, i) for i in devices if i - distance in devices]
    return lax.ppermute(block, axis, route)


def step_up(values, axis_id):
    axis_id = axis_id % values.ndim
    length = values.shape[axis_id]
    tail = lax.slice_in_dim(values, 1, length, axis=axis_id)
    zero_rim = jnp.zeros_like(lax.slice_in_dim(values, 0, 1, axis=axis_id))
    return jnp.concatenate([tail, zero_rim], axis_id) - values


def step_down(values, axis_id):
    axis_id = axis_id % values.ndim
    length = values.shape[axis_id]
    head = lax.slice_in_dim(values, 0, length - 1, axis=axis_id)
    zero_rim = jnp.zeros_like(lax.slice_in_dim(values, 0, 1, axis=axis_id))
    return values - jnp.concatenate([zero_rim, head], axis_id)


def z_down(values, below):
    return values - jnp.concatenate([below[..., None], values[..., :-1]], -1)


def z_up(values, above):
    return jnp.concatenate([values[..., 1:], above[..., None]], -1) - values


def chain_terms(corners):

    def advance(q_carry, corner_row):
        denom = 1.0 - corner_row[0] * q_carry
        q_next = corner_row[3] + corner_row[1] * q_carry * corner_row[2] / denom
        return (q_next, (q_carry, denom))

    unused, (q_prev, denom) = lax.scan(advance, jnp.zeros((), corners.dtype), corners)
    return (q_prev, denom)


def compose(earlier, later):
    return (later[0] * earlier[0], later[1] + later[0] * earlier[1])


def solve_block(stacked, block_inverse):
    local = jnp.einsum("cxyz,wz->cxyw", stacked, block_inverse, precision=HIGH)
    first_vals = local[..., 0]
    last_vals = local[..., -1]
    corners = jnp.stack(
        [block_inverse[0, 0], block_inverse[-1, 0], block_inverse[0, -1], block_inverse[-1, -1]]
    )
    own_index = lax.axis_index("gz")
    all_corners = lax.all_gather(corners[None], "gz", axis=0, tiled=True)
    q_all, den_all = chain_terms(all_corners)
    q_prev = q_all[own_index]
    denom = den_all[own_index]
    mult = corners[1] / denom
    offset = last_vals + corners[1] * q_prev / denom * first_vals
    start = (jnp.float32(1.0), jnp.zeros_like(offset))
    unused, p_prev = prefix((mult, offset), "gz", compose, start, False)
    gain = (first_vals + corners[0] * p_prev) / denom
    slope = corners[2] / denom
    unused2, t_next = prefix((slope, gain), "gz", compose, start, True)
    t_self = gain + slope * t_next
    b_prev = p_prev + q_prev * t_self
    return (
        local + block_inverse[:, 0] * b_prev[..., None] + block_inverse[:, -1] * t_next[..., None]
    )


def body(
    fields_e,
    fields_h,
    cot_e,
    cot_h,
    labels,
    region_eps,
    angle_index,
    profiles,
    zsheet,
    layer_term,
    block_inverse,
):
    permit = jnp.zeros(labels.shape, jnp.float32)
    for region in range(REGIONS):
        permit = permit + jnp.where(labels == region, region_eps[region], jnp.float32(0.0))
    inv_eps = 1.0 / permit
    picker = (angle_index[0] == jnp.arange(ANGLES, dtype=jnp.int32)).astype(jnp.float32)
    chosen = jnp.einsum("a,acxy->cxy", picker, profiles, precision=HIGH)
    current = chosen[..., None] * zsheet
    e_x, e_y, e_z = (fields_e[0, 0], fields_e[0, 1], fields_e[0, 2])
    h_x, h_y, h_z = (fields_h[0, 0], fields_h[0, 1], fields_h[0, 2])
    g_ex, g_ey, g_ez = (cot_e[0, 0], cot_e[0, 1], cot_e[0, 2])
    g_hx, g_hy, g_hz = (cot_h[0, 0], cot_h[0, 1], cot_h[0, 2])
    scaled_gez = inv_eps * g_ez
    bar_hy = g_hy - step_up(scaled_gez, -3)
    bar_hx = g_hx + step_up(scaled_gez, -2)
    top_planes = jnp.stack([h_x[..., -1], h_y[..., -1], bar_hx[..., -1], bar_hy[..., -1]])
    below = shifted(top_planes, "gz", 1)
    p_x = step_down(h_z, -2) - z_down(h_y, below[1]) - current[0]
    p_y = z_down(h_x, below[0]) - step_down(h_z, -3) - current[1]
    rhs_x = layer_term * e_x + inv_eps * p_x
    rhs_y = layer_term * e_y + inv_eps * p_y
    adj_x = g_ex - step_down(g_hz, -2) - z_down(bar_hy, below[3])
    adj_y = g_ey + step_down(g_hz, -3) - z_down(bar_hx, below[2])
    solved = solve_block(jnp.stack([rhs_x, rhs_y, adj_x, adj_y]), block_inverse)
    new_ex, new_ey, lam_x, lam_y = (solved[0], solved[1], solved[2], solved[3])
    above = shifted(jnp.stack([new_ex[..., 0], new_ey[..., 0]]), "gz", -1)
    new_hy = h_y + z_up(new_ex, above[0]) - step_up(e_z, -3)
    new_hx = h_x + z_up(new_ey, above[1]) - step_up(e_z, -2)
    curl_z = step_down(new_hy, -3) - step_down(new_hx, -2)
    new_ez = e_z + inv_eps * curl_z
    new_hz = h_z - step_up(new_ey, -3) + step_up(new_ex, -2)
    grad_terms = g_ez * curl_z + lam_x * p_x + lam_y * p_y
    summed = lax.psum(grad_terms, "src")
    eps_grad = -inv_eps * inv_eps * summed
    e_new = jnp.stack([new_ex, new_ey, new_ez])[None]
    h_new = jnp.stack([new_hx, new_hy, new_hz])[None]
    return (e_new, h_new, eps_grad)


def solution(mesh):
    return jax.shard_map(
        body,
        mesh=mesh,
        in_specs=(
            P("src", None, None, None, "gz"),
            P("src", None, None, None, "gz"),
            P("src", None, None, None, "gz"),
            P("src", None, None, None, "gz"),
            P(None, None, "gz"),
            P(),
            P("src"),
            P(),
            P("gz"),
            P("gz"),
            P("gz", None),
        ),
        out_specs=(
            P("src", None, None, None, "gz"),
            P("src", None, None, None, "gz"),
            P(None, None, "gz"),
        ),
        check_vma=False,
    )
```

profile of v0, /device:TPU:1, one launch (start us, length us, event | category | flops | bytes accessed | tf_op | source)
XLA Modules:
  0.0 566.5 jit_solution(10452365806152419086)
XLA Ops:
  8.7 4.6 bitcast_multiply_fusion.2
  18.5 4.9 collective-permute-start
  28.3 2.6 maximum_dynamic-update-slice_fusion
  30.9 62.0 %all-reduce.12 = f32[128]{0:T(128)S(1)} all-reduce(f32[128]{0:T(128)S(1)} %maximum_dynamic-update-slice_fusion), channel_id=2, replica_groups=mesh['src'=4,'gz'=32] {'gz'}, use_global_device_ids=true, to_apply=%add.12 | all-reduce | flops 128 | bytes 1024
  93.0 108.9 %while.44 = (s32[]{:T(128)}, f32[]{:T(128)}, f32[32]{0:T(128)S(1)}, f32[32]{0:T(128)S(1)}, f32[32,4]{1,0:T(8,128)S(1)}, /*index=5*/s32[]{:T(128)}, f32[]{:T(128)}) while((s32[]{:T(128)}, f32[]{:T(128)}, f32[32]{0:T(128)S(1)}, f32[32]{0:T(128)S(1)}, f32[32,4]{1,0:T(8,128)S(1)}, /*index=5*/s32[]{:T(128)}, f32[]{:T(128)}) %tuple.128), condition=%wide.region_1.2_spmd, body=%wide.region_0.1_spmd.sunk | while | flops 8 | bytes 257 | solution.py:66
  203.8 2.2 slice_bitcast_fusion.13
  214.7 7.7 %fusion.28 = (f32[1,8,256,128]{3,2,1,0:T(8,128)S(1)}, f32[8,256,128]{2,1,0:T(8,128)}) fusion(f32[1,3,8,256,128]{4,3,2,1,0:T(8,128)} %param.17, f32[128]{0:T(128)S(1)} %copy-done.32, f32[]{:T(128)} %bitcast.10, s32[8,256,128]{2,1,0:T(8,128)} %param.21, f32[]{:T(128)} %bitcast.9, f32[]{:T(128)} %bitcast.8, f32[]{:T(128)} %bitcast.7, ...), kind=kLoop, calls=%fused_computation.56 | loop fusion | flops 5242880 | bytes 9306640 | tf_op jit(solution)/shard_map/stack | solution.py:135
  222.5 6.9 %fusion.30 = (f32[1,8,256,128]{3,2,1,0:T(8,128)S(1)}, f32[8,256,128]{2,1,0:T(8,128)}) fusion(f32[1,3,8,256,128]{4,3,2,1,0:T(8,128)} %param.17, f32[128]{0:T(128)S(1)} %copy-done.32, f32[]{:T(128)} %bitcast.10, s32[8,256,128]{2,1,0:T(8,128)S(1)} %copy-done.10, f32[]{:T(128)} %bitcast.9, f32[]{:T(128)} %bitcast.8, f32[]{:T(128)} %bitcast.7, ...), kind=kLoop, calls=%fused_computation.63 | loop fusion | flops 5242880 | bytes 9433616 | tf_op jit(solution)/shard_map/stack | solution.py:135
  229.4 2.5 fusion.20
  231.9 4.2 fusion.2
  236.1 2.0 copy-done.5
  242.8 66.4 %all-reduce.15 = (f32[32]{0:T(128)S(1)}, f32[32]{0:T(128)S(1)}) all-reduce(f32[32]{0:T(128)S(1)} %dynamic-update-slice.1, f32[32]{0:T(128)S(1)} %dynamic-update-slice.2), channel_id=1, replica_groups=mesh['src'=4,'gz'=32] {'gz'}, use_global_device_ids=true, to_apply=%add.13 | all-reduce | flops 64 | bytes 512
  309.2 63.9 %while.45 = (s32[]{:T(128)}, f32[4,8,256]{2,1,0:T(8,128)S(1)}, s32[]{:T(128)}, f32[32,4,8,256]{3,2,1,0:T(8,128)}, f32[32]{0:T(128)S(1)}, /*index=5*/s32[]{:T(128)}, s32[]{:T(128)}) while((s32[]{:T(128)}, f32[4,8,256]{2,1,0:T(8,128)S(1)}, s32[]{:T(128)}, f32[32,4,8,256]{3,2,1,0:T(8,128)}, f32[32]{0:T(128)S(1)}, ...), condition=%wide.region_3.4_spmd.clone, body=%wide.region_2.3_spmd.clone.sunk | while | flops 32772 | bytes 98429 | solution.py:26
  377.6 2.2 slice_bitcast_fusion.12
  379.8 5.4 copy.158
  385.2 29.7 %all-gather.8.cloned.1.call-done = f32[128,8,256]{2,1,0:T(8,128)} async-done(((f32[4,8,256]{2,1,0:T(8,128)}), f32[128,8,256]{2,1,0:T(8,128)}) %all-gather.8.cloned.1.call-update) | async-done | bytes 1048592 | tf_op jit(solution)/shard_map/all_gather | solution.py:15
  414.9 67.0 %while.46 = (s32[]{:T(128)}, f32[4,8,256]{2,1,0:T(8,128)S(1)}, s32[]{:T(128)}, f32[32,4,8,256]{3,2,1,0:T(8,128)}, f32[32]{0:T(128)S(1)}, /*index=5*/s32[]{:T(128)}, s32[]{:T(128)}, s32[]{:T(128)}, s32[]{:T(128)}) while((s32[]{:T(128)}, f32[4,8,256]{2,1,0:T(8,128)S(1)}, s32[]{:T(128)}, f32[32,4,8,256]{3,2,1,0:T(8,128)}, ...), condition=%wide.region_5.6_spmd.clone, body=%wide.region_4.5_spmd.clone.sunk | while | flops 32776 | bytes 98491 | solution.py:26
  482.5 4.4 multiply_add_fusion
  487.8 2.4 collective-permute-start.1
  497.6 6.9 %fusion.24 = (f32[8,256,128]{2,1,0:T(8,128)S(1)}, f32[8,256,128]{2,1,0:T(8,128)S(1)}, f32[1,8,256,128]{3,2,1,0:T(8,128)}) fusion(f32[8,256,1]{2,1,0:T(8,128)} %copy.159, f32[8,256,127]{2,1,0:T(8,128)} %slice.302, f32[7,256,128]{2,1,0:T(8,128)} %slice_bitcast_fusion.12, f32[1,3,8,256,128]{4,3,2,1,0:T(8,128)S(1)} %copy-done.4, ...), kind=kLoop, calls=%fused_computation.48 | loop fusion | flops 3670016 | bytes 15458304 | tf_op jit(solution)/shard_map/sub | solution.py:138
  504.6 3.9 fusion.12
  510.1 3.2 maximum_bitcast_fusion.1
  513.3 38.9 %all-reduce.18.cloned.1.call-done = f32[8,256,128]{2,1,0:T(8,128)} async-done(((f32[8,256,128]{2,1,0:T(8,128)}), f32[8,256,128]{2,1,0:T(8,128)}) %all-reduce.18.cloned.1.call-update) | async-done | bytes 1048592 | tf_op jit(solution)/shard_map/psum | solution.py:144
  552.2 5.9 %fusion.10 = (f32[8,256,128]{2,1,0:T(8,128)}, f32[1,8,256,128]{3,2,1,0:T(8,128)S(1)}) fusion(f32[8,256,128]{2,1,0:T(8,128)} %all-reduce.18.cloned.1.call-done, f32[]{:T(128)} %bitcast.10, s32[8,256,128]{2,1,0:T(8,128)S(1)} %copy-done.11, f32[]{:T(128)} %bitcast.9, f32[]{:T(128)} %bitcast.8, f32[]{:T(128)} %bitcast.7, f32[8,256,128]{2,1,0:T(8,128)} %get-tuple-element.396, ...), kind=kLoop, calls=%fused_computation.17 | loop fusion | flops 4456448 | bytes 6291472 | tf_op jit(solution)/shard_map/mul | solution.py:145
  (388 shorter events, 196.8 us)
Async XLA Ops:
  7.2 19.0 %copy-start = (f32[8,2,8,256]{3,2,1,0:T(8,128)S(1)}, f32[8,2,8,256]{3,2,1,0:T(8,128)}, u32[]{:S(2)}) copy-start(f32[8,2,8,256]{3,2,1,0:T(8,128)} %param.24) | copy-start | bytes 393220
  7.2 302.0 %all-gather.6.cloned.1.call-start = ((), (), s32[]{:S(2)}) async-start(), calls=%async_computation.1 | async-start | bytes 1081344 | tf_op jit(solution)/shard_map/all_gather | solution.py:15
  16.1 9.5 %copy-start.6 = (f32[8,256,128]{2,1,0:T(8,128)}, f32[8,256,128]{2,1,0:T(8,128)S(1)}, u32[]{:S(2)}) copy-start(f32[8,256,128]{2,1,0:T(8,128)S(1)} %get-tuple-element.414) | copy-start | bytes 3145732
  16.1 9.5 %copy-start.8 = (f32[8,256,128]{2,1,0:T(8,128)}, f32[8,256,128]{2,1,0:T(8,128)S(1)}, u32[]{:S(2)}) copy-start(f32[8,256,128]{2,1,0:T(8,128)S(1)} %get-tuple-element.415) | copy-start | bytes 3145732
  17.3 9.2 %copy-start.30 = (f32[128,128]{1,0:T(8,128)S(1)}, f32[128,128]{1,0:T(8,128)}, u32[]{:S(2)}) copy-start(f32[128,128]{1,0:T(8,128)} %param.27) | copy-start | bytes 196612
  17.3 9.8 %copy-start.34 = (u32[128]{0:T(128)S(1)}, u32[128]{0:T(128)}, u32[]{:S(2)}) copy-start(u32[128]{0:T(128)} %constant.127) | copy-start | bytes 1540
  17.3 184.6 %copy-start.33 = (f32[128]{0:T(128)S(1)}, f32[128]{0:T(128)}, u32[]{:S(2)}) copy-start(f32[128]{0:T(128)} %param.25) | copy-start | bytes 1540
  18.5 190.6 %collective-permute-start = (f32[4,8,256]{2,1,0:T(8,128)S(1)}, f32[4,8,256]{2,1,0:T(8,128)S(1)}, u32[]{:S(2)}, u32[]{:S(2)}) collective-permute-start(f32[4,8,256]{2,1,0:T(8,128)S(1)} %pad_maximum_fusion), channel_id=1, source_target_pairs={{0,1},{1,2},{2,3},{3,4},{4,5},{5,6},{6,7},{7,8},{8,9},{9,10},{10,1... | collective-permute-start | bytes 98312 | tf_op jit(solution)/shard_map/ppermute | solution.py:32
  203.8 10.9 %copy-start.32 = (f32[128]{0:T(128)S(1)}, f32[128]{0:T(128)}, u32[]{:S(2)}) copy-start(f32[128]{0:T(128)} %param.26) | copy-start | bytes 1540
  214.7 7.7 %copy-start.10 = (s32[8,256,128]{2,1,0:T(8,128)S(1)}, s32[8,256,128]{2,1,0:T(8,128)}, u32[]{:S(2)}) copy-start(s32[8,256,128]{2,1,0:T(8,128)} %param.21) | copy-start | bytes 3145732
  214.7 7.7 %copy-start.17 = (f32[8,256,128]{2,1,0:T(8,128)S(1)}, f32[8,256,128]{2,1,0:T(8,128)}, u32[]{:S(2)}) copy-start(f32[8,256,128]{2,1,0:T(8,128)} %copy-done.16) | copy-start | bytes 3145732
  214.7 7.7 %copy-start.19 = (f32[2,8,256,128]{3,2,1,0:T(8,128)S(1)}, f32[2,8,256,128]{3,2,1,0:T(8,128)}, u32[]{:S(2)}) copy-start(f32[2,8,256,128]{3,2,1,0:T(8,128)} %broadcast_multiply_fusion) | copy-start | bytes 6291460
  214.7 7.7 %copy-start.25 = (f32[8,256,1]{2,1,0:T(8,128)S(1)}, f32[8,256,1]{2,1,0:T(8,128)}, u32[]{:S(2)}) copy-start(f32[8,256,1]{2,1,0:T(8,128)} %copy.151) | copy-start | bytes 24580
  214.7 7.7 %copy-start.26 = (f32[8,256,128]{2,1,0:T(8,128)S(1)}, f32[8,256,128]{2,1,0:T(8,128)}, u32[]{:S(2)}) copy-start(f32[8,256,128]{2,1,0:T(8,128)} %get-tuple-element.416) | copy-start | bytes 3145732
  222.4 6.9 %copy-start.7 = (f32[8,256,128]{2,1,0:T(8,128)S(1)}, f32[8,256,128]{2,1,0:T(8,128)}, u32[]{:S(2)}) copy-start(f32[8,256,128]{2,1,0:T(8,128)} %copy-done.6) | copy-start | bytes 3145732
  222.4 6.9 %copy-start.9 = (f32[8,256,128]{2,1,0:T(8,128)S(1)}, f32[8,256,128]{2,1,0:T(8,128)}, u32[]{:S(2)}) copy-start(f32[8,256,128]{2,1,0:T(8,128)} %copy-done.8) | copy-start | bytes 3145732
  238.8 176.1 %all-gather.8.cloned.1.call-start = ((), (), s32[]{:S(2)}) async-start(), calls=%async_computation.2 | async-start | bytes 1081344 | tf_op jit(solution)/shard_map/all_gather | solution.py:15
  375.0 177.2 %all-reduce.18.cloned.1.call-start = ((), (), s32[]{:S(2)}) async-start(), calls=%async_computation | async-start | bytes 2097152 | tf_op jit(solution)/shard_map/psum | solution.py:144
  379.8 102.1 %copy-start.31 = (f32[4,8,256]{2,1,0:T(8,128)S(1)}, f32[4,8,256]{2,1,0:T(8,128)}, u32[]{:S(2)}) copy-start(f32[4,8,256]{2,1,0:T(8,128)} %fusion.34) | copy-start | bytes 98308
  487.8 7.1 %collective-permute-start.1 = (f32[2,8,256]{2,1,0:T(8,128)S(1)}, f32[2,8,256]{2,1,0:T(8,128)S(1)}, u32[]{:S(2)}, u32[]{:S(2)}) collective-permute-start(f32[2,8,256]{2,1,0:T(8,128)S(1)} %pad_maximum_fusion.1), channel_id=1, source_target_pairs={{1,0},{2,1},{3,2},{4,3},{5,4},{6,5},{7,6},{8,7},{9,8},{10,9},{11,1... | collective-permute-start | bytes 49160 | tf_op jit(solution)/shard_map/ppermute | solution.py:32
  497.6 7.0 %copy-start.3 = (f32[4,8,256,128]{3,2,1,0:T(8,128)S(1)}, f32[4,8,256,128]{3,2,1,0:T(8,128)}, u32[]{:S(2)}) copy-start(f32[4,8,256,128]{3,2,1,0:T(8,128)} %copy-done.2) | copy-start | bytes 12582916
  497.6 7.0 %copy-start.27 = (f32[8,256,128]{2,1,0:T(8,128)S(1)}, f32[8,256,128]{2,1,0:T(8,128)}, u32[]{:S(2)}) copy-start(f32[8,256,128]{2,1,0:T(8,128)} %get-tuple-element.400) | copy-start | bytes 3145732
  497.6 7.0 %copy-start.28 = (f32[8,256,128]{2,1,0:T(8,128)S(1)}, f32[8,256,128]{2,1,0:T(8,128)}, u32[]{:S(2)}) copy-start(f32[8,256,128]{2,1,0:T(8,128)} %get-tuple-element.398) | copy-start | bytes 3145732
  510.1 42.1 %copy-start.11 = (s32[8,256,128]{2,1,0:T(8,128)S(1)}, s32[8,256,128]{2,1,0:T(8,128)}, u32[]{:S(2)}) copy-start(s32[8,256,128]{2,1,0:T(8,128)} %param.21) | copy-start | bytes 3145732
  (17 other events, 68.5 us)
Sparse Core Ops, SparseCore 0:
  238.9 43.4 all-gather.5
  375.1 39.7 all-gather.7
  508.7 43.4 all-reduce.17
where the time goes:
time: 574 us; the launch traced here: 567 us
  other arithmetic  147 us (26%)
  blocking collectives  128 us (22%)
  local copies, waits for them, and re-layouts  109 us (19%)
  loops' own time  80.9 us (14%)
  waiting for transfers between devices  68.7 us (12%)
  between operations  19.9 us (3%)
  starting transfers between devices  7.42 us (1%)
    unnamed x2, blocking collectives  128 us
    select_n x64, other arithmetic, step(): return jax.tree.map(lambda a, b: jnp.where(reached, a, b), new, before)  91.4 us
    another operation x1, loops' own time, chain_terms(): lax.scan(advance, jnp.zeros((), corners.dtype), corners)  80.8 us
    dynamic_slice x64, local copies, waits for them, and re-layouts, step(): new = combine(before, jax.tree.map(lambda part: part[at], everything))  39.4 us
    psum x1, waiting for transfers between devices, body(): summed = lax.psum(grad_terms, 'src')  38.9 us
    all_gather x2, waiting for transfers between devices, prefix(): everything = jax.tree.map(lambda part: lax.all_gather(part, axis), x)  29.7 us
    slice x32, local copies, waits for them, and re-layouts, advance(): denom = 1.0 - corner_row[0] * q_carry  20.9 us
    another operation x3, other arithmetic, body(): solved = solve_block(jnp.stack([rhs_x, rhs_y, adj_x, adj_y]), block_inverse)  17 us
  transfers between devices with their start and end apart: 5, of which 2 were waited for; matrix products, arithmetic and copies ran while one was open for 10% of the time, Pallas kernels for 0%

commit v1 on v0

v1 whole, which is shorter than its diff:
```python
import jax
import jax.numpy as jnp
from jax import lax
from jax.experimental import pallas as pl
from jax.experimental.pallas import tpu as pltpu
from jax.sharding import PartitionSpec as P

F32 = jnp.float32
BF = jnp.bfloat16
X, Y, CZ = 8, 256, 128
NN = (((1,), (0,)), ((), ()))
NT = (((1,), (1,)), ((), ()))
SLABS = 17
LIMIT = 40 * 1024 * 1024


def split(v):
    one = v.astype(BF)
    rest = v - one.astype(F32)
    two = rest.astype(BF)
    three = (rest - two.astype(F32)).astype(BF)
    return one, two, three


def mm(a, b, dims=NN):
    return lax.dot_general(a, b, dims, preferred_element_type=F32)


def iota(shape, axis):
    return lax.broadcasted_iota(jnp.int32, shape, axis)


def y_down(v):
    return v - jnp.where(iota(v.shape, 0) == 0, 0.0, pltpu.roll(v, 1, 0))


def y_up(v):
    n = v.shape[0]
    return jnp.where(iota(v.shape, 0) == n - 1, 0.0, pltpu.roll(v, n - 1, 0)) - v


def z_down(v):
    return v - jnp.where(iota(v.shape, 1) == 0, 0.0, pltpu.roll(v, 1, 1))


def z_up(v):
    n = v.shape[1]
    return jnp.where(iota(v.shape, 1) == n - 1, 0.0, pltpu.roll(v, n - 1, 1)) - v


def inverse_eps(labels, eps_ref):
    rows = [1.0 / jnp.full((1, CZ), eps_ref[r], F32) for r in range(4)]
    out = jnp.where(labels == 2, rows[2], rows[3])
    out = jnp.where(labels == 1, rows[1], out)
    return jnp.where(labels == 0, rows[0], out)


def six_rows(rows):
    one, two, three = (part.astype(F32) for part in split(rows))
    return [one, two, three, one, two, one]


def six_table(line, piece):
    one, two, three = (part.astype(F32) for part in split(line))
    return jnp.where(piece < 3, one, jnp.where(piece < 5, two, three))


def rhs_kernel(
    angle, eps, e, h, ge, gh, lab, ge_next, lab_next, prof, zs, lt, w,
    rx_o, ry_o, ax_o, ay_o, psx_o, psy_o, keep_o, send_o,
    hz_s, ghz_s, prof_s,
):
    i = pl.program_id(0)
    core = lax.rem(lax.axis_index("gz"), 2)

    @pl.when(i == 0)
    def _():
        hz_s[...] = jnp.zeros_like(hz_s)
        ghz_s[...] = jnp.zeros_like(ghz_s)
        a = angle[0]
        both = jnp.concatenate([prof[a, 0], prof[a, 1]], 0)
        rows = jnp.concatenate(six_rows(both) + [jnp.zeros((32, Y), F32)], 0)
        prof_s[...] = rows.T.astype(BF)
        for row, (p, q) in enumerate(((0, 0), (0, CZ - 1), (CZ - 1, CZ - 1))):
            corner = jnp.broadcast_to(w[p:p + 1, q:q + 1], (1, CZ))
            keep_o[16, row:row + 1, :] = corner
            send_o[16, row:row + 1, :] = corner
        keep_o[16, 3:8, :] = jnp.zeros((5, CZ), F32)
        send_o[16, 3:8, :] = jnp.zeros((5, CZ), F32)

    row16 = iota((16, CZ), 0)
    lane16 = iota((16, CZ), 1)
    ends = jnp.where(row16 < 8, w[0:1, :], w[CZ - 1:CZ, :])
    ends_parts = [part.astype(F32) for part in split(ends)]
    slot = lax.rem(row16, 8)

    rowz = iota((CZ, CZ), 0)
    piece, within = rowz // 16, lax.rem(rowz, 16)
    z_table = jnp.where(piece < 6, six_table(zs[...], piece), 0.0)

    lane = iota((Y, CZ), 1)
    inv0 = inverse_eps(lab[0], eps)
    inv1 = inverse_eps(lab[1], eps)
    inv2 = inverse_eps(lab_next[0], eps)
    more = (i < 3).astype(F32)
    sg = [inv0 * ge[2, 0], inv1 * ge[2, 1], inv2 * ge_next[0, 0] * more]
    inv = [inv0, inv1]
    acc_ends = jnp.zeros((16, Y), F32)
    acc_tops = jnp.zeros((16, Y), F32)
    for j in range(2):
        x = 2 * i + j
        z_pick = jnp.concatenate(
            [jnp.where(within == x, z_table, 0.0), jnp.where(within == 8 + x, z_table, 0.0)], 1
        ).astype(BF)
        cur = mm(prof_s[...], z_pick)
        h_x, h_y, h_z = h[0, j], h[1, j], h[2, j]
        hz_prev = hz_s[...] if j == 0 else h[2, 0]
        ghz_prev = ghz_s[...] if j == 0 else gh[2, 0]
        g_hz = gh[2, j]
        bar_hy = gh[1, j] - (sg[j + 1] - sg[j])
        bar_hx = gh[0, j] + y_up(sg[j])
        p_x = y_down(h_z) - z_down(h_y) - cur[:, :CZ]
        p_y = z_down(h_x) - (h_z - hz_prev) - cur[:, CZ:]
        r_x = lt[...] * e[0, j] + inv[j] * p_x
        r_y = lt[...] * e[1, j] + inv[j] * p_y
        a_x = ge[0, j] - y_down(g_hz) - z_down(bar_hy)
        a_y = ge[1, j] + (g_hz - ghz_prev) - z_down(bar_hx)
        scale = -inv[j] * inv[j]
        rx_o[j], ry_o[j], ax_o[j], ay_o[j] = r_x, r_y, a_x, a_y
        psx_o[j] = scale * p_x
        psy_o[j] = scale * p_y

        thirds = []
        for c, field in enumerate((r_x, r_y, a_x, a_y)):
            one, two, three = split(field)
            mask = slot == 4 * j + c
            w1, w2, w3 = (jnp.where(mask, part, 0.0) for part in ends_parts)
            lhs = jnp.concatenate(
                [
                    jnp.concatenate([w1, w1], 1),
                    jnp.concatenate([w2, w2], 1),
                    jnp.concatenate([w3, jnp.zeros_like(w3)], 1),
                ],
                0,
            ).astype(BF)
            out = mm(lhs, jnp.concatenate([one, two], 1), NT)
            acc_ends += out[0:16] + out[16:32] + out[32:48]
            thirds.append((w1, three))
        for c in (0, 2):
            (wa, ta), (wb, tb) = thirds[c], thirds[c + 1]
            lhs = jnp.concatenate([wa, wb], 1).astype(BF)
            acc_ends += mm(lhs, jnp.concatenate([ta, tb], 1), NT)

        packed = jnp.where(lane == CZ - 1, h_y, inv[j])
        packed = jnp.where(lane == CZ - 2, -pltpu.roll(h_x, CZ - 1, 1), packed)
        packed = jnp.where(lane == CZ - 3, pltpu.roll(bar_hy, CZ - 2, 1), packed)
        packed = jnp.where(lane == CZ - 4, pltpu.roll(bar_hx, CZ - 3, 1), packed)
        one, two, three = split(packed)
        c16 = slot - 4 * j
        own = (c16 >= 0) & (c16 < 4)
        pick = jnp.where(
            own & (row16 < 8) & (lane16 == CZ - 1 - c16), 1.0,
            jnp.where(own & (row16 >= 8) & (c16 < 2) & (lane16 == 0), 1.0, 0.0),
        )
        acc_tops += mm(jnp.concatenate([pick, pick], 1).astype(BF), jnp.concatenate([one, two], 1), NT)
        acc_tops += mm(pick.astype(BF), three, NT)

    row_y = iota((16, Y), 0)
    acc_tops = jnp.where((row_y >= 8) & (lax.rem(row_y, 4) >= 2), 1.0, acc_tops)
    hz_s[...] = h[2, 1]
    ghz_s[...] = gh[2, 1]
    for base, acc in ((0, acc_ends), (8, acc_tops)):
        low, high = acc[:, :CZ], acc[:, CZ:]
        keep = jnp.where(core == 0, low, high)
        send = jnp.where(core == 0, high, low)
        for part in range(2):
            keep_o[base + 4 * part + i] = keep[8 * part:8 * part + 8]
            send_o[base + 4 * part + i] = send[8 * part:8 * part + 8]


def unpack(ref):
    m = ref[...]
    return dict(
        f=m[0:4], l=m[4:8], t=m[8:12], k=m[12:16],
        a=m[16, 0:1, :], c=m[16, 1:2, :], z=m[16, 2:3, :],
    )


def repack(s, ref):
    ref[0:4] = s["f"]
    ref[4:8] = s["l"]
    ref[8:12] = s["t"]
    ref[12:16] = s["k"]
    ref[16] = jnp.concatenate([s["a"], s["c"], s["z"], jnp.zeros((5, CZ), F32)], 0)


def order(bit, own, other):
    lower = {n: jnp.where(bit == 0, own[n], other[n]) for n in own}
    upper = {n: jnp.where(bit == 0, other[n], own[n]) for n in own}
    return lower, upper


def coupled(lower, upper):
    delta = upper["k"] * lower["t"]
    f_up = upper["f"] + upper["a"] * delta
    l_up = upper["l"] + upper["c"] * delta
    inv = 1.0 / (1.0 - upper["a"] * lower["z"])
    return f_up, l_up, inv


def combine(lower, upper):
    f_up, l_up, inv = coupled(lower, upper)
    t = (f_up + upper["a"] * lower["l"]) * inv
    u = (lower["l"] + lower["z"] * f_up) * inv
    return dict(
        f=lower["f"] + lower["c"] * t,
        l=l_up + upper["c"] * u,
        t=upper["t"],
        k=lower["k"],
        a=lower["a"] + lower["c"] * lower["c"] * upper["a"] * inv,
        c=lower["c"] * upper["c"] * inv,
        z=upper["z"] + upper["c"] * upper["c"] * lower["z"] * inv,
    )


def outside(lower, upper, below, above):
    f_up, _, inv = coupled(lower, upper)
    l_low = lower["l"] + lower["c"] * below
    f_up = f_up + upper["c"] * above
    return (f_up + upper["a"] * l_low) * inv, (l_low + lower["z"] * f_up) * inv


def pick_outside(bit, lower, upper, below, above):
    t, u = outside(lower, upper, below, above)
    return jnp.where(bit == 0, below, u), jnp.where(bit == 0, t, above)


def bits():
    gz = lax.axis_index("gz")
    core, low_z, high_z = lax.rem(gz, 2), lax.rem(gz // 2, 2), lax.rem(gz // 4, 2)
    return core, low_z, high_z, lax.rem(gz // 8, 2), gz // 16


def chip_kernel(own, other, out):
    core = bits()[0]
    repack(combine(*order(core, unpack(own), unpack(other))), out)


def four(low, high, own, m1, m2, m3):
    first = order(low, own, m1)
    pair = combine(*first)
    return first, order(high, pair, combine(*order(low, m2, m3)))


def group_kernel(m0, m1, m2, m3, out):
    _, low, high, _, _ = bits()
    repack(combine(*four(low, high, *(unpack(m) for m in (m0, m1, m2, m3)))[1]), out)


def back_kernel(a0, a1, m0, m1, m2, m3, n0, n1, n2, n3, keep_o, send_o):
    core, zl, zh, xl, xh = bits()
    chip = order(core, unpack(a0), unpack(a1))
    m0, m1, m2, m3 = (unpack(m) for m in (m0, m1, m2, m3))
    n0, n1, n2, n3 = (unpack(n) for n in (n0, n1, n2, n3))
    z_first, z_second = four(zl, zh, m0, m1, m2, m3)
    x_first, x_second = four(xl, xh, n0, n1, n2, n3)
    zero = jnp.zeros_like(m0["f"])
    edge = (zero, zero)
    edge = pick_outside(xh, *x_second, *edge)
    edge = pick_outside(xl, *x_first, *edge)
    edge = pick_outside(zh, *z_second, *edge)
    edge = pick_outside(zl, *z_first, *edge)
    lower, upper = chip
    t, u = outside(lower, upper, *edge)
    under_x = jnp.where(xl == 1, n1["t"], jnp.where(xh == 1, n3["t"], zero))
    under = jnp.where(zl == 1, m1["t"], jnp.where(zh == 1, m3["t"], under_x))
    results = []
    for block, below, above, plane in ((lower, edge[0], t, under), (upper, u, edge[1], lower["t"])):
        below = below + block["k"] * plane
        first = block["f"] + block["a"] * below + block["c"] * above
        extra = jnp.stack([first[q] * pltpu.roll(plane[q], 2, 0) for q in range(4)])
        results.append((below, above, extra))
    for part in range(3):
        low, high = results[0][part], results[1][part]
        keep_o[4 * part:4 * part + 4] = jnp.where(core == 0, low, high)
        send_o[4 * part:4 * part + 4] = jnp.where(core == 0, high, low)


def product_tables(w):
    one, two, three = split(w.T)
    full = jnp.concatenate([one, two], 1)
    return jnp.concatenate([full, full], 0), jnp.concatenate([one, three], 0)


def product(field, tables):
    one, two, three = split(field)
    wide = mm(jnp.concatenate([one, two], 1), tables[0])
    narrow = mm(jnp.concatenate([three, one], 1), tables[1])
    return wide[:, :CZ] + wide[:, CZ:] + narrow


def adjoint_kernel(ax, ay, psx, psy, w, out):
    tables = product_tables(w[...])
    for j in range(2):
        out[j] = psx[j] * product(ax[j], tables) + psy[j] * product(ay[j], tables)


def primal_kernel(eps, rx, ry, h, ez, ez_next, gez, lab, part, w, ex_o, ey_o, grad_o, hy_s):
    i = pl.program_id(0)

    @pl.when(i == 0)
    def _():
        hy_s[...] = jnp.zeros_like(hy_s)

    tables = product_tables(w[...])
    more = (i < 3).astype(F32)
    up = [ez[0, 0], ez[0, 1], ez_next[0, 0] * more]
    hy_prev = hy_s[...]
    for j in range(2):
        e_x, e_y = product(rx[j], tables), product(ry[j], tables)
        ex_o[j], ey_o[j] = e_x, e_y
        hy = h[1, j] + z_up(e_x) - (up[j + 1] - up[j])
        hx = h[0, j] + z_up(e_y) - y_up(up[j])
        curl = hy - hy_prev - y_down(hx)
        hy_prev = hy
        inv = inverse_eps(lab[j], eps)
        grad_o[j] = part[j] - inv * inv * gez[0, j] * curl
    hy_s[...] = hy_prev


def edge_rows(keep, recv, slab):
    core = lax.rem(lax.axis_index("gz"), 2)
    a, b = keep[slab], recv[slab]
    return jnp.concatenate([jnp.where(core == 0, a, b), jnp.where(core == 0, b, a)], 1)


def columns(below, above):
    rows = six_rows(below) + six_rows(above) + [jnp.zeros((32, Y), F32)]
    return jnp.concatenate(rows, 0).T.astype(BF)


def edge_table(first, last):
    piece = iota((CZ, CZ), 0) // 8
    table = jnp.where(piece < 6, six_table(first, piece), six_table(last, piece - 6))
    return jnp.where(piece < 12, table, 0.0)


def picked(table, row):
    return jnp.where(lax.rem(iota((CZ, CZ), 0), 8) == row, table, 0.0)


def gradient_kernel(k, eps, grad, psx, psy, gez, lab, keep, recv, w, out):
    q = lax.axis_index("src") ^ k
    below, above, extra = (edge_rows(keep, recv, 4 * part + q) for part in range(3))
    before = jnp.maximum(q - 1, 0)
    has = (q > 0).astype(F32)
    row = iota((8, Y), 0)
    lane = iota((8, Y), 1)

    def curl_rows(now, previous):
        shifted = jnp.where(row < 4, pltpu.roll(previous, 4, 0), pltpu.roll(now, 4, 0))
        along_y = now - jnp.where(lane == 0, 0.0, pltpu.roll(now, 1, 1))
        return now - shifted - pltpu.roll(along_y, 7, 0)

    curl_below = curl_rows(below, edge_rows(keep, recv, before) * has)
    curl_above = curl_rows(above, edge_rows(keep, recv, 4 + before) * has)
    kind = lax.rem(row, 4)
    plane = pltpu.roll(extra, 7, 0) + pltpu.roll(extra, 6, 0)
    below = jnp.where(kind == 0, curl_below, jnp.where(kind == 1, plane, below))
    above = jnp.where(kind == 0, curl_above, jnp.where(kind == 1, 0.0, above))
    cols = columns(below, above)
    wt = w[...].T
    first, last = wt[0:1, :], wt[CZ - 1:CZ, :]
    lane1 = iota((1, CZ), 1)
    top = jnp.where(lane1 == CZ - 1, 1.0, 0.0)
    first_up = jnp.where(lane1 == CZ - 1, 0.0, pltpu.roll(first, CZ - 1, 1)) - first
    last_up = jnp.where(lane1 == CZ - 1, 0.0, pltpu.roll(last, CZ - 1, 1)) - last + top
    lam_table = edge_table(first, last)
    curl_table = edge_table(first_up, last_up)
    plane_table = edge_table(jnp.where(lane1 == 0, 1.0, 0.0), jnp.zeros((1, CZ), F32))
    for j in range(2):
        r = 4 * j
        lam = mm(cols, jnp.concatenate([picked(lam_table, r + 2), picked(lam_table, r + 3)], 1).astype(BF))
        rest = mm(cols, jnp.concatenate([picked(curl_table, r), picked(plane_table, r + 1)], 1).astype(BF))
        inv = inverse_eps(lab[j], eps)
        out[j] = (
            grad[j] + psx[j] * lam[:, :CZ] + psy[j] * lam[:, CZ:]
            - inv * inv * (gez[0, j] * rest[:, :CZ] + rest[:, CZ:])
        )


def output_kernel(eps, ex, ey, ey_next, h, ez, ez_next, lab, keep, recv, w, e_o, h_o, hy_s):
    i = pl.program_id(0)

    @pl.when(i == 0)
    def _():
        hy_s[...] = jnp.zeros_like(hy_s)

    more = (i < 3).astype(F32)
    following = jnp.minimum(i + 1, 3)
    below, above = edge_rows(keep, recv, i), edge_rows(keep, recv, 4 + i)
    wt = w[...].T
    table = edge_table(wt[0:1, :], wt[CZ - 1:CZ, :])
    cols = columns(below, above)
    cols_next = columns(edge_rows(keep, recv, following), edge_rows(keep, recv, 4 + following))

    def corrected(source, j, comp):
        return mm(source, picked(table, 4 * j + comp).astype(BF))

    lane = iota((CZ, CZ), 1)
    piece = iota((CZ, CZ), 0) // 8
    ones = jnp.where((piece >= 6) & (piece < 9) & (lane == CZ - 1), 1.0, 0.0)

    def up(v, j, comp):
        return z_up(v) + mm(cols, picked(ones, 4 * j + comp).astype(BF))

    e_x = [ex[j] + corrected(cols, j, 0) for j in range(2)]
    e_y = [ey[j] + corrected(cols, j, 1) for j in range(2)]
    e_y.append((ey_next[0] + corrected(cols_next, 0, 1)) * more)
    e_z = [ez[0, 0], ez[0, 1], ez_next[0, 0] * more]
    hy_prev = hy_s[...]
    for j in range(2):
        hy = h[1, j] + up(e_x[j], j, 0) - (e_z[j + 1] - e_z[j])
        hx = h[0, j] + up(e_y[j], j, 1) - y_up(e_z[j])
        curl = hy - hy_prev - y_down(hx)
        hy_prev = hy
        e_o[0, j] = e_x[j]
        e_o[1, j] = e_y[j]
        e_o[2, j] = e_z[j] + inverse_eps(lab[j], eps) * curl
        h_o[0, j] = hx
        h_o[1, j] = hy
        h_o[2, j] = h[2, j] - (e_y[j + 1] - e_y[j]) + y_up(e_x[j])
    hy_s[...] = hy_prev


def place_kernel(g0, g1, g2, g3, out, sems):
    src = lax.axis_index("src")
    copies = []
    for k, g in enumerate((g0, g1, g2, g3)):
        copies.append(pltpu.make_async_copy(g, out.at[pl.ds(2 * (src ^ k), 2)], sems.at[k]))
    for copy in copies:
        copy.start()
    for copy in copies:
        copy.wait()


def swap(block, axis, mask):
    return lax.ppermute(block, axis, [(i, i ^ mask) for i in range(lax.axis_size(axis))])


SMEM = pl.BlockSpec(memory_space=pltpu.SMEM)
WHOLE = pl.BlockSpec(memory_space=pltpu.VMEM)
ANY = pl.BlockSpec(memory_space=pl.ANY)


def shape(*dims):
    return jax.ShapeDtypeStruct(dims, F32)


def cost(us):
    return pl.CostEstimate(flops=1000, bytes_accessed=int(us * 3.0e6), transcendentals=0)


def params(limit=LIMIT):
    return pltpu.CompilerParams(vmem_limit_bytes=limit)


def body(
    fields_e, fields_h, cot_e, cot_h, labels, region_eps, angle_index, profiles, zsheet,
    layer_term, block_inverse,
):
    e, h, ge, gh = fields_e[0], fields_h[0], cot_e[0], cot_h[0]
    w = block_inverse
    zs, lt = zsheet.reshape(1, CZ), layer_term.reshape(1, CZ)

    pair = pl.BlockSpec((2, Y, CZ), lambda i: (i, 0, 0))

    def comps(n, index=0):
        return pl.BlockSpec((n, 2, Y, CZ), lambda i: (index, i, 0, 0))

    def const(*dims):
        return pl.BlockSpec(dims, lambda i: (0,) * len(dims))

    z_next = pl.BlockSpec((1, 1, Y, CZ), lambda i: (2, jnp.minimum(2 * i + 2, 7), 0, 0))
    x_next = pl.BlockSpec((1, Y, CZ), lambda i: (jnp.minimum(2 * i + 2, 7), 0, 0))
    slab = shape(X, Y, CZ)
    message = shape(SLABS, 8, CZ)

    rx, ry, ax, ay, psx, psy, keep, send = pl.pallas_call(
        rhs_kernel,
        grid=(4,),
        in_specs=[
            SMEM, SMEM, comps(2), comps(3), comps(3), comps(3), pair, z_next, x_next,
            const(8, 2, X, Y), const(1, CZ), const(1, CZ), const(CZ, CZ),
        ],
        out_specs=[pair] * 6 + [const(SLABS, 8, CZ)] * 2,
        out_shape=[slab] * 6 + [message] * 2,
        scratch_shapes=[pltpu.VMEM((Y, CZ), F32), pltpu.VMEM((Y, CZ), F32), pltpu.VMEM((Y, CZ), BF)],
        compiler_params=params(),
        cost_estimate=cost(6),
        name="right_hand_sides",
    )(angle_index, region_eps, e, h, ge, gh, labels, ge, labels, profiles, zs, lt, w)

    def small(kernel, name, n_in, outs):
        return pl.pallas_call(
            kernel, in_specs=[WHOLE] * n_in, out_specs=[WHOLE] * len(outs), out_shape=outs,
            compiler_params=params(), cost_estimate=cost(0.5), name=name,
        )

    other = swap(send, "gz", 1)
    (m0,) = small(chip_kernel, "chip", 2, [message])(keep, other)
    m1, m2, m3 = (swap(m0, "gz", 2 * k) for k in (1, 2, 3))

    adjoint = pl.pallas_call(
        adjoint_kernel,
        grid=(4,),
        in_specs=[pair] * 4 + [const(CZ, CZ)],
        out_specs=pair,
        out_shape=slab,
        compiler_params=params(),
        cost_estimate=cost(3),
        name="adjoint_products",
    )(ax, ay, psx, psy, w)

    (n0,) = small(group_kernel, "group", 4, [message])(m0, m1, m2, m3)
    n1, n2, n3 = (swap(n0, "gz", 8 * k) for k in (1, 2, 3))

    ex, ey, grad = pl.pallas_call(
        primal_kernel,
        grid=(4,),
        in_specs=[
            SMEM, pair, pair, comps(2), comps(1, 2), z_next, comps(1, 2), pair, pair, const(CZ, CZ),
        ],
        out_specs=[pair] * 3,
        out_shape=[slab] * 3,
        scratch_shapes=[pltpu.VMEM((Y, CZ), F32)],
        compiler_params=params(),
        cost_estimate=cost(4),
        name="primal_products",
    )(region_eps, rx, ry, h, e, e, ge, labels, adjoint, w)

    edges = shape(12, 8, CZ)
    own_edges, send_edges = small(back_kernel, "back", 10, [edges] * 2)(
        keep, other, m0, m1, m2, m3, n0, n1, n2, n3
    )
    other_edges = swap(send_edges, "gz", 1)

    def gradient(k):
        def at(*tail):
            return lambda i: (lax.axis_index("src") ^ k,) + tail

        quarter = pl.BlockSpec((2, Y, CZ), at(0, 0))
        gez_quarter = pl.BlockSpec((1, 2, Y, CZ), lambda i: (2, lax.axis_index("src") ^ k, 0, 0))
        return pl.pallas_call(
            lambda *refs: gradient_kernel(k, *refs),
            grid=(1,),
            in_specs=[
                SMEM, quarter, quarter, quarter, gez_quarter, quarter,
                const(12, 8, CZ), const(12, 8, CZ), const(CZ, CZ),
            ],
            out_specs=const(2, Y, CZ),
            out_shape=shape(2, Y, CZ),
            compiler_params=params(),
            cost_estimate=cost(1),
            name=f"gradient_{k}",
        )(region_eps, grad, psx, psy, ge, labels, own_edges, other_edges, w)

    arrived = [swap(gradient(k), "src", k) for k in (2, 1, 3)]
    own = gradient(0)

    e_new, h_new = pl.pallas_call(
        output_kernel,
        grid=(4,),
        in_specs=[
            SMEM, pair, pair, x_next, comps(3), comps(1, 2), z_next, pair,
            const(12, 8, CZ), const(12, 8, CZ), const(CZ, CZ),
        ],
        out_specs=[comps(3), comps(3)],
        out_shape=[shape(3, X, Y, CZ)] * 2,
        scratch_shapes=[pltpu.VMEM((Y, CZ), F32)],
        compiler_params=params(),
        cost_estimate=cost(6),
        name="outputs",
    )(region_eps, ex, ey, ey, h, e, e, labels, own_edges, other_edges, w)

    total = own + arrived[0] + arrived[1] + arrived[2]
    two, one, three = (swap(total, "src", k) for k in (2, 1, 3))
    eps_grad = pl.pallas_call(
        place_kernel,
        in_specs=[ANY] * 4,
        out_specs=ANY,
        out_shape=slab,
        scratch_shapes=[pltpu.SemaphoreType.DMA((4,))],
        compiler_params=params(),
        cost_estimate=cost(1),
        name="place",
    )(total, one, two, three)
    return (e_new[None], h_new[None], eps_grad)


def solution(mesh):
    field = P("src", None, None, None, "gz")
    return jax.shard_map(
        body,
        mesh=mesh,
        in_specs=(
            field, field, field, field, P(None, None, "gz"), P(), P("src"), P(), P("gz"), P("gz"),
            P("gz", None),
        ),
        out_specs=(field, field, P(None, None, "gz")),
        check_vma=False,
    )
```

time: 574 us -> 82.3 us (0.14); the launches traced: 567 us -> 81.4 us
  other arithmetic: 147 us -> 0.05 us
  blocking collectives: 128 us -> 0 us
  local copies, waits for them, and re-layouts: 109 us -> 12.2 us
  loops' own time: 80.9 us -> 0 us
  waiting for transfers between devices: 68.7 us -> 23.4 us
  Pallas kernels: 0 us -> 24 us
  between operations: 19.9 us -> 1.49 us
  starting transfers between devices: 7.42 us -> 20.3 us
    unnamed x2 -> x0, blocking collectives: 128 us -> none
    select_n x64 -> x0, other arithmetic: 91.4 us -> none  [step(): return jax.tree.map(lambda a, b: jnp.where(reached, a, b), new, before)]
    another operation x3 -> x0, loops' own time: 80.9 us -> none  [the longest x1 80.8 us: chain_terms(): lax.scan(advance, jnp.zeros((), corners.dtype), corners)]
    dynamic_slice x98 -> x0, local copies, waits for them, and re-layouts: 40.8 us -> none  [the longest x64 39.4 us: step(): new = combine(before, jax.tree.map(lambda part: part[at], everything))]
    psum x1 -> x0, waiting for transfers between devices: 38.9 us -> none  [body(): summed = lax.psum(grad_terms, 'src')]
    slice x53 -> x0, local copies, waits for them, and re-layouts: 37.5 us -> none  [the longest x32 20.9 us: advance(): denom = 1.0 - corner_row[0] * q_carry]
    all_gather x2 -> x0, waiting for transfers between devices: 29.7 us -> none  [prefix(): everything = jax.tree.map(lambda part: lax.all_gather(part, axis), x)]
    pallas_call x0 -> x12, Pallas kernels: none -> 24 us  [the longest x1 7.17 us: body(): pl.pallas_call(rhs_kernel, grid=(4,), in_specs=[SMEM, SMEM, comps(2), com...]
  transfers between devices with their start and end apart: 5 -> 14, of which waited for: 2 -> 9; matrix products, arithmetic and copies ran while one was open for 10% -> 0% of each run, Pallas kernels for 0% -> 18%
where the time goes in v1:
time: 82.3 us; the launch traced here: 81.4 us
  Pallas kernels  24 us (29%)
  waiting for transfers between devices  23.4 us (28%)
  starting transfers between devices  20.3 us (25%)
  local copies, waits for them, and re-layouts  12.2 us (15%)
  between operations  1.49 us (2%)
    ppermute x14, waiting for transfers between devices, swap(): lax.ppermute(block, axis, [(i, i ^ mask) for i in range(lax.axis_size(axi...  23.4 us
    ppermute x14, starting transfers between devices, swap(): lax.ppermute(block, axis, [(i, i ^ mask) for i in range(lax.axis_size(axi...  20.3 us
    unnamed x40, local copies, waits for them, and re-layouts  12.2 us
    pallas_call x1, Pallas kernels, body(): pl.pallas_call(rhs_kernel, grid=(4,), in_specs=[SMEM, SMEM, comps(2), com...  7.17 us
    pallas_call x1, Pallas kernels, body(): pl.pallas_call(output_kernel, grid=(4,), in_specs=[SMEM, pair, pair, x_ne...  5.08 us
    pallas_call x1, Pallas kernels, body(): pl.pallas_call(primal_kernel, grid=(4,), in_specs=[SMEM, pair, pair, comp...  4.34 us
    pallas_call x4, Pallas kernels, gradient(): pl.pallas_call(lambda *refs: gradient_kernel(k, *refs), grid=(1,), in_spe...  4.01 us
    pallas_call x1, Pallas kernels, body(): pl.pallas_call(adjoint_kernel, grid=(4,), in_specs=[pair] * 4 + [const(CZ...  2.1 us
  transfers between devices with their start and end apart: 14, of which 9 were waited for; matrix products, arithmetic and copies ran while one was open for 0% of the time, Pallas kernels for 18%

profile of v1, /device:TPU:1, one launch (start us, length us, event | category | flops | bytes accessed | tf_op | source)
XLA Modules:
  0.0 81.4 jit_solution(13064337421129869431)
XLA Ops:
  1.3 1.9 %copy-done.1 = f32[1,3,8,256,128]{4,3,2,1,0:T(8,128)S(1)} copy-done((f32[1,3,8,256,128]{4,3,2,1,0:T(8,128)S(1)}, f32[1,3,8,256,128]{4,3,2,1,0:T(8,128)}, u32[]{:S(2)}) %copy-start.1) | copy-done | bytes 3145752
  3.2 1.2 %copy-done.3 = s32[8,256,128]{2,1,0:T(8,128)S(1)} copy-done((s32[8,256,128]{2,1,0:T(8,128)S(1)}, s32[8,256,128]{2,1,0:T(8,128)}, u32[]{:S(2)}) %copy-start.3) | copy-done | bytes 1048600
  4.4 1.9 %copy-done.5 = f32[1,3,8,256,128]{4,3,2,1,0:T(8,128)S(1)} copy-done((f32[1,3,8,256,128]{4,3,2,1,0:T(8,128)S(1)}, f32[1,3,8,256,128]{4,3,2,1,0:T(8,128)}, u32[]{:S(2)}) %copy-start.5) | copy-done | bytes 3145752
  10.0 7.2 %right_hand_sides.1 = (f32[8,256,128]{2,1,0:T(8,128)S(1)}, f32[8,256,128]{2,1,0:T(8,128)S(1)}, f32[8,256,128]{2,1,0:T(8,128)S(1)}, f32[8,256,128]{2,1,0:T(8,128)...) custom-call(s32[1]{0:T(128)S(6)} %copy.14.angle, ...), custom_call_target="tpu_custom_call" | custom-call | flops 1000 | bytes 18000000 | tf_op jit(solution)/shard_map/right_hand_sides/pallas_call | solution.py:489
  18.2 1.4 %collective-permute-start = (f32[17,8,128]{2,1,0:T(8,128)S(1)}, f32[17,8,128]{2,1,0:T(8,128)S(1)}, u32[]{:S(2)}, u32[]{:S(2)}) collective-permute-start(f32[17,8,128]{2,1,0:T(8,128)S(1)} %get-tuple-element.27), channel_id=1, source_target_pairs={{0,1},{1,0},{2,3},{3,2},{4,5},{5,4},{6,7},{7,6},{8,9},{9,8},{10,11... | collective-permute-start | bytes 208904 | tf_op jit(solution)/shard_map/ppermute | solution.py:448
  20.6 3.9 %collective-permute-start.3 = (f32[17,8,128]{2,1,0:T(8,128)S(1)}, f32[17,8,128]{2,1,0:T(8,128)S(1)}, u32[]{:S(2)}, u32[]{:S(2)}) collective-permute-start(f32[17,8,128]{2,1,0:T(8,128)S(1)} %chip.1.m0), channel_id=1, source_target_pairs={{0,6},{1,7},{2,4},{3,5},{4,2},{5,3},{6,0},{7,1},{8,14},{9,15},{10,... | collective-permute-start | bytes 208904 | tf_op jit(solution)/shard_map/ppermute | solution.py:448
  25.2 1.7 %collective-permute-done.3.m3 = f32[17,8,128]{2,1,0:T(8,128)S(1)} collective-permute-done((f32[17,8,128]{2,1,0:T(8,128)S(1)}, f32[17,8,128]{2,1,0:T(8,128)S(1)}, u32[]{:S(2)}, u32[]{:S(2)}) %collective-permute-start.3) | collective-permute-done | bytes 69664 | tf_op jit(solution)/shard_map/ppermute | solution.py:448
  26.9 2.3 %collective-permute-done.2.m2 = f32[17,8,128]{2,1,0:T(8,128)S(1)} collective-permute-done((f32[17,8,128]{2,1,0:T(8,128)S(1)}, f32[17,8,128]{2,1,0:T(8,128)S(1)}, u32[]{:S(2)}, u32[]{:S(2)}) %collective-permute-start.2) | collective-permute-done | bytes 69664 | tf_op jit(solution)/shard_map/ppermute | solution.py:448
  29.3 2.6 %collective-permute-start.6 = (f32[17,8,128]{2,1,0:T(8,128)S(1)}, f32[17,8,128]{2,1,0:T(8,128)S(1)}, u32[]{:S(2)}, u32[]{:S(2)}) collective-permute-start(f32[17,8,128]{2,1,0:T(8,128)S(1)} %group.1.n0), channel_id=1, source_target_pairs={{0,24},{1,25},{2,26},{3,27},{4,28},{5,29},{6,30},{7,31},{8,16},{9,... | collective-permute-start | bytes 208904 | tf_op jit(solution)/shard_map/ppermute | solution.py:448
  32.6 1.1 %collective-permute-done.6.n3 = f32[17,8,128]{2,1,0:T(8,128)S(1)} collective-permute-done((f32[17,8,128]{2,1,0:T(8,128)S(1)}, f32[17,8,128]{2,1,0:T(8,128)S(1)}, u32[]{:S(2)}, u32[]{:S(2)}) %collective-permute-start.6) | collective-permute-done | bytes 69664 | tf_op jit(solution)/shard_map/ppermute | solution.py:448
  33.7 2.9 %collective-permute-done.5.n2 = f32[17,8,128]{2,1,0:T(8,128)S(1)} collective-permute-done((f32[17,8,128]{2,1,0:T(8,128)S(1)}, f32[17,8,128]{2,1,0:T(8,128)S(1)}, u32[]{:S(2)}, u32[]{:S(2)}) %collective-permute-start.5) | collective-permute-done | bytes 69664 | tf_op jit(solution)/shard_map/ppermute | solution.py:448
  36.8 3.6 %collective-permute-start.7 = (f32[12,8,128]{2,1,0:T(8,128)S(1)}, f32[12,8,128]{2,1,0:T(8,128)S(1)}, u32[]{:S(2)}, u32[]{:S(2)}) collective-permute-start(f32[12,8,128]{2,1,0:T(8,128)S(1)} %get-tuple-element.29), channel_id=1, source_target_pairs={{0,1},{1,0},{2,3},{3,2},{4,5},{5,4},{6,7},{7,6},{8,9},{9,8},{10,11... | collective-permute-start | bytes 147464 | tf_op jit(solution)/shard_map/ppermute | solution.py:448
  40.4 2.1 %adjoint_products.1.part = f32[8,256,128]{2,1,0:T(8,128)S(1)} custom-call(f32[8,256,128]{2,1,0:T(8,128)S(1)} %get-tuple-element.20.ax, f32[8,256,128]{2,1,0:T(8,128)S(1)} %get-tuple-element.21.ay, f32[8,256,128]{2,1,0:T(8,128)S(1)} %get-tuple-element.22.psx.refs_2_, f32[8,256,128]{2,1,0:T(8,128)S(1)} %get-tuple-element.23.psy.refs_3_, f32[128,128]{1,0:T(8,128)S(1)} %copy-done.9), custom_call_target="tpu_custom_call" | custom-call | flops 1000 | bytes 9000000 | tf_op jit(solution)/shard_map/adjoint_products/pallas_call | solution.py:514
  42.5 1.2 %copy-done.12 = f32[8,256,128]{2,1,0:T(8,128)S(1)} copy-done((f32[8,256,128]{2,1,0:T(8,128)S(1)}, f32[8,256,128]{2,1,0:T(8,128)}, u32[]{:S(2)}) %copy-start.12) | copy-done | bytes 1048600
  43.8 1.2 %copy-done.14 = f32[8,256,128]{2,1,0:T(8,128)S(1)} copy-done((f32[8,256,128]{2,1,0:T(8,128)S(1)}, f32[8,256,128]{2,1,0:T(8,128)}, u32[]{:S(2)}) %copy-start.14) | copy-done | bytes 1048600
  45.0 4.3 %primal_products.1 = (f32[8,256,128]{2,1,0:T(8,128)S(1)}, f32[8,256,128]{2,1,0:T(8,128)S(1)}, f32[8,256,128]{2,1,0:T(8,128)S(1)}) custom-call(f32[4]{0:T(128)S(1)} %copy-done.17, f32[8,256,128]{2,1,0:T(8,128)S(1)} %copy-done.12, f32[8,256,128]{2,1,0:T(8,128)S(1)} %copy-done.14, f32[3,8,256,128]{3,2,1,0:T(8,128)S(1)} %bitcast.21, ...), custom_call_target="tpu_custom_call" | custom-call | flops 1000 | bytes 12000000 | tf_op jit(solution)/shard_map/primal_products/pallas_call | solution.py:528
  49.4 1.0 %gradient_2.1 = f32[2,256,128]{2,1,0:T(8,128)S(1)} custom-call(f32[4]{0:T(128)S(1)} %copy-done.17, f32[8,256,128]{2,1,0:T(8,128)S(1)} %get-tuple-element.32.refs_1_, f32[8,256,128]{2,1,0:T(8,128)S(1)} %get-tuple-element.22.psx.refs_2_, f32[8,256,128]{2,1,0:T(8,128)S(1)} %copy-done.8, f32[3,8,256,128]{3,2,1,0:T(8,128)S(1)} %bitcast.11, ...), custom_call_target="tpu_custom_call" | custom-call | flops 1000 | bytes 3000000 | tf_op jit(solution)/shard_map/gradient_2/pallas_call | solution.py:554
  50.4 3.0 %collective-permute-start.8 = (f32[2,256,128]{2,1,0:T(8,128)S(1)}, f32[2,256,128]{2,1,0:T(8,128)S(1)}, u32[]{:S(2)}, u32[]{:S(2)}) collective-permute-start(f32[2,256,128]{2,1,0:T(8,128)S(1)} %gradient_2.1), channel_id=1, source_target_pairs={{0,64},{32,96},{64,0},{96,32},{1,65},{33,97},{65,1},{97,33},{2,66}... | collective-permute-start | bytes 786440 | tf_op jit(solution)/shard_map/ppermute | solution.py:448
  56.3 1.0 %gradient_0.1 = f32[2,256,128]{2,1,0:T(8,128)S(1)} custom-call(f32[4]{0:T(128)S(1)} %copy-done.17, f32[8,256,128]{2,1,0:T(8,128)S(1)} %get-tuple-element.32.refs_1_, f32[8,256,128]{2,1,0:T(8,128)S(1)} %get-tuple-element.22.psx.refs_2_, f32[8,256,128]{2,1,0:T(8,128)S(1)} %copy-done.8, f32[3,8,256,128]{3,2,1,0:T(8,128)S(1)} %bitcast.14, ...), custom_call_target="tpu_custom_call" | custom-call | flops 1000 | bytes 3000000 | tf_op jit(solution)/shard_map/gradient_0/pallas_call | solution.py:554
  57.4 2.5 %collective-permute-done.8 = f32[2,256,128]{2,1,0:T(8,128)S(1)} collective-permute-done((f32[2,256,128]{2,1,0:T(8,128)S(1)}, f32[2,256,128]{2,1,0:T(8,128)S(1)}, u32[]{:S(2)}, u32[]{:S(2)}) %collective-permute-start.8) | collective-permute-done | bytes 262176 | tf_op jit(solution)/shard_map/ppermute | solution.py:448
  59.9 6.0 %collective-permute-done.9 = f32[2,256,128]{2,1,0:T(8,128)S(1)} collective-permute-done((f32[2,256,128]{2,1,0:T(8,128)S(1)}, f32[2,256,128]{2,1,0:T(8,128)S(1)}, u32[]{:S(2)}, u32[]{:S(2)}) %collective-permute-start.9) | collective-permute-done | bytes 262176 | tf_op jit(solution)/shard_map/ppermute | solution.py:448
  65.9 2.8 %collective-permute-start.13 = (f32[2,256,128]{2,1,0:T(8,128)S(1)}, f32[2,256,128]{2,1,0:T(8,128)S(1)}, u32[]{:S(2)}, u32[]{:S(2)}) collective-permute-start(f32[2,256,128]{2,1,0:T(8,128)S(1)} %add_add_fusion.g0), channel_id=1, source_target_pairs={{0,96},{32,64},{64,32},{96,0},{1,97},{33,65},{65,33},{97,1},{2,98}... | collective-permute-start | bytes 786440 | tf_op jit(solution)/shard_map/ppermute | solution.py:448
  69.4 5.1 %outputs.1 = (f32[3,8,256,128]{3,2,1,0:T(8,128)}, f32[3,8,256,128]{3,2,1,0:T(8,128)}) custom-call(f32[4]{0:T(128)S(1)} %copy-done.17, f32[8,256,128]{2,1,0:T(8,128)S(1)} %get-tuple-element.24.ex, f32[8,256,128]{2,1,0:T(8,128)S(1)} %get-tuple-element.25.ey.ey_next, f32[8,256,128]{2,1,0:T(8,128)S(1)} %get-tuple-element.25.ey.ey_next, ...), custom_call_target="tpu_custom_call" | custom-call | flops 1000 | bytes 18000000 | tf_op jit(solution)/shard_map/outputs/pallas_call | solution.py:571
  74.5 5.5 %collective-permute-done.13.g3 = f32[2,256,128]{2,1,0:T(8,128)S(1)} collective-permute-done((f32[2,256,128]{2,1,0:T(8,128)S(1)}, f32[2,256,128]{2,1,0:T(8,128)S(1)}, u32[]{:S(2)}, u32[]{:S(2)}) %collective-permute-start.13) | collective-permute-done | bytes 262176 | tf_op jit(solution)/shard_map/ppermute | solution.py:448
  (57 shorter events, 12.5 us)
Async XLA Ops:
  1.3 1.9 %copy-start.1 = (f32[1,3,8,256,128]{4,3,2,1,0:T(8,128)S(1)}, f32[1,3,8,256,128]{4,3,2,1,0:T(8,128)}, u32[]{:S(2)}) copy-start(f32[1,3,8,256,128]{4,3,2,1,0:T(8,128)} %param.11) | copy-start | bytes 9437188
  18.2 24.3 %copy-start.7 = (f32[8,256,128]{2,1,0:T(8,128)}, f32[8,256,128]{2,1,0:T(8,128)S(1)}, u32[]{:S(2)}) copy-start(f32[8,256,128]{2,1,0:T(8,128)S(1)} %get-tuple-element.23.psy.refs_3_) | copy-start | bytes 3145732
  18.2 24.3 %copy-start.11 = (f32[8,256,128]{2,1,0:T(8,128)}, f32[8,256,128]{2,1,0:T(8,128)S(1)}, u32[]{:S(2)}) copy-start(f32[8,256,128]{2,1,0:T(8,128)S(1)} %get-tuple-element.18.rx) | copy-start | bytes 3145732
  18.2 2.3 %collective-permute-start = (f32[17,8,128]{2,1,0:T(8,128)S(1)}, f32[17,8,128]{2,1,0:T(8,128)S(1)}, u32[]{:S(2)}, u32[]{:S(2)}) collective-permute-start(f32[17,8,128]{2,1,0:T(8,128)S(1)} %get-tuple-element.27), channel_id=1, source_target_pairs={{0,1},{1,0},{2,3},{3,2},{4,5},{5,4},{6,7},{7,6},{8,9},{9,8},{10,11... | collective-permute-start | bytes 208904 | tf_op jit(solution)/shard_map/ppermute | solution.py:448
  20.5 21.9 %copy-start.2 = (f32[1,3,8,256,128]{4,3,2,1,0:T(8,128)S(1)}, f32[1,3,8,256,128]{4,3,2,1,0:T(8,128)}, u32[]{:S(2)}) copy-start(f32[1,3,8,256,128]{4,3,2,1,0:T(8,128)} %param.11) | copy-start | bytes 9437188
  20.6 21.9 %copy-start.6 = (f32[1,3,8,256,128]{4,3,2,1,0:T(8,128)S(1)}, f32[1,3,8,256,128]{4,3,2,1,0:T(8,128)}, u32[]{:S(2)}) copy-start(f32[1,3,8,256,128]{4,3,2,1,0:T(8,128)} %param.12) | copy-start | bytes 9437188
  20.6 21.9 %copy-start.10 = (f32[128,128]{1,0:T(8,128)S(1)}, f32[128,128]{1,0:T(8,128)}, u32[]{:S(2)}) copy-start(f32[128,128]{1,0:T(8,128)} %refs_8_.7) | copy-start | bytes 196612
  20.6 21.9 %copy-start.17 = (f32[4]{0:T(128)S(1)}, f32[4]{0:T(128)}, u32[]{:S(2)}) copy-start(f32[4]{0:T(128)} %refs_0_.7) | copy-start | bytes 52
  20.6 6.3 %collective-permute-start.3 = (f32[17,8,128]{2,1,0:T(8,128)S(1)}, f32[17,8,128]{2,1,0:T(8,128)S(1)}, u32[]{:S(2)}, u32[]{:S(2)}) collective-permute-start(f32[17,8,128]{2,1,0:T(8,128)S(1)} %chip.1.m0), channel_id=1, source_target_pairs={{0,6},{1,7},{2,4},{3,5},{4,2},{5,3},{6,0},{7,1},{8,14},{9,15},{10,... | collective-permute-start | bytes 208904 | tf_op jit(solution)/shard_map/ppermute | solution.py:448
  24.5 4.7 %collective-permute-start.2 = (f32[17,8,128]{2,1,0:T(8,128)S(1)}, f32[17,8,128]{2,1,0:T(8,128)S(1)}, u32[]{:S(2)}, u32[]{:S(2)}) collective-permute-start(f32[17,8,128]{2,1,0:T(8,128)S(1)} %chip.1.m0), channel_id=1, source_target_pairs={{0,4},{1,5},{2,6},{3,7},{4,0},{5,1},{6,2},{7,3},{8,12},{9,13},{10,... | collective-permute-start | bytes 208904 | tf_op jit(solution)/shard_map/ppermute | solution.py:448
  24.5 4.7 %collective-permute-start.1 = (f32[17,8,128]{2,1,0:T(8,128)S(1)}, f32[17,8,128]{2,1,0:T(8,128)S(1)}, u32[]{:S(2)}, u32[]{:S(2)}) collective-permute-start(f32[17,8,128]{2,1,0:T(8,128)S(1)} %chip.1.m0), channel_id=1, source_target_pairs={{0,2},{1,3},{2,0},{3,1},{4,6},{5,7},{6,4},{7,5},{8,10},{9,11},{10,... | collective-permute-start | bytes 208904 | tf_op jit(solution)/shard_map/ppermute | solution.py:448
  29.3 4.5 %collective-permute-start.6 = (f32[17,8,128]{2,1,0:T(8,128)S(1)}, f32[17,8,128]{2,1,0:T(8,128)S(1)}, u32[]{:S(2)}, u32[]{:S(2)}) collective-permute-start(f32[17,8,128]{2,1,0:T(8,128)S(1)} %group.1.n0), channel_id=1, source_target_pairs={{0,24},{1,25},{2,26},{3,27},{4,28},{5,29},{6,30},{7,31},{8,16},{9,... | collective-permute-start | bytes 208904 | tf_op jit(solution)/shard_map/ppermute | solution.py:448
  31.8 4.8 %collective-permute-start.5 = (f32[17,8,128]{2,1,0:T(8,128)S(1)}, f32[17,8,128]{2,1,0:T(8,128)S(1)}, u32[]{:S(2)}, u32[]{:S(2)}) collective-permute-start(f32[17,8,128]{2,1,0:T(8,128)S(1)} %group.1.n0), channel_id=1, source_target_pairs={{0,16},{1,17},{2,18},{3,19},{4,20},{5,21},{6,22},{7,23},{8,24},{9,... | collective-permute-start | bytes 208904 | tf_op jit(solution)/shard_map/ppermute | solution.py:448
  32.3 4.3 %collective-permute-start.4 = (f32[17,8,128]{2,1,0:T(8,128)S(1)}, f32[17,8,128]{2,1,0:T(8,128)S(1)}, u32[]{:S(2)}, u32[]{:S(2)}) collective-permute-start(f32[17,8,128]{2,1,0:T(8,128)S(1)} %group.1.n0), channel_id=1, source_target_pairs={{0,8},{1,9},{2,10},{3,11},{4,12},{5,13},{6,14},{7,15},{8,0},{9,1},... | collective-permute-start | bytes 208904 | tf_op jit(solution)/shard_map/ppermute | solution.py:448
  36.8 12.6 %collective-permute-start.7 = (f32[12,8,128]{2,1,0:T(8,128)S(1)}, f32[12,8,128]{2,1,0:T(8,128)S(1)}, u32[]{:S(2)}, u32[]{:S(2)}) collective-permute-start(f32[12,8,128]{2,1,0:T(8,128)S(1)} %get-tuple-element.29), channel_id=1, source_target_pairs={{0,1},{1,0},{2,3},{3,2},{4,5},{5,4},{6,7},{7,6},{8,9},{9,8},{10,11... | collective-permute-start | bytes 147464 | tf_op jit(solution)/shard_map/ppermute | solution.py:448
  45.0 4.4 %copy-start = (f32[1,3,8,256,128]{4,3,2,1,0:T(8,128)S(1)}, f32[1,3,8,256,128]{4,3,2,1,0:T(8,128)}, u32[]{:S(2)}) copy-start(f32[1,3,8,256,128]{4,3,2,1,0:T(8,128)} %param.13) | copy-start | bytes 9437188
  45.0 4.4 %copy-start.4 = (s32[8,256,128]{2,1,0:T(8,128)S(1)}, s32[8,256,128]{2,1,0:T(8,128)}, u32[]{:S(2)}) copy-start(s32[8,256,128]{2,1,0:T(8,128)} %refs_5_.7) | copy-start | bytes 3145732
  45.0 4.4 %copy-start.8 = (f32[8,256,128]{2,1,0:T(8,128)S(1)}, f32[8,256,128]{2,1,0:T(8,128)}, u32[]{:S(2)}) copy-start(f32[8,256,128]{2,1,0:T(8,128)} %copy-done.7) | copy-start | bytes 3145732
  50.4 9.5 %collective-permute-start.8 = (f32[2,256,128]{2,1,0:T(8,128)S(1)}, f32[2,256,128]{2,1,0:T(8,128)S(1)}, u32[]{:S(2)}, u32[]{:S(2)}) collective-permute-start(f32[2,256,128]{2,1,0:T(8,128)S(1)} %gradient_2.1), channel_id=1, source_target_pairs={{0,64},{32,96},{64,0},{96,32},{1,65},{33,97},{65,1},{97,33},{2,66}... | collective-permute-start | bytes 786440 | tf_op jit(solution)/shard_map/ppermute | solution.py:448
  54.4 11.5 %collective-permute-start.9 = (f32[2,256,128]{2,1,0:T(8,128)S(1)}, f32[2,256,128]{2,1,0:T(8,128)S(1)}, u32[]{:S(2)}, u32[]{:S(2)}) collective-permute-start(f32[2,256,128]{2,1,0:T(8,128)S(1)} %gradient_1.1), channel_id=1, source_target_pairs={{0,32},{32,0},{64,96},{96,64},{1,33},{33,1},{65,97},{97,65},{2,34}... | collective-permute-start | bytes 786440 | tf_op jit(solution)/shard_map/ppermute | solution.py:448
  55.9 10.0 %collective-permute-start.10 = (f32[2,256,128]{2,1,0:T(8,128)S(1)}, f32[2,256,128]{2,1,0:T(8,128)S(1)}, u32[]{:S(2)}, u32[]{:S(2)}) collective-permute-start(f32[2,256,128]{2,1,0:T(8,128)S(1)} %gradient_3.1), channel_id=1, source_target_pairs={{0,96},{32,64},{64,32},{96,0},{1,97},{33,65},{65,33},{97,1},{2,98}... | collective-permute-start | bytes 786440 | tf_op jit(solution)/shard_map/ppermute | solution.py:448
  65.9 14.0 %collective-permute-start.13 = (f32[2,256,128]{2,1,0:T(8,128)S(1)}, f32[2,256,128]{2,1,0:T(8,128)S(1)}, u32[]{:S(2)}, u32[]{:S(2)}) collective-permute-start(f32[2,256,128]{2,1,0:T(8,128)S(1)} %add_add_fusion.g0), channel_id=1, source_target_pairs={{0,96},{32,64},{64,32},{96,0},{1,97},{33,65},{65,33},{97,1},{2,98}... | collective-permute-start | bytes 786440 | tf_op jit(solution)/shard_map/ppermute | solution.py:448
  68.7 11.3 %collective-permute-start.12 = (f32[2,256,128]{2,1,0:T(8,128)S(1)}, f32[2,256,128]{2,1,0:T(8,128)S(1)}, u32[]{:S(2)}, u32[]{:S(2)}) collective-permute-start(f32[2,256,128]{2,1,0:T(8,128)S(1)} %add_add_fusion.g0), channel_id=1, source_target_pairs={{0,64},{32,96},{64,0},{96,32},{1,65},{33,97},{65,1},{97,33},{2,66}... | collective-permute-start | bytes 786440 | tf_op jit(solution)/shard_map/ppermute | solution.py:448
  69.0 11.4 %collective-permute-start.11 = (f32[2,256,128]{2,1,0:T(8,128)S(1)}, f32[2,256,128]{2,1,0:T(8,128)S(1)}, u32[]{:S(2)}, u32[]{:S(2)}) collective-permute-start(f32[2,256,128]{2,1,0:T(8,128)S(1)} %add_add_fusion.g0), channel_id=1, source_target_pairs={{0,32},{32,0},{64,96},{96,64},{1,33},{33,1},{65,97},{97,65},{2,34}... | collective-permute-start | bytes 786440 | tf_op jit(solution)/shard_map/ppermute | solution.py:448
  (10 other events, 10.3 us)

commit v2 on v1

--- a/solution.py
+++ b/solution.py
@@ -12,6 +12,7 @@
 NT = (((1,), (1,)), ((), ()))
 SLABS = 17
 LIMIT = 40 * 1024 * 1024
+BIG = 60 * 1024 * 1024
 
 
 def split(v):
@@ -252,12 +253,12 @@
     return first, order(high, pair, combine(*order(low, m2, m3)))
 
 
-def group_kernel(m0, m1, m2, m3, out):
+def group_kernel(m0, m1, m2, m3, after, out):
     _, low, high, _, _ = bits()
     repack(combine(*four(low, high, *(unpack(m) for m in (m0, m1, m2, m3)))[1]), out)
 
 
-def back_kernel(a0, a1, m0, m1, m2, m3, n0, n1, n2, n3, keep_o, send_o):
+def back_kernel(a0, a1, m0, m1, m2, m3, n0, n1, n2, n3, after, keep_o, send_o):
     core, zl, zh, xl, xh = bits()
     chip = order(core, unpack(a0), unpack(a1))
     m0, m1, m2, m3 = (unpack(m) for m in (m0, m1, m2, m3))
@@ -299,13 +300,13 @@
     return wide[:, :CZ] + wide[:, CZ:] + narrow
 
 
-def adjoint_kernel(ax, ay, psx, psy, w, out):
+def adjoint_kernel(ax, ay, psx, psy, w, after, out):
     tables = product_tables(w[...])
     for j in range(2):
         out[j] = psx[j] * product(ax[j], tables) + psy[j] * product(ay[j], tables)
 
 
-def primal_kernel(eps, rx, ry, h, ez, ez_next, gez, lab, part, w, ex_o, ey_o, grad_o, hy_s):
+def primal_kernel(eps, rx, ry, h, ez, ez_next, gez, lab, part, w, after, ex_o, ey_o, grad_o, hy_s):
     i = pl.program_id(0)
 
     @pl.when(i == 0)
@@ -496,14 +497,14 @@
         out_specs=[pair] * 6 + [const(SLABS, 8, CZ)] * 2,
         out_shape=[slab] * 6 + [message] * 2,
         scratch_shapes=[pltpu.VMEM((Y, CZ), F32), pltpu.VMEM((Y, CZ), F32), pltpu.VMEM((Y, CZ), BF)],
-        compiler_params=params(),
+        compiler_params=params(BIG),
         cost_estimate=cost(6),
         name="right_hand_sides",
     )(angle_index, region_eps, e, h, ge, gh, labels, ge, labels, profiles, zs, lt, w)
 
-    def small(kernel, name, n_in, outs):
+    def small(kernel, name, n_in, outs, after=0):
         return pl.pallas_call(
-            kernel, in_specs=[WHOLE] * n_in, out_specs=[WHOLE] * len(outs), out_shape=outs,
+            kernel, in_specs=[WHOLE] * n_in + [ANY] * after, out_specs=[WHOLE] * len(outs), out_shape=outs,
             compiler_params=params(), cost_estimate=cost(0.5), name=name,
         )
 
@@ -514,22 +515,22 @@
     adjoint = pl.pallas_call(
         adjoint_kernel,
         grid=(4,),
-        in_specs=[pair] * 4 + [const(CZ, CZ)],
+        in_specs=[pair] * 4 + [const(CZ, CZ), ANY],
         out_specs=pair,
         out_shape=slab,
         compiler_params=params(),
         cost_estimate=cost(3),
         name="adjoint_products",
-    )(ax, ay, psx, psy, w)
-
-    (n0,) = small(group_kernel, "group", 4, [message])(m0, m1, m2, m3)
+    )(ax, ay, psx, psy, w, m0)
+
+    (n0,) = small(group_kernel, "group", 4, [message], 1)(m0, m1, m2, m3, adjoint)
     n1, n2, n3 = (swap(n0, "gz", 8 * k) for k in (1, 2, 3))
 
     ex, ey, grad = pl.pallas_call(
         primal_kernel,
         grid=(4,),
         in_specs=[
-            SMEM, pair, pair, comps(2), comps(1, 2), z_next, comps(1, 2), pair, pair, const(CZ, CZ),
+            SMEM, pair, pair, comps(2), comps(1, 2), z_next, comps(1, 2), pair, pair, const(CZ, CZ), ANY,
         ],
         out_specs=[pair] * 3,
         out_shape=[slab] * 3,
@@ -537,11 +538,11 @@
         compiler_params=params(),
         cost_estimate=cost(4),
         name="primal_products",
-    )(region_eps, rx, ry, h, e, e, ge, labels, adjoint, w)
+    )(region_eps, rx, ry, h, e, e, ge, labels, adjoint, w, n0)
 
     edges = shape(12, 8, CZ)
-    own_edges, send_edges = small(back_kernel, "back", 10, [edges] * 2)(
-        keep, other, m0, m1, m2, m3, n0, n1, n2, n3
+    own_edges, send_edges = small(back_kernel, "back", 10, [edges] * 2, 1)(
+        keep, other, m0, m1, m2, m3, n0, n1, n2, n3, ex
     )
     other_edges = swap(send_edges, "gz", 1)
 

time: 82.3 us -> 70.4 us (0.86)
  waiting for transfers between devices: 23.4 us -> 16 us
  local copies, waits for them, and re-layouts: 12.2 us -> 5.82 us
  Pallas kernels: 24 us -> 27.1 us
  starting transfers between devices: 20.3 us -> 19 us
    ppermute x14, waiting for transfers between devices: 23.4 us -> 16 us  [swap(): lax.ppermute(block, axis, [(i, i ^ mask) for i in range(lax.axis_size(axi...]
    unnamed x40 -> x30, local copies, waits for them, and re-layouts: 12.2 us -> 5.82 us
    pallas_call x1, Pallas kernels: 7.17 us -> 10.2 us  [body(): pl.pallas_call(rhs_kernel, grid=(4,), in_specs=[SMEM, SMEM, comps(2), com...]
    ppermute x14, starting transfers between devices: 20.3 us -> 19 us  [swap(): lax.ppermute(block, axis, [(i, i ^ mask) for i in range(lax.axis_size(axi...]
  transfers between devices with their start and end apart: 14 -> 14, of which waited for: 9 -> 6; matrix products, arithmetic and copies ran while one was open for 0% -> 0% of each run, Pallas kernels for 18% -> 21%
where the time goes in v2:
time: 70.4 us; the launch traced here: 69.5 us
  Pallas kernels  27.1 us (38%)
  starting transfers between devices  19 us (27%)
  waiting for transfers between devices  16 us (23%)
  local copies, waits for them, and re-layouts  5.82 us (8%)
  between operations  1.49 us (2%)
    ppermute x14, starting transfers between devices, swap(): lax.ppermute(block, axis, [(i, i ^ mask) for i in range(lax.axis_size(axi...  19 us
    ppermute x14, waiting for transfers between devices, swap(): lax.ppermute(block, axis, [(i, i ^ mask) for i in range(lax.axis_size(axi...  16 us
    pallas_call x1, Pallas kernels, body(): pl.pallas_call(rhs_kernel, grid=(4,), in_specs=[SMEM, SMEM, comps(2), com...  10.2 us
    unnamed x30, local copies, waits for them, and re-layouts  5.82 us
    pallas_call x1, Pallas kernels, body(): pl.pallas_call(output_kernel, grid=(4,), in_specs=[SMEM, pair, pair, x_ne...  5.09 us
    pallas_call x1, Pallas kernels, body(): pl.pallas_call(primal_kernel, grid=(4,), in_specs=[SMEM, pair, pair, comp...  4.37 us
    pallas_call x4, Pallas kernels, gradient(): pl.pallas_call(lambda *refs: gradient_kernel(k, *refs), grid=(1,), in_spe...  4.08 us
    pallas_call x1, Pallas kernels, body(): pl.pallas_call(adjoint_kernel, grid=(4,), in_specs=[pair] * 4 + [const(CZ...  2.1 us
  transfers between devices with their start and end apart: 14, of which 6 were waited for; matrix products, arithmetic and copies ran while one was open for 0% of the time, Pallas kernels for 21%

profile of v2, /device:TPU:1, one launch (start us, length us, event | category | flops | bytes accessed | tf_op | source)
XLA Modules:
  0.0 69.5 jit_solution(2890174140438215909)
XLA Ops:
  1.3 10.2 %right_hand_sides.1 = (f32[8,256,128]{2,1,0:T(8,128)}, f32[8,256,128]{2,1,0:T(8,128)}, f32[8,256,128]{2,1,0:T(8,128)}, f32[8,256,128]{2,1,0:T(8,128)}, f32[8,256...) custom-call(s32[1]{0:T(128)S(6)} %copy.14.angle, f32[4]{0:T(128)} %refs_0_.7, ...), custom_call_target="tpu_custom_call" | custom-call | flops 1000 | bytes 18000000 | tf_op jit(solution)/shard_map/right_hand_sides/pallas_call | solution.py:490
  11.5 1.5 %collective-permute-start = (f32[17,8,128]{2,1,0:T(8,128)}, f32[17,8,128]{2,1,0:T(8,128)S(1)}, u32[]{:S(2)}, u32[]{:S(2)}) collective-permute-start(f32[17,8,128]{2,1,0:T(8,128)} %get-tuple-element.25), channel_id=1, source_target_pairs={{0,1},{1,0},{2,3},{3,2},{4,5},{5,4},{6,7},{7,6},{8,9},{9,8},{10,11... | collective-permute-start | bytes 208904 | tf_op jit(solution)/shard_map/ppermute | solution.py:449
  13.0 1.1 %collective-permute-done.other.a1 = f32[17,8,128]{2,1,0:T(8,128)S(1)} collective-permute-done((f32[17,8,128]{2,1,0:T(8,128)}, f32[17,8,128]{2,1,0:T(8,128)S(1)}, u32[]{:S(2)}, u32[]{:S(2)}) %collective-permute-start) | collective-permute-done | bytes 69664 | tf_op jit(solution)/shard_map/ppermute | solution.py:449
  15.0 3.9 %collective-permute-start.3 = (f32[17,8,128]{2,1,0:T(8,128)S(1)}, f32[17,8,128]{2,1,0:T(8,128)S(1)}, u32[]{:S(2)}, u32[]{:S(2)}) collective-permute-start(f32[17,8,128]{2,1,0:T(8,128)S(1)} %chip.1.after.m0), channel_id=1, source_target_pairs={{0,6},{1,7},{2,4},{3,5},{4,2},{5,3},{6,0},{7,1},{8,14},{9,15},{10,... | collective-permute-start | bytes 208904 | tf_op jit(solution)/shard_map/ppermute | solution.py:449
  19.6 1.2 %copy-done.4 = f32[8,256,128]{2,1,0:T(8,128)S(1)} copy-done((f32[8,256,128]{2,1,0:T(8,128)S(1)}, f32[8,256,128]{2,1,0:T(8,128)}, u32[]{:S(2)}) %copy-start.4) | copy-done | bytes 1048600
  20.9 1.2 %copy-done.5 = f32[8,256,128]{2,1,0:T(8,128)S(1)} copy-done((f32[8,256,128]{2,1,0:T(8,128)S(1)}, f32[8,256,128]{2,1,0:T(8,128)}, u32[]{:S(2)}) %copy-start.5) | copy-done | bytes 1048600
  22.1 1.2 %copy-done.10 = f32[8,256,128]{2,1,0:T(8,128)S(1)} copy-done((f32[8,256,128]{2,1,0:T(8,128)S(1)}, f32[8,256,128]{2,1,0:T(8,128)}, u32[]{:S(2)}) %copy-start.10) | copy-done | bytes 1048600
  23.3 1.2 %copy-done.11 = f32[8,256,128]{2,1,0:T(8,128)S(1)} copy-done((f32[8,256,128]{2,1,0:T(8,128)S(1)}, f32[8,256,128]{2,1,0:T(8,128)}, u32[]{:S(2)}) %copy-start.11) | copy-done | bytes 1048600
  24.6 2.1 %adjoint_products.1.after.part = f32[8,256,128]{2,1,0:T(8,128)S(1)} custom-call(f32[8,256,128]{2,1,0:T(8,128)S(1)} %copy-done.10, f32[8,256,128]{2,1,0:T(8,128)S(1)} %copy-done.11, f32[8,256,128]{2,1,0:T(8,128)S(1)} %copy-done.4, f32[8,256,128]{2,1,0:T(8,128)S(1)} %copy-done.5, f32[128,128]{1,0:T(8,128)S(1)} %copy-done.7, f32[17,8,128]{2,1,0:T(8,128)S(1)} %chip.1.after.m0), custom_call_target="tpu_custom_call" | custom-call | flops 1000 | bytes 9000000 | tf_op jit(solution)/shard_map/adjoint_products/pallas_call | solution.py:515
  26.8 2.6 %collective-permute-start.6 = (f32[17,8,128]{2,1,0:T(8,128)S(1)}, f32[17,8,128]{2,1,0:T(8,128)S(1)}, u32[]{:S(2)}, u32[]{:S(2)}) collective-permute-start(f32[17,8,128]{2,1,0:T(8,128)S(1)} %group.1.after.n0), channel_id=1, source_target_pairs={{0,24},{1,25},{2,26},{3,27},{4,28},{5,29},{6,30},{7,31},{8,16},{9,... | collective-permute-start | bytes 208904 | tf_op jit(solution)/shard_map/ppermute | solution.py:449
  30.2 4.4 %primal_products.1 = (f32[8,256,128]{2,1,0:T(8,128)S(1)}, f32[8,256,128]{2,1,0:T(8,128)S(1)}, f32[8,256,128]{2,1,0:T(8,128)S(1)}) custom-call(f32[4]{0:T(128)S(1)} %copy-done.14, f32[8,256,128]{2,1,0:T(8,128)S(1)} %copy-done.8, f32[8,256,128]{2,1,0:T(8,128)S(1)} %copy-done.9, f32[3,8,256,128]{3,2,1,0:T(8,128)S(1)} %bitcast.21, ...), custom_call_target="tpu_custom_call" | custom-call | flops 1000 | bytes 12000000 | tf_op jit(solution)/shard_map/primal_products/pallas_call | solution.py:529
  34.8 1.8 %collective-permute-start.7 = (f32[12,8,128]{2,1,0:T(8,128)S(1)}, f32[12,8,128]{2,1,0:T(8,128)S(1)}, u32[]{:S(2)}, u32[]{:S(2)}) collective-permute-start(f32[12,8,128]{2,1,0:T(8,128)S(1)} %get-tuple-element.29), channel_id=1, source_target_pairs={{0,1},{1,0},{2,3},{3,2},{4,5},{5,4},{6,7},{7,6},{8,9},{9,8},{10,11... | collective-permute-start | bytes 147464 | tf_op jit(solution)/shard_map/ppermute | solution.py:449
  36.6 0.9 %collective-permute-done.7.recv.refs_7_ = f32[12,8,128]{2,1,0:T(8,128)S(1)} collective-permute-done((f32[12,8,128]{2,1,0:T(8,128)S(1)}, f32[12,8,128]{2,1,0:T(8,128)S(1)}, u32[]{:S(2)}, u32[]{:S(2)}) %collective-permute-start.7) | collective-permute-done | bytes 49184 | tf_op jit(solution)/shard_map/ppermute | solution.py:449
  37.5 1.0 %gradient_2.1 = f32[2,256,128]{2,1,0:T(8,128)S(1)} custom-call(f32[4]{0:T(128)S(1)} %copy-done.14, f32[8,256,128]{2,1,0:T(8,128)S(1)} %get-tuple-element.32.refs_1_, f32[8,256,128]{2,1,0:T(8,128)S(1)} %copy-done.4, f32[8,256,128]{2,1,0:T(8,128)S(1)} %copy-done.6, f32[3,8,256,128]{3,2,1,0:T(8,128)S(1)} %bitcast.11, s32[8,256,128]{2,1,0:T(8,128)S(1)} %copy-done.2, ...), custom_call_target="tpu_custom_call" | custom-call | flops 1000 | bytes 3000000 | tf_op jit(solution)/shard_map/gradient_2/pallas_call | solution.py:555
  38.5 3.0 %collective-permute-start.8 = (f32[2,256,128]{2,1,0:T(8,128)S(1)}, f32[2,256,128]{2,1,0:T(8,128)S(1)}, u32[]{:S(2)}, u32[]{:S(2)}) collective-permute-start(f32[2,256,128]{2,1,0:T(8,128)S(1)} %gradient_2.1), channel_id=1, source_target_pairs={{0,64},{32,96},{64,0},{96,32},{1,65},{33,97},{65,1},{97,33},{2,66}... | collective-permute-start | bytes 786440 | tf_op jit(solution)/shard_map/ppermute | solution.py:449
  41.5 1.0 %gradient_1.1 = f32[2,256,128]{2,1,0:T(8,128)S(1)} custom-call(f32[4]{0:T(128)S(1)} %copy-done.14, f32[8,256,128]{2,1,0:T(8,128)S(1)} %get-tuple-element.32.refs_1_, f32[8,256,128]{2,1,0:T(8,128)S(1)} %copy-done.4, f32[8,256,128]{2,1,0:T(8,128)S(1)} %copy-done.6, f32[3,8,256,128]{3,2,1,0:T(8,128)S(1)} %bitcast.12, s32[8,256,128]{2,1,0:T(8,128)S(1)} %copy-done.2, ...), custom_call_target="tpu_custom_call" | custom-call | flops 1000 | bytes 3000000 | tf_op jit(solution)/shard_map/gradient_1/pallas_call | solution.py:555
  43.0 1.0 %gradient_3.1 = f32[2,256,128]{2,1,0:T(8,128)S(1)} custom-call(f32[4]{0:T(128)S(1)} %copy-done.14, f32[8,256,128]{2,1,0:T(8,128)S(1)} %get-tuple-element.32.refs_1_, f32[8,256,128]{2,1,0:T(8,128)S(1)} %copy-done.4, f32[8,256,128]{2,1,0:T(8,128)S(1)} %copy-done.6, f32[3,8,256,128]{3,2,1,0:T(8,128)S(1)} %bitcast.13, s32[8,256,128]{2,1,0:T(8,128)S(1)} %copy-done.2, ...), custom_call_target="tpu_custom_call" | custom-call | flops 1000 | bytes 3000000 | tf_op jit(solution)/shard_map/gradient_3/pallas_call | solution.py:555
  44.5 1.0 %gradient_0.1 = f32[2,256,128]{2,1,0:T(8,128)S(1)} custom-call(f32[4]{0:T(128)S(1)} %copy-done.14, f32[8,256,128]{2,1,0:T(8,128)S(1)} %get-tuple-element.32.refs_1_, f32[8,256,128]{2,1,0:T(8,128)S(1)} %copy-done.4, f32[8,256,128]{2,1,0:T(8,128)S(1)} %copy-done.6, f32[3,8,256,128]{3,2,1,0:T(8,128)S(1)} %bitcast.14, s32[8,256,128]{2,1,0:T(8,128)S(1)} %copy-done.2, ...), custom_call_target="tpu_custom_call" | custom-call | flops 1000 | bytes 3000000 | tf_op jit(solution)/shard_map/gradient_0/pallas_call | solution.py:555
  45.6 2.1 %collective-permute-done.8 = f32[2,256,128]{2,1,0:T(8,128)S(1)} collective-permute-done((f32[2,256,128]{2,1,0:T(8,128)S(1)}, f32[2,256,128]{2,1,0:T(8,128)S(1)}, u32[]{:S(2)}, u32[]{:S(2)}) %collective-permute-start.8) | collective-permute-done | bytes 262176 | tf_op jit(solution)/shard_map/ppermute | solution.py:449
  47.7 6.0 %collective-permute-done.9 = f32[2,256,128]{2,1,0:T(8,128)S(1)} collective-permute-done((f32[2,256,128]{2,1,0:T(8,128)S(1)}, f32[2,256,128]{2,1,0:T(8,128)S(1)}, u32[]{:S(2)}, u32[]{:S(2)}) %collective-permute-start.9) | collective-permute-done | bytes 262176 | tf_op jit(solution)/shard_map/ppermute | solution.py:449
  53.7 3.1 %collective-permute-start.13 = (f32[2,256,128]{2,1,0:T(8,128)S(1)}, f32[2,256,128]{2,1,0:T(8,128)S(1)}, u32[]{:S(2)}, u32[]{:S(2)}) collective-permute-start(f32[2,256,128]{2,1,0:T(8,128)S(1)} %add_add_fusion.g0), channel_id=1, source_target_pairs={{0,96},{32,64},{64,32},{96,0},{1,97},{33,65},{65,33},{97,1},{2,98}... | collective-permute-start | bytes 786440 | tf_op jit(solution)/shard_map/ppermute | solution.py:449
  57.5 5.1 %outputs.1 = (f32[3,8,256,128]{3,2,1,0:T(8,128)}, f32[3,8,256,128]{3,2,1,0:T(8,128)}) custom-call(f32[4]{0:T(128)S(1)} %copy-done.14, f32[8,256,128]{2,1,0:T(8,128)S(1)} %get-tuple-element.26.after.ex, f32[8,256,128]{2,1,0:T(8,128)S(1)} %get-tuple-element.27.ey.ey_next, f32[8,256,128]{2,1,0:T(8,128)S(1)} %get-tuple-element.27.ey.ey_next, ...), custom_call_target="tpu_custom_call" | custom-call | flops 1000 | bytes 18000000 | tf_op jit(solution)/shard_map/outputs/pallas_call | solution.py:572
  62.6 5.5 %collective-permute-done.13.g3 = f32[2,256,128]{2,1,0:T(8,128)S(1)} collective-permute-done((f32[2,256,128]{2,1,0:T(8,128)S(1)}, f32[2,256,128]{2,1,0:T(8,128)S(1)}, u32[]{:S(2)}, u32[]{:S(2)}) %collective-permute-start.13) | collective-permute-done | bytes 262176 | tf_op jit(solution)/shard_map/ppermute | solution.py:449
  68.5 1.0 %place.1 = f32[8,256,128]{2,1,0:T(8,128)} custom-call(f32[2,256,128]{2,1,0:T(8,128)S(1)} %add_add_fusion.g0, f32[2,256,128]{2,1,0:T(8,128)S(1)} %collective-permute-done.11.g1, f32[2,256,128]{2,1,0:T(8,128)S(1)} %collective-permute-done.12.g2, f32[2,256,128]{2,1,0:T(8,128)S(1)} %collective-permute-done.13.g3), custom_call_target="tpu_custom_call" | custom-call | flops 1000 | bytes 3000000 | tf_op jit(solution)/shard_map/place/pallas_call | solution.py:589
  (47 shorter events, 4.8 us)
Async XLA Ops:
  1.3 18.4 %copy-start.7 = (f32[128,128]{1,0:T(8,128)S(1)}, f32[128,128]{1,0:T(8,128)}, u32[]{:S(2)}) copy-start(f32[128,128]{1,0:T(8,128)} %refs_8_.7) | copy-start | bytes 196612
  1.3 28.8 %copy-start.3 = (f32[1,3,8,256,128]{4,3,2,1,0:T(8,128)S(1)}, f32[1,3,8,256,128]{4,3,2,1,0:T(8,128)}, u32[]{:S(2)}) copy-start(f32[1,3,8,256,128]{4,3,2,1,0:T(8,128)} %param.12) | copy-start | bytes 9437188
  11.5 2.6 %collective-permute-start = (f32[17,8,128]{2,1,0:T(8,128)}, f32[17,8,128]{2,1,0:T(8,128)S(1)}, u32[]{:S(2)}, u32[]{:S(2)}) collective-permute-start(f32[17,8,128]{2,1,0:T(8,128)} %get-tuple-element.25), channel_id=1, source_target_pairs={{0,1},{1,0},{2,3},{3,2},{4,5},{5,4},{6,7},{7,6},{8,9},{9,8},{10,11... | collective-permute-start | bytes 208904 | tf_op jit(solution)/shard_map/ppermute | solution.py:449
  15.0 11.6 %collective-permute-start.3 = (f32[17,8,128]{2,1,0:T(8,128)S(1)}, f32[17,8,128]{2,1,0:T(8,128)S(1)}, u32[]{:S(2)}, u32[]{:S(2)}) collective-permute-start(f32[17,8,128]{2,1,0:T(8,128)S(1)} %chip.1.after.m0), channel_id=1, source_target_pairs={{0,6},{1,7},{2,4},{3,5},{4,2},{5,3},{6,0},{7,1},{8,14},{9,15},{10,... | collective-permute-start | bytes 208904 | tf_op jit(solution)/shard_map/ppermute | solution.py:449
  19.0 7.7 %collective-permute-start.2 = (f32[17,8,128]{2,1,0:T(8,128)S(1)}, f32[17,8,128]{2,1,0:T(8,128)S(1)}, u32[]{:S(2)}, u32[]{:S(2)}) collective-permute-start(f32[17,8,128]{2,1,0:T(8,128)S(1)} %chip.1.after.m0), channel_id=1, source_target_pairs={{0,4},{1,5},{2,6},{3,7},{4,0},{5,1},{6,2},{7,3},{8,12},{9,13},{10,... | collective-permute-start | bytes 208904 | tf_op jit(solution)/shard_map/ppermute | solution.py:449
  19.0 7.7 %collective-permute-start.1 = (f32[17,8,128]{2,1,0:T(8,128)S(1)}, f32[17,8,128]{2,1,0:T(8,128)S(1)}, u32[]{:S(2)}, u32[]{:S(2)}) collective-permute-start(f32[17,8,128]{2,1,0:T(8,128)S(1)} %chip.1.after.m0), channel_id=1, source_target_pairs={{0,2},{1,3},{2,0},{3,1},{4,6},{5,7},{6,4},{7,5},{8,10},{9,11},{10,... | collective-permute-start | bytes 208904 | tf_op jit(solution)/shard_map/ppermute | solution.py:449
  24.5 5.6 %copy-start.1 = (f32[1,3,8,256,128]{4,3,2,1,0:T(8,128)S(1)}, f32[1,3,8,256,128]{4,3,2,1,0:T(8,128)}, u32[]{:S(2)}) copy-start(f32[1,3,8,256,128]{4,3,2,1,0:T(8,128)} %param.11) | copy-start | bytes 9437188
  24.5 5.6 %copy-start.2 = (s32[8,256,128]{2,1,0:T(8,128)S(1)}, s32[8,256,128]{2,1,0:T(8,128)}, u32[]{:S(2)}) copy-start(s32[8,256,128]{2,1,0:T(8,128)} %refs_5_.7) | copy-start | bytes 3145732
  24.5 5.6 %copy-start.8 = (f32[8,256,128]{2,1,0:T(8,128)S(1)}, f32[8,256,128]{2,1,0:T(8,128)}, u32[]{:S(2)}) copy-start(f32[8,256,128]{2,1,0:T(8,128)} %get-tuple-element.18.rx) | copy-start | bytes 3145732
  24.6 5.6 %copy-start.9 = (f32[8,256,128]{2,1,0:T(8,128)S(1)}, f32[8,256,128]{2,1,0:T(8,128)}, u32[]{:S(2)}) copy-start(f32[8,256,128]{2,1,0:T(8,128)} %get-tuple-element.19.ry) | copy-start | bytes 3145732
  24.6 5.6 %copy-start.14 = (f32[4]{0:T(128)S(1)}, f32[4]{0:T(128)}, u32[]{:S(2)}) copy-start(f32[4]{0:T(128)} %refs_0_.7) | copy-start | bytes 52
  26.8 7.8 %collective-permute-start.6 = (f32[17,8,128]{2,1,0:T(8,128)S(1)}, f32[17,8,128]{2,1,0:T(8,128)S(1)}, u32[]{:S(2)}, u32[]{:S(2)}) collective-permute-start(f32[17,8,128]{2,1,0:T(8,128)S(1)} %group.1.after.n0), channel_id=1, source_target_pairs={{0,24},{1,25},{2,26},{3,27},{4,28},{5,29},{6,30},{7,31},{8,16},{9,... | collective-permute-start | bytes 208904 | tf_op jit(solution)/shard_map/ppermute | solution.py:449
  29.4 5.2 %collective-permute-start.5 = (f32[17,8,128]{2,1,0:T(8,128)S(1)}, f32[17,8,128]{2,1,0:T(8,128)S(1)}, u32[]{:S(2)}, u32[]{:S(2)}) collective-permute-start(f32[17,8,128]{2,1,0:T(8,128)S(1)} %group.1.after.n0), channel_id=1, source_target_pairs={{0,16},{1,17},{2,18},{3,19},{4,20},{5,21},{6,22},{7,23},{8,24},{9,... | collective-permute-start | bytes 208904 | tf_op jit(solution)/shard_map/ppermute | solution.py:449
  29.9 4.7 %collective-permute-start.4 = (f32[17,8,128]{2,1,0:T(8,128)S(1)}, f32[17,8,128]{2,1,0:T(8,128)S(1)}, u32[]{:S(2)}, u32[]{:S(2)}) collective-permute-start(f32[17,8,128]{2,1,0:T(8,128)S(1)} %group.1.after.n0), channel_id=1, source_target_pairs={{0,8},{1,9},{2,10},{3,11},{4,12},{5,13},{6,14},{7,15},{8,0},{9,1},... | collective-permute-start | bytes 208904 | tf_op jit(solution)/shard_map/ppermute | solution.py:449
  30.2 4.4 %copy-start.13 = (f32[17,8,128]{2,1,0:T(8,128)S(1)}, f32[17,8,128]{2,1,0:T(8,128)}, u32[]{:S(2)}) copy-start(f32[17,8,128]{2,1,0:T(8,128)} %get-tuple-element.24.own.a0) | copy-start | bytes 208900
  30.2 7.3 %copy-start = (f32[1,3,8,256,128]{4,3,2,1,0:T(8,128)S(1)}, f32[1,3,8,256,128]{4,3,2,1,0:T(8,128)}, u32[]{:S(2)}) copy-start(f32[1,3,8,256,128]{4,3,2,1,0:T(8,128)} %param.13) | copy-start | bytes 9437188
  30.2 7.3 %copy-start.6 = (f32[8,256,128]{2,1,0:T(8,128)S(1)}, f32[8,256,128]{2,1,0:T(8,128)}, u32[]{:S(2)}) copy-start(f32[8,256,128]{2,1,0:T(8,128)} %get-tuple-element.23.psy.refs_3_) | copy-start | bytes 3145732
  34.8 2.7 %collective-permute-start.7 = (f32[12,8,128]{2,1,0:T(8,128)S(1)}, f32[12,8,128]{2,1,0:T(8,128)S(1)}, u32[]{:S(2)}, u32[]{:S(2)}) collective-permute-start(f32[12,8,128]{2,1,0:T(8,128)S(1)} %get-tuple-element.29), channel_id=1, source_target_pairs={{0,1},{1,0},{2,3},{3,2},{4,5},{5,4},{6,7},{7,6},{8,9},{9,8},{10,11... | collective-permute-start | bytes 147464 | tf_op jit(solution)/shard_map/ppermute | solution.py:449
  38.5 9.1 %collective-permute-start.8 = (f32[2,256,128]{2,1,0:T(8,128)S(1)}, f32[2,256,128]{2,1,0:T(8,128)S(1)}, u32[]{:S(2)}, u32[]{:S(2)}) collective-permute-start(f32[2,256,128]{2,1,0:T(8,128)S(1)} %gradient_2.1), channel_id=1, source_target_pairs={{0,64},{32,96},{64,0},{96,32},{1,65},{33,97},{65,1},{97,33},{2,66}... | collective-permute-start | bytes 786440 | tf_op jit(solution)/shard_map/ppermute | solution.py:449
  42.5 11.1 %collective-permute-start.9 = (f32[2,256,128]{2,1,0:T(8,128)S(1)}, f32[2,256,128]{2,1,0:T(8,128)S(1)}, u32[]{:S(2)}, u32[]{:S(2)}) collective-permute-start(f32[2,256,128]{2,1,0:T(8,128)S(1)} %gradient_1.1), channel_id=1, source_target_pairs={{0,32},{32,0},{64,96},{96,64},{1,33},{33,1},{65,97},{97,65},{2,34}... | collective-permute-start | bytes 786440 | tf_op jit(solution)/shard_map/ppermute | solution.py:449
  44.0 9.6 %collective-permute-start.10 = (f32[2,256,128]{2,1,0:T(8,128)S(1)}, f32[2,256,128]{2,1,0:T(8,128)S(1)}, u32[]{:S(2)}, u32[]{:S(2)}) collective-permute-start(f32[2,256,128]{2,1,0:T(8,128)S(1)} %gradient_3.1), channel_id=1, source_target_pairs={{0,96},{32,64},{64,32},{96,0},{1,97},{33,65},{65,33},{97,1},{2,98}... | collective-permute-start | bytes 786440 | tf_op jit(solution)/shard_map/ppermute | solution.py:449
  53.7 14.4 %collective-permute-start.13 = (f32[2,256,128]{2,1,0:T(8,128)S(1)}, f32[2,256,128]{2,1,0:T(8,128)S(1)}, u32[]{:S(2)}, u32[]{:S(2)}) collective-permute-start(f32[2,256,128]{2,1,0:T(8,128)S(1)} %add_add_fusion.g0), channel_id=1, source_target_pairs={{0,96},{32,64},{64,32},{96,0},{1,97},{33,65},{65,33},{97,1},{2,98}... | collective-permute-start | bytes 786440 | tf_op jit(solution)/shard_map/ppermute | solution.py:449
  56.8 11.3 %collective-permute-start.12 = (f32[2,256,128]{2,1,0:T(8,128)S(1)}, f32[2,256,128]{2,1,0:T(8,128)S(1)}, u32[]{:S(2)}, u32[]{:S(2)}) collective-permute-start(f32[2,256,128]{2,1,0:T(8,128)S(1)} %add_add_fusion.g0), channel_id=1, source_target_pairs={{0,64},{32,96},{64,0},{96,32},{1,65},{33,97},{65,1},{97,33},{2,66}... | collective-permute-start | bytes 786440 | tf_op jit(solution)/shard_map/ppermute | solution.py:449
  57.2 11.4 %collective-permute-start.11 = (f32[2,256,128]{2,1,0:T(8,128)S(1)}, f32[2,256,128]{2,1,0:T(8,128)S(1)}, u32[]{:S(2)}, u32[]{:S(2)}) collective-permute-start(f32[2,256,128]{2,1,0:T(8,128)S(1)} %add_add_fusion.g0), channel_id=1, source_target_pairs={{0,32},{32,0},{64,96},{96,64},{1,33},{33,1},{65,97},{97,65},{2,34}... | collective-permute-start | bytes 786440 | tf_op jit(solution)/shard_map/ppermute | solution.py:449
  (5 other events, 5.8 us)

commit v3 on v2

v3 whole, which is shorter than its diff:
```python
import jax
import jax.numpy as jnp
from jax import lax
from jax.experimental import pallas as pl
from jax.experimental.pallas import tpu as pltpu
from jax.sharding import PartitionSpec as P

F32 = jnp.float32
BF = jnp.bfloat16
X, Y, CZ = 8, 256, 128
NN = (((1,), (0,)), ((), ()))
NT = (((1,), (1,)), ((), ()))
SLABS = 17
MIB = 1024 * 1024


def split(v):
    one = v.astype(BF)
    rest = v - one.astype(F32)
    two = rest.astype(BF)
    three = (rest - two.astype(F32)).astype(BF)
    return one, two, three


def mm(a, b, dims=NN):
    return lax.dot_general(a, b, dims, preferred_element_type=F32)


def iota(shape, axis):
    return lax.broadcasted_iota(jnp.int32, shape, axis)


def y_down(v):
    return v - jnp.where(iota(v.shape, 0) == 0, 0.0, pltpu.roll(v, 1, 0))


def y_up(v):
    n = v.shape[0]
    return jnp.where(iota(v.shape, 0) == n - 1, 0.0, pltpu.roll(v, n - 1, 0)) - v


def z_down(v):
    return v - jnp.where(iota(v.shape, 1) == 0, 0.0, pltpu.roll(v, 1, 1))


def z_up(v):
    n = v.shape[1]
    return jnp.where(iota(v.shape, 1) == n - 1, 0.0, pltpu.roll(v, n - 1, 1)) - v


def inverse_eps(labels, eps_ref):
    rows = [1.0 / jnp.full((1, CZ), eps_ref[r], F32) for r in range(4)]
    out = jnp.where(labels == 2, rows[2], rows[3])
    out = jnp.where(labels == 1, rows[1], out)
    return jnp.where(labels == 0, rows[0], out)


def six_rows(rows):
    one, two, three = (part.astype(F32) for part in split(rows))
    return [one, two, three, one, two, one]


def six_table(line, piece):
    one, two, three = (part.astype(F32) for part in split(line))
    return jnp.where(piece < 3, one, jnp.where(piece < 5, two, three))


def rhs_kernel(
    angle, eps, e, h, ge, gh, lab, prof_in, zs_in, lt_in, w_in,
    rx_o, ry_o, ax_o, ay_o, psx_o, psy_o, gs_o, inv_o, ez_o, h_o, w, keep_o, send_o,
    e_s, ge_s, gh_s, lab_s, sems, prof_s, prof, zs, lt,
):
    core = lax.rem(lax.axis_index("gz"), 2)

    def fetch(which, x):
        at = pl.ds(x, 1)
        return (
            lambda: pltpu.make_async_copy(lab.at[at], lab_s.at[at], sems.at[0, x]),
            lambda: pltpu.make_async_copy(ge.at[:, at], ge_s.at[:, at], sems.at[1, x]),
            lambda: pltpu.make_async_copy(h.at[:, at], h_o.at[:, at], sems.at[2, x]),
            lambda: pltpu.make_async_copy(gh.at[:, at], gh_s.at[:, at], sems.at[3, x]),
            lambda: pltpu.make_async_copy(e.at[pl.ds(0, 2), at], e_s.at[:, at], sems.at[4, x]),
        )[which]()

    tables = [
        pltpu.make_async_copy(source, target, sems.at[5, n + 1])
        for n, (source, target) in enumerate(
            ((prof_in.at[angle[0]], prof), (w_in, w), (zs_in, zs), (lt_in, lt))
        )
    ]
    for copy in tables:
        copy.start()
    early, late = (0, 1), (2, 3, 4)
    for which in early:
        fetch(which, 0).start()
    for x in range(X):
        if x + 1 < X:
            for which in early:
                fetch(which, x + 1).start()
        for which in late:
            fetch(which, x).start()
    ez_copy = pltpu.make_async_copy(e.at[2], ez_o, sems.at[5, 0])
    ez_copy.start()

    for copy in tables:
        copy.wait()
    both = jnp.concatenate([prof[0], prof[1]], 0)
    rows = jnp.concatenate(six_rows(both) + [jnp.zeros((32, Y), F32)], 0)
    prof_s[...] = rows.T.astype(BF)
    corners = [
        jnp.broadcast_to(w[p:p + 1, q:q + 1], (1, CZ))
        for p, q in ((0, 0), (0, CZ - 1), (CZ - 1, CZ - 1))
    ]
    corners = jnp.concatenate(corners + [jnp.zeros((5, CZ), F32)], 0)
    keep_o[16] = corners
    send_o[16] = corners

    row16 = iota((16, CZ), 0)
    lane16 = iota((16, CZ), 1)
    ends = jnp.where(row16 < 8, w[0:1, :], w[CZ - 1:CZ, :])
    ends_parts = [part.astype(F32) for part in split(ends)]
    slot = lax.rem(row16, 8)

    rowz = iota((CZ, CZ), 0)
    piece, within = rowz // 16, lax.rem(rowz, 16)
    z_table = jnp.where(piece < 6, six_table(zs[...], piece), 0.0)

    lane = iota((Y, CZ), 1)
    row_y = iota((16, Y), 0)
    for which in early:
        fetch(which, 0).wait()
    inv_o[0] = inverse_eps(lab_s[0], eps)

    def one_pair(i, carry):
        acc_ends = jnp.zeros((16, Y), F32)
        acc_tops = jnp.zeros((16, Y), F32)
        for j in range(2):
            x = 2 * i + j
            following = jnp.minimum(x + 1, X - 1)
            previous = jnp.maximum(x - 1, 0)
            more = (x < X - 1).astype(F32)
            less = (x > 0).astype(F32)

            @pl.when(x < X - 1)
            def _():
                for which in early:
                    fetch(which, x + 1).wait()

            for which in late:
                fetch(which, x).wait()
            inv = inv_o[x]
            inv_up = inverse_eps(lab_s[following], eps)
            inv_o[following] = inv_up
            sg = inv * ge_s[2, x]
            sg_up = inv_up * ge_s[2, following] * more
            z_pick = jnp.concatenate(
                [jnp.where(within == x, z_table, 0.0), jnp.where(within == 8 + x, z_table, 0.0)], 1
            ).astype(BF)
            cur = mm(prof_s[...], z_pick)
            h_x, h_y, h_z = h_o[0, x], h_o[1, x], h_o[2, x]
            g_hz = gh_s[2, x]
            bar_hy = gh_s[1, x] - (sg_up - sg)
            bar_hx = gh_s[0, x] + y_up(sg)
            p_x = y_down(h_z) - z_down(h_y) - cur[:, :CZ]
            p_y = z_down(h_x) - (h_z - h_o[2, previous] * less) - cur[:, CZ:]
            r_x = lt[...] * e_s[0, x] + inv * p_x
            r_y = lt[...] * e_s[1, x] + inv * p_y
            a_x = ge_s[0, x] - y_down(g_hz) - z_down(bar_hy)
            a_y = ge_s[1, x] + (g_hz - gh_s[2, previous] * less) - z_down(bar_hx)
            rx_o[x], ry_o[x], ax_o[x], ay_o[x] = r_x, r_y, a_x, a_y
            psx_o[x] = -inv * (inv * p_x)
            psy_o[x] = -inv * (inv * p_y)
            gs_o[x] = -inv * sg
            thirds = []
            for c, field in enumerate((r_x, r_y, a_x, a_y)):
                one, two, three = split(field)
                mask = slot == 4 * j + c
                w1, w2, w3 = (jnp.where(mask, part, 0.0) for part in ends_parts)
                lhs = jnp.concatenate(
                    [
                        jnp.concatenate([w1, w1], 1),
                        jnp.concatenate([w2, w2], 1),
                        jnp.concatenate([w3, jnp.zeros_like(w3)], 1),
                    ],
                    0,
                ).astype(BF)
                out = mm(lhs, jnp.concatenate([one, two], 1), NT)
                acc_ends += out[0:16] + out[16:32] + out[32:48]
                thirds.append((w1, three))
            for c in (0, 2):
                (wa, ta), (wb, tb) = thirds[c], thirds[c + 1]
                lhs = jnp.concatenate([wa, wb], 1).astype(BF)
                acc_ends += mm(lhs, jnp.concatenate([ta, tb], 1), NT)

            packed = jnp.where(lane == CZ - 1, h_y, inv)
            packed = jnp.where(lane == CZ - 2, -pltpu.roll(h_x, CZ - 1, 1), packed)
            packed = jnp.where(lane == CZ - 3, pltpu.roll(bar_hy, CZ - 2, 1), packed)
            packed = jnp.where(lane == CZ - 4, pltpu.roll(bar_hx, CZ - 3, 1), packed)
            one, two, three = split(packed)
            c16 = slot - 4 * j
            own = (c16 >= 0) & (c16 < 4)
            pick = jnp.where(
                own & (row16 < 8) & (lane16 == CZ - 1 - c16), 1.0,
                jnp.where(own & (row16 >= 8) & (c16 < 2) & (lane16 == 0), 1.0, 0.0),
            )
            acc_tops += mm(jnp.concatenate([pick, pick], 1).astype(BF), jnp.concatenate([one, two], 1), NT)
            acc_tops += mm(pick.astype(BF), three, NT)

        acc_tops = jnp.where((row_y >= 8) & (lax.rem(row_y, 4) >= 2), 1.0, acc_tops)
        for base, acc in ((0, acc_ends), (8, acc_tops)):
            low, high = acc[:, :CZ], acc[:, CZ:]
            keep = jnp.where(core == 0, low, high)
            send = jnp.where(core == 0, high, low)
            for part in range(2):
                keep_o[base + 4 * part + i] = keep[8 * part:8 * part + 8]
                send_o[base + 4 * part + i] = send[8 * part:8 * part + 8]
        return carry

    lax.fori_loop(0, X // 2, one_pair, 0)
    ez_copy.wait()


def unpack(ref):
    m = ref[...]
    return dict(
        f=m[0:4], l=m[4:8], t=m[8:12], k=m[12:16],
        a=m[16, 0:1, :], c=m[16, 1:2, :], z=m[16, 2:3, :],
    )


def repack(s, ref):
    ref[0:4] = s["f"]
    ref[4:8] = s["l"]
    ref[8:12] = s["t"]
    ref[12:16] = s["k"]
    ref[16] = jnp.concatenate([s["a"], s["c"], s["z"], jnp.zeros((5, CZ), F32)], 0)


def order(bit, own, other):
    lower = {n: jnp.where(bit == 0, own[n], other[n]) for n in own}
    upper = {n: jnp.where(bit == 0, other[n], own[n]) for n in own}
    return lower, upper


def coupled(lower, upper):
    delta = upper["k"] * lower["t"]
    f_up = upper["f"] + upper["a"] * delta
    l_up = upper["l"] + upper["c"] * delta
    inv = 1.0 / (1.0 - upper["a"] * lower["z"])
    return f_up, l_up, inv


def combine(lower, upper):
    f_up, l_up, inv = coupled(lower, upper)
    t = (f_up + upper["a"] * lower["l"]) * inv
    u = (lower["l"] + lower["z"] * f_up) * inv
    return dict(
        f=lower["f"] + lower["c"] * t,
        l=l_up + upper["c"] * u,
        t=upper["t"],
        k=lower["k"],
        a=lower["a"] + lower["c"] * lower["c"] * upper["a"] * inv,
        c=lower["c"] * upper["c"] * inv,
        z=upper["z"] + upper["c"] * upper["c"] * lower["z"] * inv,
    )


def outside(lower, upper, below, above):
    f_up, _, inv = coupled(lower, upper)
    l_low = lower["l"] + lower["c"] * below
    f_up = f_up + upper["c"] * above
    return (f_up + upper["a"] * l_low) * inv, (l_low + lower["z"] * f_up) * inv


def pick_outside(bit, lower, upper, below, above):
    t, u = outside(lower, upper, below, above)
    return jnp.where(bit == 0, below, u), jnp.where(bit == 0, t, above)


def bits():
    gz = lax.axis_index("gz")
    core, low_z, high_z = lax.rem(gz, 2), lax.rem(gz // 2, 2), lax.rem(gz // 4, 2)
    return core, low_z, high_z, lax.rem(gz // 8, 2), gz // 16


def chip_kernel(own, other, out):
    core = bits()[0]
    repack(combine(*order(core, unpack(own), unpack(other))), out)


def four(low, high, own, m1, m2, m3):
    first = order(low, own, m1)
    pair = combine(*first)
    return first, order(high, pair, combine(*order(low, m2, m3)))


def group_kernel(m0, m1, m2, m3, after, out):
    _, low, high, _, _ = bits()
    repack(combine(*four(low, high, *(unpack(m) for m in (m0, m1, m2, m3)))[1]), out)


def back_kernel(a0, a1, m0, m1, m2, m3, n0, n1, n2, n3, after, keep_o, send_o):
    core, zl, zh, xl, xh = bits()
    chip = order(core, unpack(a0), unpack(a1))
    m0, m1, m2, m3 = (unpack(m) for m in (m0, m1, m2, m3))
    n0, n1, n2, n3 = (unpack(n) for n in (n0, n1, n2, n3))
    z_first, z_second = four(zl, zh, m0, m1, m2, m3)
    x_first, x_second = four(xl, xh, n0, n1, n2, n3)
    zero = jnp.zeros_like(m0["f"])
    edge = (zero, zero)
    edge = pick_outside(xh, *x_second, *edge)
    edge = pick_outside(xl, *x_first, *edge)
    edge = pick_outside(zh, *z_second, *edge)
    edge = pick_outside(zl, *z_first, *edge)
    lower, upper = chip
    t, u = outside(lower, upper, *edge)
    under_x = jnp.where(xl == 1, n1["t"], jnp.where(xh == 1, n3["t"], zero))
    under = jnp.where(zl == 1, m1["t"], jnp.where(zh == 1, m3["t"], under_x))
    results = []
    for block, below, above, plane in ((lower, edge[0], t, under), (upper, u, edge[1], lower["t"])):
        below = below + block["k"] * plane
        first = block["f"] + block["a"] * below + block["c"] * above
        extra = jnp.stack([first[q] * pltpu.roll(plane[q], 2, 0) for q in range(4)])
        results.append((below, above, extra))
    for part in range(3):
        low, high = results[0][part], results[1][part]
        keep_o[4 * part:4 * part + 4] = jnp.where(core == 0, low, high)
        send_o[4 * part:4 * part + 4] = jnp.where(core == 0, high, low)


def product_tables(w):
    one, two, three = split(w.T)
    full = jnp.concatenate([one, two], 1)
    return jnp.concatenate([full, full], 0), jnp.concatenate([one, three], 0)


def product(field, tables):
    one, two, three = split(field)
    wide = mm(jnp.concatenate([one, two], 1), tables[0])
    narrow = mm(jnp.concatenate([three, one], 1), tables[1])
    return wide[:, :CZ] + wide[:, CZ:] + narrow


def adjoint_kernel(ax, ay, psx, psy, w, after, out):
    tables = product_tables(w[...])

    def one(x, carry):
        out[x] = psx[x] * product(ax[x], tables) + psy[x] * product(ay[x], tables)
        return carry

    lax.fori_loop(0, X, one, 0, unroll=2)


def primal_kernel(rx, ry, h, ez, gs, part, w, after, ex_o, ey_o, grad_o):
    tables = product_tables(w[...])

    def one(x, hy_prev):
        more = (x < X - 1).astype(F32)
        e_x, e_y = product(rx[x], tables), product(ry[x], tables)
        ex_o[x], ey_o[x] = e_x, e_y
        e_z = ez[x]
        hy = h[1, x] + z_up(e_x) - (ez[jnp.minimum(x + 1, X - 1)] * more - e_z)
        hx = h[0, x] + z_up(e_y) - y_up(e_z)
        grad_o[x] = part[x] + gs[x] * (hy - hy_prev - y_down(hx))
        return hy

    lax.fori_loop(0, X, one, jnp.zeros((Y, CZ), F32), unroll=2)


def edge_rows(keep, recv, slab):
    core = lax.rem(lax.axis_index("gz"), 2)
    a, b = keep[slab], recv[slab]
    return jnp.concatenate([jnp.where(core == 0, a, b), jnp.where(core == 0, b, a)], 1)


def columns(below, above):
    rows = six_rows(below) + six_rows(above) + [jnp.zeros((32, Y), F32)]
    return jnp.concatenate(rows, 0).T.astype(BF)


def edge_table(first, last):
    piece = iota((CZ, CZ), 0) // 8
    table = jnp.where(piece < 6, six_table(first, piece), six_table(last, piece - 6))
    return jnp.where(piece < 12, table, 0.0)


def picked(table, row):
    return jnp.where(lax.rem(iota((CZ, CZ), 0), 8) == row, table, 0.0)


def gradient_kernel(k, grad, psx, psy, gs, inv, keep, recv, w, out):
    q = lax.axis_index("src") ^ k
    below, above, extra = (edge_rows(keep, recv, 4 * part + q) for part in range(3))
    before = jnp.maximum(q - 1, 0)
    has = (q > 0).astype(F32)
    row = iota((8, Y), 0)
    lane = iota((8, Y), 1)

    def curl_rows(now, previous):
        shifted = jnp.where(row < 4, pltpu.roll(previous, 4, 0), pltpu.roll(now, 4, 0))
        along_y = now - jnp.where(lane == 0, 0.0, pltpu.roll(now, 1, 1))
        return now - shifted - pltpu.roll(along_y, 7, 0)

    curl_below = curl_rows(below, edge_rows(keep, recv, before) * has)
    curl_above = curl_rows(above, edge_rows(keep, recv, 4 + before) * has)
    kind = lax.rem(row, 4)
    plane = pltpu.roll(extra, 7, 0) + pltpu.roll(extra, 6, 0)
    below = jnp.where(kind == 0, curl_below, jnp.where(kind == 1, plane, below))
    above = jnp.where(kind == 0, curl_above, jnp.where(kind == 1, 0.0, above))
    cols = columns(below, above)
    wt = w[...].T
    first, last = wt[0:1, :], wt[CZ - 1:CZ, :]
    lane1 = iota((1, CZ), 1)
    top = jnp.where(lane1 == CZ - 1, 1.0, 0.0)
    first_up = jnp.where(lane1 == CZ - 1, 0.0, pltpu.roll(first, CZ - 1, 1)) - first
    last_up = jnp.where(lane1 == CZ - 1, 0.0, pltpu.roll(last, CZ - 1, 1)) - last + top
    lam_table = edge_table(first, last)
    curl_table = edge_table(first_up, last_up)
    plane_table = edge_table(jnp.where(lane1 == 0, 1.0, 0.0), jnp.zeros((1, CZ), F32))
    for j in range(2):
        r = 4 * j
        lam = mm(cols, jnp.concatenate([picked(lam_table, r + 2), picked(lam_table, r + 3)], 1).astype(BF))
        rest = mm(cols, jnp.concatenate([picked(curl_table, r), picked(plane_table, r + 1)], 1).astype(BF))
        x = 2 * q + j
        out[j] = (
            grad[x] + psx[x] * lam[:, :CZ] + psy[x] * lam[:, CZ:]
            + gs[x] * rest[:, :CZ] - inv[x] * inv[x] * rest[:, CZ:]
        )


def output_kernel(ex, ey, h, ez, inv, keep, recv, w, e_o, h_o, e_s, h_s, sems):
    wt = w[...].T
    table = edge_table(wt[0:1, :], wt[CZ - 1:CZ, :])
    lane = iota((CZ, CZ), 1)
    piece = iota((CZ, CZ), 0) // 8
    ones = jnp.where((piece >= 6) & (piece < 9) & (lane == CZ - 1), 1.0, 0.0)

    def edges(i):
        return columns(edge_rows(keep, recv, i), edge_rows(keep, recv, 4 + i))

    def corrected(source, table, row):
        return mm(source, picked(table, row).astype(BF))

    def copies(x):
        at = pl.ds(x, 1)
        return (
            pltpu.make_async_copy(e_s.at[:, at], e_o.at[:, at], sems.at[0, x]),
            pltpu.make_async_copy(h_s.at[:, at], h_o.at[:, at], sems.at[1, x]),
        )

    def one_pair(i, carry):
        cols, hy_prev = carry
        last = i == X // 2 - 1
        cols_next = edges(jnp.minimum(i + 1, X // 2 - 1))
        x = 2 * i
        more = jnp.where(last, 0.0, 1.0)
        following = jnp.minimum(x + 2, X - 1)
        e_x = [ex[x + j] + corrected(cols, table, 4 * j) for j in range(2)]
        e_y = [ey[x + j] + corrected(cols, table, 4 * j + 1) for j in range(2)]
        e_y.append((ey[following] + corrected(cols_next, table, 1)) * more)
        e_z = [ez[x], ez[x + 1], ez[following] * more]
        for j in range(2):
            hy = h[1, x + j] + z_up(e_x[j]) + corrected(cols, ones, 4 * j) - (e_z[j + 1] - e_z[j])
            hx = h[0, x + j] + z_up(e_y[j]) + corrected(cols, ones, 4 * j + 1) - y_up(e_z[j])
            curl = hy - hy_prev - y_down(hx)
            hy_prev = hy
            e_s[0, x + j] = e_x[j]
            e_s[1, x + j] = e_y[j]
            e_s[2, x + j] = e_z[j] + inv[x + j] * curl
            h_s[0, x + j] = hx
            h_s[1, x + j] = hy
            h_s[2, x + j] = h[2, x + j] - (e_y[j + 1] - e_y[j]) + y_up(e_x[j])
            for copy in copies(x + j):
                copy.start()
        return cols_next, hy_prev

    lax.fori_loop(0, X // 2, one_pair, (edges(0), jnp.zeros((Y, CZ), F32)))
    for x in range(X):
        for copy in copies(x):
            copy.wait()


def place_kernel(g0, g1, g2, g3, out, sems):
    src = lax.axis_index("src")
    copies = []
    for k, g in enumerate((g0, g1, g2, g3)):
        copies.append(pltpu.make_async_copy(g, out.at[pl.ds(2 * (src ^ k), 2)], sems.at[k]))
    for copy in copies:
        copy.start()
    for copy in copies:
        copy.wait()


def swap(block, axis, mask):
    return lax.ppermute(block, axis, [(i, i ^ mask) for i in range(lax.axis_size(axis))])


SMEM = pl.BlockSpec(memory_space=pltpu.SMEM)
VMEM = pl.BlockSpec(memory_space=pltpu.VMEM)
HBM = pl.BlockSpec(memory_space=pltpu.HBM)
ANY = pl.BlockSpec(memory_space=pl.ANY)


def shape(*dims):
    return jax.ShapeDtypeStruct(dims, F32)


def call(kernel, name, in_specs, outs, us, mib, out_specs=None, scratch=()):
    return pl.pallas_call(
        kernel,
        in_specs=in_specs,
        out_specs=out_specs or [VMEM] * len(outs),
        out_shape=outs,
        scratch_shapes=scratch,
        compiler_params=pltpu.CompilerParams(vmem_limit_bytes=mib * MIB),
        cost_estimate=pl.CostEstimate(flops=1000, bytes_accessed=int(us * 3.0e6), transcendentals=0),
        name=name,
    )


def in_hbm(array):
    return pltpu.with_memory_space_constraint(array, pltpu.HBM)


def body(
    fields_e, fields_h, cot_e, cot_h, labels, region_eps, angle_index, profiles, zsheet,
    layer_term, block_inverse,
):
    e, h, ge, gh = fields_e[0], fields_h[0], cot_e[0], cot_h[0]
    zs, lt = zsheet.reshape(1, CZ), layer_term.reshape(1, CZ)
    slab = shape(X, Y, CZ)
    message = shape(SLABS, 8, CZ)

    def space(*dims, dtype=F32):
        return pltpu.VMEM(dims, dtype)

    rx, ry, ax, ay, psx, psy, gs, inv, ez, hv, w, keep, send = call(
        rhs_kernel, "right_hand_sides",
        [SMEM, SMEM] + [HBM] * 9,
        [slab] * 9 + [shape(3, X, Y, CZ), shape(CZ, CZ)] + [message] * 2,
        6, 24,
        scratch=[
            space(2, X, Y, CZ), space(3, X, Y, CZ), space(3, X, Y, CZ),
            space(X, Y, CZ, dtype=jnp.int32), pltpu.SemaphoreType.DMA((6, X)),
            space(Y, CZ, dtype=BF), space(2, X, Y), space(1, CZ), space(1, CZ),
        ],
    )(angle_index, *map(in_hbm, (region_eps, e, h, ge, gh, labels, profiles, zs, lt, block_inverse)))

    other = swap(send, "gz", 1)
    (m0,) = call(chip_kernel, "chip", [VMEM] * 2, [message], 0.5, 4)(keep, other)
    m1, m2, m3 = (swap(m0, "gz", 2 * k) for k in (1, 2, 3))

    (adjoint,) = call(adjoint_kernel, "adjoint_products", [VMEM] * 5 + [ANY], [slab], 3, 8)(
        ax, ay, psx, psy, w, m0
    )
    (n0,) = call(group_kernel, "group", [VMEM] * 4 + [ANY], [message], 0.5, 4)(m0, m1, m2, m3, adjoint)
    n1, n2, n3 = (swap(n0, "gz", 8 * k) for k in (1, 2, 3))

    ex, ey, grad = call(primal_kernel, "primal_products", [VMEM] * 7 + [ANY], [slab] * 3, 4, 8)(
        rx, ry, hv, ez, gs, adjoint, w, n0
    )
    own_edges, send_edges = call(
        back_kernel, "back", [VMEM] * 10 + [ANY], [shape(12, 8, CZ)] * 2, 0.5, 4
    )(keep, other, m0, m1, m2, m3, n0, n1, n2, n3, ex)
    other_edges = swap(send_edges, "gz", 1)

    def gradient(k):
        return call(
            lambda *refs: gradient_kernel(k, *refs), f"gradient_{k}", [VMEM] * 8,
            [shape(2, Y, CZ)], 1, 8,
        )(grad, psx, psy, gs, inv, own_edges, other_edges, w)[0]

    arrived = [swap(gradient(k), "src", k) for k in (2, 1, 3)]
    own = gradient(0)

    e_new, h_new = call(
        output_kernel, "outputs", [VMEM] * 8, [shape(3, X, Y, CZ)] * 2, 6, 16,
        out_specs=[HBM] * 2,
        scratch=[space(3, X, Y, CZ), space(3, X, Y, CZ), pltpu.SemaphoreType.DMA((2, X))],
    )(ex, ey, hv, ez, inv, own_edges, other_edges, w)

    total = own + arrived[0] + arrived[1] + arrived[2]
    two, one, three = (swap(total, "src", k) for k in (2, 1, 3))
    (eps_grad,) = call(
        place_kernel, "place", [ANY] * 4, [slab], 1, 4, out_specs=[HBM],
        scratch=[pltpu.SemaphoreType.DMA((4,))],
    )(total, one, two, three)
    return (e_new[None], h_new[None], eps_grad)


def solution(mesh):
    field = P("src", None, None, None, "gz")
    return jax.shard_map(
        body,
        mesh=mesh,
        in_specs=(
            field, field, field, field, P(None, None, "gz"), P(), P("src"), P(), P("gz"), P("gz"),
            P("gz", None),
        ),
        out_specs=(field, field, P(None, None, "gz")),
        check_vma=False,
    )
```

time: 70.4 us -> 69.7 us (0.990)
  waiting for transfers between devices: 16 us -> 27 us
  Pallas kernels: 27.1 us -> 19 us
  local copies, waits for them, and re-layouts: 5.82 us -> 0 us
  starting transfers between devices: 19 us -> 21.5 us
    ppermute x14, waiting for transfers between devices: 16 us -> 27 us  [swap(): lax.ppermute(block, axis, [(i, i ^ mask) for i in range(lax.axis_size(axi...]
    pallas_call x12, Pallas kernels: 27.1 us -> 19 us  [the longest x1 8.13 us: body(): call(rhs_kernel, 'right_hand_sides', [SMEM, SMEM] + [HBM] * 9, [slab] * 9...]
    unnamed x30 -> x0, local copies, waits for them, and re-layouts: 5.82 us -> none
    ppermute x14, starting transfers between devices: 19 us -> 21.5 us  [swap(): lax.ppermute(block, axis, [(i, i ^ mask) for i in range(lax.axis_size(axi...]
  transfers between devices with their start and end apart: 14 -> 14, of which waited for: 6 -> 10; matrix products, arithmetic and copies ran while one was open for 0% -> 0% of each run, Pallas kernels for 21% -> 13%
where the time goes in v3:
time: 69.7 us; the launch traced here: 69 us
  waiting for transfers between devices  27 us (39%)
  starting transfers between devices  21.5 us (31%)
  Pallas kernels  19 us (27%)
  between operations  1.4 us (2%)
    ppermute x14, waiting for transfers between devices, swap(): lax.ppermute(block, axis, [(i, i ^ mask) for i in range(lax.axis_size(axi...  27 us
    ppermute x14, starting transfers between devices, swap(): lax.ppermute(block, axis, [(i, i ^ mask) for i in range(lax.axis_size(axi...  21.5 us
    pallas_call x1, Pallas kernels, body(): call(rhs_kernel, 'right_hand_sides', [SMEM, SMEM] + [HBM] * 9, [slab] * 9...  8.13 us
    pallas_call x1, Pallas kernels, body(): call(output_kernel, 'outputs', [VMEM] * 8, [shape(3, X, Y, CZ)] * 2, 6, 1...  3.57 us
    pallas_call x1, Pallas kernels, body(): call(primal_kernel, 'primal_products', [VMEM] * 7 + [ANY], [slab] * 3, 4, 8)  2.36 us
    pallas_call x4, Pallas kernels, gradient(): call(lambda *refs: gradient_kernel(k, *refs), f'gradient_{k}', [VMEM] * 8...  1.84 us
    pallas_call x1, Pallas kernels, body(): call(adjoint_kernel, 'adjoint_products', [VMEM] * 5 + [ANY], [slab], 3, 8)  1.83 us
  transfers between devices with their start and end apart: 14, of which 10 were waited for; matrix products, arithmetic and copies ran while one was open for 0% of the time, Pallas kernels for 13%

profile of v3, /device:TPU:1, one launch (start us, length us, event | category | flops | bytes accessed | tf_op | source)
XLA Modules:
  0.0 69.0 jit_solution(1477129129012517210)
XLA Ops:
  1.3 8.1 %right_hand_sides.1 = (f32[8,256,128]{2,1,0:T(8,128)S(1)}, f32[8,256,128]{2,1,0:T(8,128)S(1)}, f32[8,256,128]{2,1,0:T(8,128)S(1)}, f32[8,256,128]{2,1,0:T(8,128)...) custom-call(s32[1]{0:T(128)S(6)} %copy.14.angle, ...), custom_call_target="tpu_custom_call" | custom-call | flops 1000 | bytes 18000000 | tf_op jit(solution)/shard_map/right_hand_sides/pallas_call | solution.py:537
  9.4 1.5 %collective-permute-start = (f32[17,8,128]{2,1,0:T(8,128)S(1)}, f32[17,8,128]{2,1,0:T(8,128)S(1)}, u32[]{:S(2)}, u32[]{:S(2)}) collective-permute-start(f32[17,8,128]{2,1,0:T(8,128)S(1)} %get-tuple-element.34), channel_id=1, source_target_pairs={{0,1},{1,0},{2,3},{3,2},{4,5},{5,4},{6,7},{7,6},{8,9},{9,8},{10,11... | collective-permute-start | bytes 208904 | tf_op jit(solution)/shard_map/ppermute | solution.py:495
  10.9 0.9 %collective-permute-done.other.a1 = f32[17,8,128]{2,1,0:T(8,128)S(1)} collective-permute-done((f32[17,8,128]{2,1,0:T(8,128)S(1)}, f32[17,8,128]{2,1,0:T(8,128)S(1)}, u32[]{:S(2)}, u32[]{:S(2)}) %collective-permute-start) | collective-permute-done | bytes 69664 | tf_op jit(solution)/shard_map/ppermute | solution.py:495
  11.9 1.8 %collective-permute-start.1 = (f32[17,8,128]{2,1,0:T(8,128)S(1)}, f32[17,8,128]{2,1,0:T(8,128)S(1)}, u32[]{:S(2)}, u32[]{:S(2)}) collective-permute-start(f32[17,8,128]{2,1,0:T(8,128)S(1)} %chip.1.after.m0), channel_id=1, source_target_pairs={{0,2},{1,3},{2,0},{3,1},{4,6},{5,7},{6,4},{7,5},{8,10},{9,11},{10,... | collective-permute-start | bytes 208904 | tf_op jit(solution)/shard_map/ppermute | solution.py:495
  13.7 3.3 %collective-permute-start.2 = (f32[17,8,128]{2,1,0:T(8,128)S(1)}, f32[17,8,128]{2,1,0:T(8,128)S(1)}, u32[]{:S(2)}, u32[]{:S(2)}) collective-permute-start(f32[17,8,128]{2,1,0:T(8,128)S(1)} %chip.1.after.m0), channel_id=1, source_target_pairs={{0,4},{1,5},{2,6},{3,7},{4,0},{5,1},{6,2},{7,3},{8,12},{9,13},{10,... | collective-permute-start | bytes 208904 | tf_op jit(solution)/shard_map/ppermute | solution.py:495
  17.0 1.8 %adjoint_products.1.after.part = f32[8,256,128]{2,1,0:T(8,128)S(1)} custom-call(f32[8,256,128]{2,1,0:T(8,128)S(1)} %get-tuple-element.28.ax, f32[8,256,128]{2,1,0:T(8,128)S(1)} %get-tuple-element.29.ay, f32[8,256,128]{2,1,0:T(8,128)S(1)} %get-tuple-element.30.psx.refs_1_, f32[8,256,128]{2,1,0:T(8,128)S(1)} %get-tuple-element.31.psy.refs_2_, ...), custom_call_target="tpu_custom_call" | custom-call | flops 1000 | bytes 9000000 | tf_op jit(solution)/shard_map/adjoint_products/pallas_call | solution.py:553
  18.8 1.3 %collective-permute-done.2.m2 = f32[17,8,128]{2,1,0:T(8,128)S(1)} collective-permute-done((f32[17,8,128]{2,1,0:T(8,128)S(1)}, f32[17,8,128]{2,1,0:T(8,128)S(1)}, u32[]{:S(2)}, u32[]{:S(2)}) %collective-permute-start.2) | collective-permute-done | bytes 69664 | tf_op jit(solution)/shard_map/ppermute | solution.py:495
  20.1 1.5 %collective-permute-done.3.m3 = f32[17,8,128]{2,1,0:T(8,128)S(1)} collective-permute-done((f32[17,8,128]{2,1,0:T(8,128)S(1)}, f32[17,8,128]{2,1,0:T(8,128)S(1)}, u32[]{:S(2)}, u32[]{:S(2)}) %collective-permute-start.3) | collective-permute-done | bytes 69664 | tf_op jit(solution)/shard_map/ppermute | solution.py:495
  21.7 1.3 %collective-permute-start.4 = (f32[17,8,128]{2,1,0:T(8,128)S(1)}, f32[17,8,128]{2,1,0:T(8,128)S(1)}, u32[]{:S(2)}, u32[]{:S(2)}) collective-permute-start(f32[17,8,128]{2,1,0:T(8,128)S(1)} %group.1.after.n0), channel_id=1, source_target_pairs={{0,8},{1,9},{2,10},{3,11},{4,12},{5,13},{6,14},{7,15},{8,0},{9,1},... | collective-permute-start | bytes 208904 | tf_op jit(solution)/shard_map/ppermute | solution.py:495
  23.0 2.5 %collective-permute-start.5 = (f32[17,8,128]{2,1,0:T(8,128)S(1)}, f32[17,8,128]{2,1,0:T(8,128)S(1)}, u32[]{:S(2)}, u32[]{:S(2)}) collective-permute-start(f32[17,8,128]{2,1,0:T(8,128)S(1)} %group.1.after.n0), channel_id=1, source_target_pairs={{0,16},{1,17},{2,18},{3,19},{4,20},{5,21},{6,22},{7,23},{8,24},{9,... | collective-permute-start | bytes 208904 | tf_op jit(solution)/shard_map/ppermute | solution.py:495
  25.7 2.4 %primal_products.1 = (f32[8,256,128]{2,1,0:T(8,128)S(1)}, f32[8,256,128]{2,1,0:T(8,128)S(1)}, f32[8,256,128]{2,1,0:T(8,128)S(1)}) custom-call(f32[8,256,128]{2,1,0:T(8,128)S(1)} %get-tuple-element.23.rx, f32[8,256,128]{2,1,0:T(8,128)S(1)} %get-tuple-element.24.ry, f32[3,8,256,128]{3,2,1,0:T(8,128)S(1)} %get-tuple-element.25.h, ...), custom_call_target="tpu_custom_call" | custom-call | flops 1000 | bytes 12000000 | tf_op jit(solution)/shard_map/primal_products/pallas_call | solution.py:559
  28.0 2.5 %collective-permute-done.6.n3 = f32[17,8,128]{2,1,0:T(8,128)S(1)} collective-permute-done((f32[17,8,128]{2,1,0:T(8,128)S(1)}, f32[17,8,128]{2,1,0:T(8,128)S(1)}, u32[]{:S(2)}, u32[]{:S(2)}) %collective-permute-start.6) | collective-permute-done | bytes 69664 | tf_op jit(solution)/shard_map/ppermute | solution.py:495
  30.8 2.8 %collective-permute-start.7 = (f32[12,8,128]{2,1,0:T(8,128)S(1)}, f32[12,8,128]{2,1,0:T(8,128)S(1)}, u32[]{:S(2)}, u32[]{:S(2)}) collective-permute-start(f32[12,8,128]{2,1,0:T(8,128)S(1)} %get-tuple-element.39), channel_id=1, source_target_pairs={{0,1},{1,0},{2,3},{3,2},{4,5},{5,4},{6,7},{7,6},{8,9},{9,8},{10,11... | collective-permute-start | bytes 147464 | tf_op jit(solution)/shard_map/ppermute | solution.py:495
  33.6 0.9 %collective-permute-done.7.recv.refs_6_ = f32[12,8,128]{2,1,0:T(8,128)S(1)} collective-permute-done((f32[12,8,128]{2,1,0:T(8,128)S(1)}, f32[12,8,128]{2,1,0:T(8,128)S(1)}, u32[]{:S(2)}, u32[]{:S(2)}) %collective-permute-start.7) | collective-permute-done | bytes 49184 | tf_op jit(solution)/shard_map/ppermute | solution.py:495
  34.9 3.0 %collective-permute-start.8 = (f32[2,256,128]{2,1,0:T(8,128)S(1)}, f32[2,256,128]{2,1,0:T(8,128)S(1)}, u32[]{:S(2)}, u32[]{:S(2)}) collective-permute-start(f32[2,256,128]{2,1,0:T(8,128)S(1)} %gradient_2.1), channel_id=1, source_target_pairs={{0,64},{32,96},{64,0},{96,32},{1,65},{33,97},{65,1},{97,33},{2,66}... | collective-permute-start | bytes 786440 | tf_op jit(solution)/shard_map/ppermute | solution.py:495
  39.3 0.5 collective-permute-start.10
  40.3 3.8 %collective-permute-done.8 = f32[2,256,128]{2,1,0:T(8,128)S(1)} collective-permute-done((f32[2,256,128]{2,1,0:T(8,128)S(1)}, f32[2,256,128]{2,1,0:T(8,128)S(1)}, u32[]{:S(2)}, u32[]{:S(2)}) %collective-permute-start.8) | collective-permute-done | bytes 262176 | tf_op jit(solution)/shard_map/ppermute | solution.py:495
  44.0 6.0 %collective-permute-done.9 = f32[2,256,128]{2,1,0:T(8,128)S(1)} collective-permute-done((f32[2,256,128]{2,1,0:T(8,128)S(1)}, f32[2,256,128]{2,1,0:T(8,128)S(1)}, u32[]{:S(2)}, u32[]{:S(2)}) %collective-permute-start.9) | collective-permute-done | bytes 262176 | tf_op jit(solution)/shard_map/ppermute | solution.py:495
  50.2 1.6 %collective-permute-start.11 = (f32[2,256,128]{2,1,0:T(8,128)S(1)}, f32[2,256,128]{2,1,0:T(8,128)S(1)}, u32[]{:S(2)}, u32[]{:S(2)}) collective-permute-start(f32[2,256,128]{2,1,0:T(8,128)S(1)} %add_add_fusion.g0), channel_id=1, source_target_pairs={{0,32},{32,0},{64,96},{96,64},{1,33},{33,1},{65,97},{97,65},{2,34}... | collective-permute-start | bytes 786440 | tf_op jit(solution)/shard_map/ppermute | solution.py:495
  51.8 2.6 %collective-permute-start.12 = (f32[2,256,128]{2,1,0:T(8,128)S(1)}, f32[2,256,128]{2,1,0:T(8,128)S(1)}, u32[]{:S(2)}, u32[]{:S(2)}) collective-permute-start(f32[2,256,128]{2,1,0:T(8,128)S(1)} %add_add_fusion.g0), channel_id=1, source_target_pairs={{0,64},{32,96},{64,0},{96,32},{1,65},{33,97},{65,1},{97,33},{2,66}... | collective-permute-start | bytes 786440 | tf_op jit(solution)/shard_map/ppermute | solution.py:495
  54.4 3.6 %outputs.1 = (f32[3,8,256,128]{3,2,1,0:T(8,128)}, f32[3,8,256,128]{3,2,1,0:T(8,128)}) custom-call(f32[8,256,128]{2,1,0:T(8,128)S(1)} %get-tuple-element.35.after.ex, f32[8,256,128]{2,1,0:T(8,128)S(1)} %get-tuple-element.36.ey, f32[3,8,256,128]{3,2,1,0:T(8,128)S(1)} %get-tuple-element.25.h, f32[8,256,128]{2,1,0:T(8,128)S(1)} %get-tuple-element.26.ez, ...), custom_call_target="tpu_custom_call" | custom-call | flops 1000 | bytes 18000000 | tf_op jit(solution)/shard_map/outputs/pallas_call | solution.py:576
  58.0 8.0 %collective-permute-done.12.g2 = f32[2,256,128]{2,1,0:T(8,128)S(1)} collective-permute-done((f32[2,256,128]{2,1,0:T(8,128)S(1)}, f32[2,256,128]{2,1,0:T(8,128)S(1)}, u32[]{:S(2)}, u32[]{:S(2)}) %collective-permute-start.12) | collective-permute-done | bytes 262176 | tf_op jit(solution)/shard_map/ppermute | solution.py:495
  66.0 2.0 %collective-permute-done.13.g3 = f32[2,256,128]{2,1,0:T(8,128)S(1)} collective-permute-done((f32[2,256,128]{2,1,0:T(8,128)S(1)}, f32[2,256,128]{2,1,0:T(8,128)S(1)}, u32[]{:S(2)}, u32[]{:S(2)}) %collective-permute-start.13) | collective-permute-done | bytes 262176 | tf_op jit(solution)/shard_map/ppermute | solution.py:495
  68.0 1.0 %place.1 = f32[8,256,128]{2,1,0:T(8,128)} custom-call(f32[2,256,128]{2,1,0:T(8,128)S(1)} %add_add_fusion.g0, f32[2,256,128]{2,1,0:T(8,128)S(1)} %collective-permute-done.11.g1, f32[2,256,128]{2,1,0:T(8,128)S(1)} %collective-permute-done.12.g2, f32[2,256,128]{2,1,0:T(8,128)S(1)} %collective-permute-done.13.g3), custom_call_target="tpu_custom_call" | custom-call | flops 1000 | bytes 3000000 | tf_op jit(solution)/shard_map/place/pallas_call | solution.py:584
  (17 shorter events, 3.0 us)
Async XLA Ops:
  9.4 2.4 %collective-permute-start = (f32[17,8,128]{2,1,0:T(8,128)S(1)}, f32[17,8,128]{2,1,0:T(8,128)S(1)}, u32[]{:S(2)}, u32[]{:S(2)}) collective-permute-start(f32[17,8,128]{2,1,0:T(8,128)S(1)} %get-tuple-element.34), channel_id=1, source_target_pairs={{0,1},{1,0},{2,3},{3,2},{4,5},{5,4},{6,7},{7,6},{8,9},{9,8},{10,11... | collective-permute-start | bytes 208904 | tf_op jit(solution)/shard_map/ppermute | solution.py:495
  11.9 6.9 %collective-permute-start.1 = (f32[17,8,128]{2,1,0:T(8,128)S(1)}, f32[17,8,128]{2,1,0:T(8,128)S(1)}, u32[]{:S(2)}, u32[]{:S(2)}) collective-permute-start(f32[17,8,128]{2,1,0:T(8,128)S(1)} %chip.1.after.m0), channel_id=1, source_target_pairs={{0,2},{1,3},{2,0},{3,1},{4,6},{5,7},{6,4},{7,5},{8,10},{9,11},{10,... | collective-permute-start | bytes 208904 | tf_op jit(solution)/shard_map/ppermute | solution.py:495
  13.7 6.4 %collective-permute-start.2 = (f32[17,8,128]{2,1,0:T(8,128)S(1)}, f32[17,8,128]{2,1,0:T(8,128)S(1)}, u32[]{:S(2)}, u32[]{:S(2)}) collective-permute-start(f32[17,8,128]{2,1,0:T(8,128)S(1)} %chip.1.after.m0), channel_id=1, source_target_pairs={{0,4},{1,5},{2,6},{3,7},{4,0},{5,1},{6,2},{7,3},{8,12},{9,13},{10,... | collective-permute-start | bytes 208904 | tf_op jit(solution)/shard_map/ppermute | solution.py:495
  17.0 4.7 %collective-permute-start.3 = (f32[17,8,128]{2,1,0:T(8,128)S(1)}, f32[17,8,128]{2,1,0:T(8,128)S(1)}, u32[]{:S(2)}, u32[]{:S(2)}) collective-permute-start(f32[17,8,128]{2,1,0:T(8,128)S(1)} %chip.1.after.m0), channel_id=1, source_target_pairs={{0,6},{1,7},{2,4},{3,5},{4,2},{5,3},{6,0},{7,1},{8,14},{9,15},{10,... | collective-permute-start | bytes 208904 | tf_op jit(solution)/shard_map/ppermute | solution.py:495
  21.7 6.3 %collective-permute-start.4 = (f32[17,8,128]{2,1,0:T(8,128)S(1)}, f32[17,8,128]{2,1,0:T(8,128)S(1)}, u32[]{:S(2)}, u32[]{:S(2)}) collective-permute-start(f32[17,8,128]{2,1,0:T(8,128)S(1)} %group.1.after.n0), channel_id=1, source_target_pairs={{0,8},{1,9},{2,10},{3,11},{4,12},{5,13},{6,14},{7,15},{8,0},{9,1},... | collective-permute-start | bytes 208904 | tf_op jit(solution)/shard_map/ppermute | solution.py:495
  23.0 5.0 %collective-permute-start.5 = (f32[17,8,128]{2,1,0:T(8,128)S(1)}, f32[17,8,128]{2,1,0:T(8,128)S(1)}, u32[]{:S(2)}, u32[]{:S(2)}) collective-permute-start(f32[17,8,128]{2,1,0:T(8,128)S(1)} %group.1.after.n0), channel_id=1, source_target_pairs={{0,16},{1,17},{2,18},{3,19},{4,20},{5,21},{6,22},{7,23},{8,24},{9,... | collective-permute-start | bytes 208904 | tf_op jit(solution)/shard_map/ppermute | solution.py:495
  25.5 5.1 %collective-permute-start.6 = (f32[17,8,128]{2,1,0:T(8,128)S(1)}, f32[17,8,128]{2,1,0:T(8,128)S(1)}, u32[]{:S(2)}, u32[]{:S(2)}) collective-permute-start(f32[17,8,128]{2,1,0:T(8,128)S(1)} %group.1.after.n0), channel_id=1, source_target_pairs={{0,24},{1,25},{2,26},{3,27},{4,28},{5,29},{6,30},{7,31},{8,16},{9,... | collective-permute-start | bytes 208904 | tf_op jit(solution)/shard_map/ppermute | solution.py:495
  30.8 3.7 %collective-permute-start.7 = (f32[12,8,128]{2,1,0:T(8,128)S(1)}, f32[12,8,128]{2,1,0:T(8,128)S(1)}, u32[]{:S(2)}, u32[]{:S(2)}) collective-permute-start(f32[12,8,128]{2,1,0:T(8,128)S(1)} %get-tuple-element.39), channel_id=1, source_target_pairs={{0,1},{1,0},{2,3},{3,2},{4,5},{5,4},{6,7},{7,6},{8,9},{9,8},{10,11... | collective-permute-start | bytes 147464 | tf_op jit(solution)/shard_map/ppermute | solution.py:495
  34.9 9.1 %collective-permute-start.8 = (f32[2,256,128]{2,1,0:T(8,128)S(1)}, f32[2,256,128]{2,1,0:T(8,128)S(1)}, u32[]{:S(2)}, u32[]{:S(2)}) collective-permute-start(f32[2,256,128]{2,1,0:T(8,128)S(1)} %gradient_2.1), channel_id=1, source_target_pairs={{0,64},{32,96},{64,0},{96,32},{1,65},{33,97},{65,1},{97,33},{2,66}... | collective-permute-start | bytes 786440 | tf_op jit(solution)/shard_map/ppermute | solution.py:495
  38.4 11.7 %collective-permute-start.9 = (f32[2,256,128]{2,1,0:T(8,128)S(1)}, f32[2,256,128]{2,1,0:T(8,128)S(1)}, u32[]{:S(2)}, u32[]{:S(2)}) collective-permute-start(f32[2,256,128]{2,1,0:T(8,128)S(1)} %gradient_1.1), channel_id=1, source_target_pairs={{0,32},{32,0},{64,96},{96,64},{1,33},{33,1},{65,97},{97,65},{2,34}... | collective-permute-start | bytes 786440 | tf_op jit(solution)/shard_map/ppermute | solution.py:495
  39.3 10.8 %collective-permute-start.10 = (f32[2,256,128]{2,1,0:T(8,128)S(1)}, f32[2,256,128]{2,1,0:T(8,128)S(1)}, u32[]{:S(2)}, u32[]{:S(2)}) collective-permute-start(f32[2,256,128]{2,1,0:T(8,128)S(1)} %gradient_3.1), channel_id=1, source_target_pairs={{0,96},{32,64},{64,32},{96,0},{1,97},{33,65},{65,33},{97,1},{2,98}... | collective-permute-start | bytes 786440 | tf_op jit(solution)/shard_map/ppermute | solution.py:495
  50.2 7.8 %collective-permute-start.11 = (f32[2,256,128]{2,1,0:T(8,128)S(1)}, f32[2,256,128]{2,1,0:T(8,128)S(1)}, u32[]{:S(2)}, u32[]{:S(2)}) collective-permute-start(f32[2,256,128]{2,1,0:T(8,128)S(1)} %add_add_fusion.g0), channel_id=1, source_target_pairs={{0,32},{32,0},{64,96},{96,64},{1,33},{33,1},{65,97},{97,65},{2,34}... | collective-permute-start | bytes 786440 | tf_op jit(solution)/shard_map/ppermute | solution.py:495
  51.8 14.2 %collective-permute-start.12 = (f32[2,256,128]{2,1,0:T(8,128)S(1)}, f32[2,256,128]{2,1,0:T(8,128)S(1)}, u32[]{:S(2)}, u32[]{:S(2)}) collective-permute-start(f32[2,256,128]{2,1,0:T(8,128)S(1)} %add_add_fusion.g0), channel_id=1, source_target_pairs={{0,64},{32,96},{64,0},{96,32},{1,65},{33,97},{65,1},{97,33},{2,66}... | collective-permute-start | bytes 786440 | tf_op jit(solution)/shard_map/ppermute | solution.py:495
  54.4 13.6 %collective-permute-start.13 = (f32[2,256,128]{2,1,0:T(8,128)S(1)}, f32[2,256,128]{2,1,0:T(8,128)S(1)}, u32[]{:S(2)}, u32[]{:S(2)}) collective-permute-start(f32[2,256,128]{2,1,0:T(8,128)S(1)} %add_add_fusion.g0), channel_id=1, source_target_pairs={{0,96},{32,64},{64,32},{96,0},{1,97},{33,65},{65,33},{97,1},{2,98}... | collective-permute-start | bytes 786440 | tf_op jit(solution)/shard_map/ppermute | solution.py:495

commit v4 on v3

--- a/solution.py
+++ b/solution.py
@@ -22,6 +22,11 @@
     return one, two, three
 
 
+def in_two(v):
+    one = v.astype(BF)
+    return jnp.concatenate([one, (v - one.astype(F32)).astype(BF)], 1)
+
+
 def mm(a, b, dims=NN):
     return lax.dot_general(a, b, dims, preferred_element_type=F32)
 
@@ -67,7 +72,7 @@
 
 def rhs_kernel(
     angle, eps, e, h, ge, gh, lab, prof_in, zs_in, lt_in, w_in,
-    rx_o, ry_o, ax_o, ay_o, psx_o, psy_o, gs_o, inv_o, ez_o, h_o, w, keep_o, send_o,
+    rx_o, ry_o, ax_o, ay_o, psx_o, psy_o, gs_o, inv_o, h_o, w, keep_o, send_o,
     e_s, ge_s, gh_s, lab_s, sems, prof_s, prof, zs, lt,
 ):
     core = lax.rem(lax.axis_index("gz"), 2)
@@ -99,8 +104,6 @@
                 fetch(which, x + 1).start()
         for which in late:
             fetch(which, x).start()
-    ez_copy = pltpu.make_async_copy(e.at[2], ez_o, sems.at[5, 0])
-    ez_copy.start()
 
     for copy in tables:
         copy.wait()
@@ -171,40 +174,24 @@
             psx_o[x] = -inv * (inv * p_x)
             psy_o[x] = -inv * (inv * p_y)
             gs_o[x] = -inv * sg
-            thirds = []
             for c, field in enumerate((r_x, r_y, a_x, a_y)):
-                one, two, three = split(field)
                 mask = slot == 4 * j + c
-                w1, w2, w3 = (jnp.where(mask, part, 0.0) for part in ends_parts)
-                lhs = jnp.concatenate(
-                    [
-                        jnp.concatenate([w1, w1], 1),
-                        jnp.concatenate([w2, w2], 1),
-                        jnp.concatenate([w3, jnp.zeros_like(w3)], 1),
-                    ],
-                    0,
-                ).astype(BF)
-                out = mm(lhs, jnp.concatenate([one, two], 1), NT)
+                lhs = jnp.concatenate([jnp.where(mask, part, 0.0) for part in ends_parts], 0)
+                lhs = jnp.concatenate([lhs, lhs], 1).astype(BF)
+                out = mm(lhs, in_two(field), NT)
                 acc_ends += out[0:16] + out[16:32] + out[32:48]
-                thirds.append((w1, three))
-            for c in (0, 2):
-                (wa, ta), (wb, tb) = thirds[c], thirds[c + 1]
-                lhs = jnp.concatenate([wa, wb], 1).astype(BF)
-                acc_ends += mm(lhs, jnp.concatenate([ta, tb], 1), NT)
 
             packed = jnp.where(lane == CZ - 1, h_y, inv)
             packed = jnp.where(lane == CZ - 2, -pltpu.roll(h_x, CZ - 1, 1), packed)
             packed = jnp.where(lane == CZ - 3, pltpu.roll(bar_hy, CZ - 2, 1), packed)
             packed = jnp.where(lane == CZ - 4, pltpu.roll(bar_hx, CZ - 3, 1), packed)
-            one, two, three = split(packed)
             c16 = slot - 4 * j
             own = (c16 >= 0) & (c16 < 4)
             pick = jnp.where(
                 own & (row16 < 8) & (lane16 == CZ - 1 - c16), 1.0,
                 jnp.where(own & (row16 >= 8) & (c16 < 2) & (lane16 == 0), 1.0, 0.0),
             )
-            acc_tops += mm(jnp.concatenate([pick, pick], 1).astype(BF), jnp.concatenate([one, two], 1), NT)
-            acc_tops += mm(pick.astype(BF), three, NT)
+            acc_tops += mm(jnp.concatenate([pick, pick], 1).astype(BF), in_two(packed), NT)
 
         acc_tops = jnp.where((row_y >= 8) & (lax.rem(row_y, 4) >= 2), 1.0, acc_tops)
         for base, acc in ((0, acc_ends), (8, acc_tops)):
@@ -217,7 +204,6 @@
         return carry
 
     lax.fori_loop(0, X // 2, one_pair, 0)
-    ez_copy.wait()
 
 
 def unpack(ref):
@@ -341,7 +327,9 @@
     return wide[:, :CZ] + wide[:, CZ:] + narrow
 
 
-def adjoint_kernel(ax, ay, psx, psy, w, after, out):
+def adjoint_kernel(ax, ay, psx, psy, w, e, after, out, ez_o, sem):
+    ez_copy = pltpu.make_async_copy(e.at[2], ez_o, sem)
+    ez_copy.start()
     tables = product_tables(w[...])
 
     def one(x, carry):
@@ -349,6 +337,7 @@
         return carry
 
     lax.fori_loop(0, X, one, 0, unroll=2)
+    ez_copy.wait()
 
 
 def primal_kernel(rx, ry, h, ez, gs, part, w, after, ex_o, ey_o, grad_o):
@@ -480,10 +469,10 @@
             copy.wait()
 
 
-def place_kernel(g0, g1, g2, g3, out, sems):
+def place_kernel(g2, g1, g3, g0, out, sems):
     src = lax.axis_index("src")
     copies = []
-    for k, g in enumerate((g0, g1, g2, g3)):
+    for k, g in zip((2, 1, 3, 0), (g2, g1, g3, g0)):
         copies.append(pltpu.make_async_copy(g, out.at[pl.ds(2 * (src ^ k), 2)], sems.at[k]))
     for copy in copies:
         copy.start()
@@ -534,10 +523,10 @@
     def space(*dims, dtype=F32):
         return pltpu.VMEM(dims, dtype)
 
-    rx, ry, ax, ay, psx, psy, gs, inv, ez, hv, w, keep, send = call(
+    rx, ry, ax, ay, psx, psy, gs, inv, hv, w, keep, send = call(
         rhs_kernel, "right_hand_sides",
         [SMEM, SMEM] + [HBM] * 9,
-        [slab] * 9 + [shape(3, X, Y, CZ), shape(CZ, CZ)] + [message] * 2,
+        [slab] * 8 + [shape(3, X, Y, CZ), shape(CZ, CZ)] + [message] * 2,
         6, 24,
         scratch=[
             space(2, X, Y, CZ), space(3, X, Y, CZ), space(3, X, Y, CZ),
@@ -550,9 +539,10 @@
     (m0,) = call(chip_kernel, "chip", [VMEM] * 2, [message], 0.5, 4)(keep, other)
     m1, m2, m3 = (swap(m0, "gz", 2 * k) for k in (1, 2, 3))
 
-    (adjoint,) = call(adjoint_kernel, "adjoint_products", [VMEM] * 5 + [ANY], [slab], 3, 8)(
-        ax, ay, psx, psy, w, m0
-    )
+    adjoint, ez = call(
+        adjoint_kernel, "adjoint_products", [VMEM] * 5 + [HBM, ANY], [slab] * 2, 3, 8,
+        scratch=[pltpu.SemaphoreType.DMA],
+    )(ax, ay, psx, psy, w, in_hbm(e), m0)
     (n0,) = call(group_kernel, "group", [VMEM] * 4 + [ANY], [message], 0.5, 4)(m0, m1, m2, m3, adjoint)
     n1, n2, n3 = (swap(n0, "gz", 8 * k) for k in (1, 2, 3))
 
@@ -584,7 +574,7 @@
     (eps_grad,) = call(
         place_kernel, "place", [ANY] * 4, [slab], 1, 4, out_specs=[HBM],
         scratch=[pltpu.SemaphoreType.DMA((4,))],
-    )(total, one, two, three)
+    )(two, one, three, total)
     return (e_new[None], h_new[None], eps_grad)
 
 

time: 69.7 us -> 66 us (0.947)
  waiting for transfers between devices: 27 us -> 25 us
  Pallas kernels: 19 us -> 18 us
    ppermute x14, waiting for transfers between devices: 27 us -> 25 us  [swap(): lax.ppermute(block, axis, [(i, i ^ mask) for i in range(lax.axis_size(axi...]
    pallas_call x2, Pallas kernels: 9.96 us -> 9.13 us  [the longest x1 7.28 us: body(): call(rhs_kernel, 'right_hand_sides', [SMEM, SMEM] + [HBM] * 9, [slab] * 8...]
  transfers between devices with their start and end apart: 14 -> 14, of which waited for: 10 -> 11; matrix products, arithmetic and copies ran while one was open for 0% -> 0% of each run, Pallas kernels for 13% -> 14%
where the time goes in v4:
time: 66 us; the launch traced here: 65.8 us
  waiting for transfers between devices  25 us (38%)
  starting transfers between devices  21.3 us (32%)
  Pallas kernels  18 us (27%)
  between operations  1.39 us (2%)
    ppermute x14, waiting for transfers between devices, swap(): lax.ppermute(block, axis, [(i, i ^ mask) for i in range(lax.axis_size(axi...  25 us
    ppermute x14, starting transfers between devices, swap(): lax.ppermute(block, axis, [(i, i ^ mask) for i in range(lax.axis_size(axi...  21.3 us
    pallas_call x1, Pallas kernels, body(): call(rhs_kernel, 'right_hand_sides', [SMEM, SMEM] + [HBM] * 9, [slab] * 8...  7.28 us
    pallas_call x1, Pallas kernels, body(): call(output_kernel, 'outputs', [VMEM] * 8, [shape(3, X, Y, CZ)] * 2, 6, 1...  3.48 us
    pallas_call x1, Pallas kernels, body(): call(primal_kernel, 'primal_products', [VMEM] * 7 + [ANY], [slab] * 3, 4, 8)  2.33 us
    pallas_call x1, Pallas kernels, body(): call(adjoint_kernel, 'adjoint_products', [VMEM] * 5 + [HBM, ANY], [slab]...  1.84 us
    pallas_call x4, Pallas kernels, gradient(): call(lambda *refs: gradient_kernel(k, *refs), f'gradient_{k}', [VMEM] * 8...  1.84 us
  transfers between devices with their start and end apart: 14, of which 11 were waited for; matrix products, arithmetic and copies ran while one was open for 0% of the time, Pallas kernels for 14%

profile of v4, /device:TPU:1, one launch (start us, length us, event | category | flops | bytes accessed | tf_op | source)
XLA Modules:
  0.0 65.8 jit_solution(16117937916083764531)
XLA Ops:
  1.3 7.3 %right_hand_sides.1 = (f32[8,256,128]{2,1,0:T(8,128)S(1)}, f32[8,256,128]{2,1,0:T(8,128)S(1)}, f32[8,256,128]{2,1,0:T(8,128)S(1)}, f32[8,256,128]{2,1,0:T(8,128)...) custom-call(s32[1]{0:T(128)S(6)} %copy.14.angle, ...), custom_call_target="tpu_custom_call" | custom-call | flops 1000 | bytes 18000000 | tf_op jit(solution)/shard_map/right_hand_sides/pallas_call | solution.py:526
  8.6 1.5 %collective-permute-start = (f32[17,8,128]{2,1,0:T(8,128)S(1)}, f32[17,8,128]{2,1,0:T(8,128)S(1)}, u32[]{:S(2)}, u32[]{:S(2)}) collective-permute-start(f32[17,8,128]{2,1,0:T(8,128)S(1)} %get-tuple-element.33), channel_id=1, source_target_pairs={{0,1},{1,0},{2,3},{3,2},{4,5},{5,4},{6,7},{7,6},{8,9},{9,8},{10,11... | collective-permute-start | bytes 208904 | tf_op jit(solution)/shard_map/ppermute | solution.py:484
  10.1 0.9 %collective-permute-done.other.a1 = f32[17,8,128]{2,1,0:T(8,128)S(1)} collective-permute-done((f32[17,8,128]{2,1,0:T(8,128)S(1)}, f32[17,8,128]{2,1,0:T(8,128)S(1)}, u32[]{:S(2)}, u32[]{:S(2)}) %collective-permute-start) | collective-permute-done | bytes 69664 | tf_op jit(solution)/shard_map/ppermute | solution.py:484
  11.0 1.8 %collective-permute-start.1 = (f32[17,8,128]{2,1,0:T(8,128)S(1)}, f32[17,8,128]{2,1,0:T(8,128)S(1)}, u32[]{:S(2)}, u32[]{:S(2)}) collective-permute-start(f32[17,8,128]{2,1,0:T(8,128)S(1)} %chip.1.after.m0), channel_id=1, source_target_pairs={{0,2},{1,3},{2,0},{3,1},{4,6},{5,7},{6,4},{7,5},{8,10},{9,11},{10,... | collective-permute-start | bytes 208904 | tf_op jit(solution)/shard_map/ppermute | solution.py:484
  12.8 3.3 %collective-permute-start.2 = (f32[17,8,128]{2,1,0:T(8,128)S(1)}, f32[17,8,128]{2,1,0:T(8,128)S(1)}, u32[]{:S(2)}, u32[]{:S(2)}) collective-permute-start(f32[17,8,128]{2,1,0:T(8,128)S(1)} %chip.1.after.m0), channel_id=1, source_target_pairs={{0,4},{1,5},{2,6},{3,7},{4,0},{5,1},{6,2},{7,3},{8,12},{9,13},{10,... | collective-permute-start | bytes 208904 | tf_op jit(solution)/shard_map/ppermute | solution.py:484
  16.1 1.8 %adjoint_products.1 = (f32[8,256,128]{2,1,0:T(8,128)S(1)}, f32[8,256,128]{2,1,0:T(8,128)S(1)}) custom-call(f32[8,256,128]{2,1,0:T(8,128)S(1)} %get-tuple-element.27.ax, f32[8,256,128]{2,1,0:T(8,128)S(1)} %get-tuple-element.28.ay, f32[8,256,128]{2,1,0:T(8,128)S(1)} %get-tuple-element.29.psx.refs_1_, f32[8,256,128]{2,1,0:T(8,128)S(1)} %get-tuple-element.30.psy.refs_2_, ...), custom_call_target="tpu_custom_call" | custom-call | flops 1000 | bytes 9000000 | tf_op jit(solution)/shard_map/adjoint_products/pallas_call | solution.py:542
  18.0 1.3 %collective-permute-done.2.m2 = f32[17,8,128]{2,1,0:T(8,128)S(1)} collective-permute-done((f32[17,8,128]{2,1,0:T(8,128)S(1)}, f32[17,8,128]{2,1,0:T(8,128)S(1)}, u32[]{:S(2)}, u32[]{:S(2)}) %collective-permute-start.2) | collective-permute-done | bytes 69664 | tf_op jit(solution)/shard_map/ppermute | solution.py:484
  19.3 1.5 %collective-permute-done.3.m3 = f32[17,8,128]{2,1,0:T(8,128)S(1)} collective-permute-done((f32[17,8,128]{2,1,0:T(8,128)S(1)}, f32[17,8,128]{2,1,0:T(8,128)S(1)}, u32[]{:S(2)}, u32[]{:S(2)}) %collective-permute-start.3) | collective-permute-done | bytes 69664 | tf_op jit(solution)/shard_map/ppermute | solution.py:484
  20.9 1.3 %collective-permute-start.4 = (f32[17,8,128]{2,1,0:T(8,128)S(1)}, f32[17,8,128]{2,1,0:T(8,128)S(1)}, u32[]{:S(2)}, u32[]{:S(2)}) collective-permute-start(f32[17,8,128]{2,1,0:T(8,128)S(1)} %group.1.after.n0), channel_id=1, source_target_pairs={{0,8},{1,9},{2,10},{3,11},{4,12},{5,13},{6,14},{7,15},{8,0},{9,1},... | collective-permute-start | bytes 208904 | tf_op jit(solution)/shard_map/ppermute | solution.py:484
  22.2 2.5 %collective-permute-start.5 = (f32[17,8,128]{2,1,0:T(8,128)S(1)}, f32[17,8,128]{2,1,0:T(8,128)S(1)}, u32[]{:S(2)}, u32[]{:S(2)}) collective-permute-start(f32[17,8,128]{2,1,0:T(8,128)S(1)} %group.1.after.n0), channel_id=1, source_target_pairs={{0,16},{1,17},{2,18},{3,19},{4,20},{5,21},{6,22},{7,23},{8,24},{9,... | collective-permute-start | bytes 208904 | tf_op jit(solution)/shard_map/ppermute | solution.py:484
  24.8 2.3 %primal_products.1 = (f32[8,256,128]{2,1,0:T(8,128)S(1)}, f32[8,256,128]{2,1,0:T(8,128)S(1)}, f32[8,256,128]{2,1,0:T(8,128)S(1)}) custom-call(f32[8,256,128]{2,1,0:T(8,128)S(1)} %get-tuple-element.24.rx, f32[8,256,128]{2,1,0:T(8,128)S(1)} %get-tuple-element.25.ry, f32[3,8,256,128]{3,2,1,0:T(8,128)S(1)} %get-tuple-element.26.h, ...), custom_call_target="tpu_custom_call" | custom-call | flops 1000 | bytes 12000000 | tf_op jit(solution)/shard_map/primal_products/pallas_call | solution.py:549
  27.2 2.6 %collective-permute-done.6.n3 = f32[17,8,128]{2,1,0:T(8,128)S(1)} collective-permute-done((f32[17,8,128]{2,1,0:T(8,128)S(1)}, f32[17,8,128]{2,1,0:T(8,128)S(1)}, u32[]{:S(2)}, u32[]{:S(2)}) %collective-permute-start.6) | collective-permute-done | bytes 69664 | tf_op jit(solution)/shard_map/ppermute | solution.py:484
  29.9 2.8 %collective-permute-start.7 = (f32[12,8,128]{2,1,0:T(8,128)S(1)}, f32[12,8,128]{2,1,0:T(8,128)S(1)}, u32[]{:S(2)}, u32[]{:S(2)}) collective-permute-start(f32[12,8,128]{2,1,0:T(8,128)S(1)} %get-tuple-element.41), channel_id=1, source_target_pairs={{0,1},{1,0},{2,3},{3,2},{4,5},{5,4},{6,7},{7,6},{8,9},{9,8},{10,11... | collective-permute-start | bytes 147464 | tf_op jit(solution)/shard_map/ppermute | solution.py:484
  32.7 0.9 %collective-permute-done.7.recv.refs_6_ = f32[12,8,128]{2,1,0:T(8,128)S(1)} collective-permute-done((f32[12,8,128]{2,1,0:T(8,128)S(1)}, f32[12,8,128]{2,1,0:T(8,128)S(1)}, u32[]{:S(2)}, u32[]{:S(2)}) %collective-permute-start.7) | collective-permute-done | bytes 49184 | tf_op jit(solution)/shard_map/ppermute | solution.py:484
  34.1 3.0 %collective-permute-start.8 = (f32[2,256,128]{2,1,0:T(8,128)S(1)}, f32[2,256,128]{2,1,0:T(8,128)S(1)}, u32[]{:S(2)}, u32[]{:S(2)}) collective-permute-start(f32[2,256,128]{2,1,0:T(8,128)S(1)} %gradient_2.1), channel_id=1, source_target_pairs={{0,64},{32,96},{64,0},{96,32},{1,65},{33,97},{65,1},{97,33},{2,66}... | collective-permute-start | bytes 786440 | tf_op jit(solution)/shard_map/ppermute | solution.py:484
  37.5 0.5 collective-permute-start.9
  38.5 0.5 collective-permute-start.10
  39.4 3.8 %collective-permute-done.8 = f32[2,256,128]{2,1,0:T(8,128)S(1)} collective-permute-done((f32[2,256,128]{2,1,0:T(8,128)S(1)}, f32[2,256,128]{2,1,0:T(8,128)S(1)}, u32[]{:S(2)}, u32[]{:S(2)}) %collective-permute-start.8) | collective-permute-done | bytes 262176 | tf_op jit(solution)/shard_map/ppermute | solution.py:484
  43.2 6.0 %collective-permute-done.9 = f32[2,256,128]{2,1,0:T(8,128)S(1)} collective-permute-done((f32[2,256,128]{2,1,0:T(8,128)S(1)}, f32[2,256,128]{2,1,0:T(8,128)S(1)}, u32[]{:S(2)}, u32[]{:S(2)}) %collective-permute-start.9) | collective-permute-done | bytes 262176 | tf_op jit(solution)/shard_map/ppermute | solution.py:484
  49.3 3.2 %collective-permute-start.11 = (f32[2,256,128]{2,1,0:T(8,128)S(1)}, f32[2,256,128]{2,1,0:T(8,128)S(1)}, u32[]{:S(2)}, u32[]{:S(2)}) collective-permute-start(f32[2,256,128]{2,1,0:T(8,128)S(1)} %add_add_fusion.g0), channel_id=1, source_target_pairs={{0,64},{32,96},{64,0},{96,32},{1,65},{33,97},{65,1},{97,33},{2,66}... | collective-permute-start | bytes 786440 | tf_op jit(solution)/shard_map/ppermute | solution.py:484
  53.3 3.5 %outputs.1 = (f32[3,8,256,128]{3,2,1,0:T(8,128)}, f32[3,8,256,128]{3,2,1,0:T(8,128)}) custom-call(f32[8,256,128]{2,1,0:T(8,128)S(1)} %get-tuple-element.37.after.ex, f32[8,256,128]{2,1,0:T(8,128)S(1)} %get-tuple-element.38.ey, f32[3,8,256,128]{3,2,1,0:T(8,128)S(1)} %get-tuple-element.26.h, f32[8,256,128]{2,1,0:T(8,128)S(1)} %get-tuple-element.34.ez, ...), custom_call_target="tpu_custom_call" | custom-call | flops 1000 | bytes 18000000 | tf_op jit(solution)/shard_map/outputs/pallas_call | solution.py:566
  56.8 1.2 %collective-permute-done.11.g2 = f32[2,256,128]{2,1,0:T(8,128)S(1)} collective-permute-done((f32[2,256,128]{2,1,0:T(8,128)S(1)}, f32[2,256,128]{2,1,0:T(8,128)S(1)}, u32[]{:S(2)}, u32[]{:S(2)}) %collective-permute-start.11) | collective-permute-done | bytes 262176 | tf_op jit(solution)/shard_map/ppermute | solution.py:484
  58.0 6.6 %collective-permute-done.12.g1 = f32[2,256,128]{2,1,0:T(8,128)S(1)} collective-permute-done((f32[2,256,128]{2,1,0:T(8,128)S(1)}, f32[2,256,128]{2,1,0:T(8,128)S(1)}, u32[]{:S(2)}, u32[]{:S(2)}) %collective-permute-start.12) | collective-permute-done | bytes 262176 | tf_op jit(solution)/shard_map/ppermute | solution.py:484
  64.8 1.0 %place.1 = f32[8,256,128]{2,1,0:T(8,128)} custom-call(f32[2,256,128]{2,1,0:T(8,128)S(1)} %collective-permute-done.11.g2, f32[2,256,128]{2,1,0:T(8,128)S(1)} %collective-permute-done.12.g1, f32[2,256,128]{2,1,0:T(8,128)S(1)} %collective-permute-done.13.g3, f32[2,256,128]{2,1,0:T(8,128)S(1)} %add_add_fusion.g0), custom_call_target="tpu_custom_call" | custom-call | flops 1000 | bytes 3000000 | tf_op jit(solution)/shard_map/place/pallas_call | solution.py:574
  (17 shorter events, 3.6 us)
Async XLA Ops:
  8.6 2.4 %collective-permute-start = (f32[17,8,128]{2,1,0:T(8,128)S(1)}, f32[17,8,128]{2,1,0:T(8,128)S(1)}, u32[]{:S(2)}, u32[]{:S(2)}) collective-permute-start(f32[17,8,128]{2,1,0:T(8,128)S(1)} %get-tuple-element.33), channel_id=1, source_target_pairs={{0,1},{1,0},{2,3},{3,2},{4,5},{5,4},{6,7},{7,6},{8,9},{9,8},{10,11... | collective-permute-start | bytes 208904 | tf_op jit(solution)/shard_map/ppermute | solution.py:484
  11.0 7.0 %collective-permute-start.1 = (f32[17,8,128]{2,1,0:T(8,128)S(1)}, f32[17,8,128]{2,1,0:T(8,128)S(1)}, u32[]{:S(2)}, u32[]{:S(2)}) collective-permute-start(f32[17,8,128]{2,1,0:T(8,128)S(1)} %chip.1.after.m0), channel_id=1, source_target_pairs={{0,2},{1,3},{2,0},{3,1},{4,6},{5,7},{6,4},{7,5},{8,10},{9,11},{10,... | collective-permute-start | bytes 208904 | tf_op jit(solution)/shard_map/ppermute | solution.py:484
  12.8 6.4 %collective-permute-start.2 = (f32[17,8,128]{2,1,0:T(8,128)S(1)}, f32[17,8,128]{2,1,0:T(8,128)S(1)}, u32[]{:S(2)}, u32[]{:S(2)}) collective-permute-start(f32[17,8,128]{2,1,0:T(8,128)S(1)} %chip.1.after.m0), channel_id=1, source_target_pairs={{0,4},{1,5},{2,6},{3,7},{4,0},{5,1},{6,2},{7,3},{8,12},{9,13},{10,... | collective-permute-start | bytes 208904 | tf_op jit(solution)/shard_map/ppermute | solution.py:484
  16.1 4.7 %collective-permute-start.3 = (f32[17,8,128]{2,1,0:T(8,128)S(1)}, f32[17,8,128]{2,1,0:T(8,128)S(1)}, u32[]{:S(2)}, u32[]{:S(2)}) collective-permute-start(f32[17,8,128]{2,1,0:T(8,128)S(1)} %chip.1.after.m0), channel_id=1, source_target_pairs={{0,6},{1,7},{2,4},{3,5},{4,2},{5,3},{6,0},{7,1},{8,14},{9,15},{10,... | collective-permute-start | bytes 208904 | tf_op jit(solution)/shard_map/ppermute | solution.py:484
  20.9 6.3 %collective-permute-start.4 = (f32[17,8,128]{2,1,0:T(8,128)S(1)}, f32[17,8,128]{2,1,0:T(8,128)S(1)}, u32[]{:S(2)}, u32[]{:S(2)}) collective-permute-start(f32[17,8,128]{2,1,0:T(8,128)S(1)} %group.1.after.n0), channel_id=1, source_target_pairs={{0,8},{1,9},{2,10},{3,11},{4,12},{5,13},{6,14},{7,15},{8,0},{9,1},... | collective-permute-start | bytes 208904 | tf_op jit(solution)/shard_map/ppermute | solution.py:484
  22.2 5.0 %collective-permute-start.5 = (f32[17,8,128]{2,1,0:T(8,128)S(1)}, f32[17,8,128]{2,1,0:T(8,128)S(1)}, u32[]{:S(2)}, u32[]{:S(2)}) collective-permute-start(f32[17,8,128]{2,1,0:T(8,128)S(1)} %group.1.after.n0), channel_id=1, source_target_pairs={{0,16},{1,17},{2,18},{3,19},{4,20},{5,21},{6,22},{7,23},{8,24},{9,... | collective-permute-start | bytes 208904 | tf_op jit(solution)/shard_map/ppermute | solution.py:484
  24.6 5.1 %collective-permute-start.6 = (f32[17,8,128]{2,1,0:T(8,128)S(1)}, f32[17,8,128]{2,1,0:T(8,128)S(1)}, u32[]{:S(2)}, u32[]{:S(2)}) collective-permute-start(f32[17,8,128]{2,1,0:T(8,128)S(1)} %group.1.after.n0), channel_id=1, source_target_pairs={{0,24},{1,25},{2,26},{3,27},{4,28},{5,29},{6,30},{7,31},{8,16},{9,... | collective-permute-start | bytes 208904 | tf_op jit(solution)/shard_map/ppermute | solution.py:484
  29.9 3.7 %collective-permute-start.7 = (f32[12,8,128]{2,1,0:T(8,128)S(1)}, f32[12,8,128]{2,1,0:T(8,128)S(1)}, u32[]{:S(2)}, u32[]{:S(2)}) collective-permute-start(f32[12,8,128]{2,1,0:T(8,128)S(1)} %get-tuple-element.41), channel_id=1, source_target_pairs={{0,1},{1,0},{2,3},{3,2},{4,5},{5,4},{6,7},{7,6},{8,9},{9,8},{10,11... | collective-permute-start | bytes 147464 | tf_op jit(solution)/shard_map/ppermute | solution.py:484
  34.1 9.1 %collective-permute-start.8 = (f32[2,256,128]{2,1,0:T(8,128)S(1)}, f32[2,256,128]{2,1,0:T(8,128)S(1)}, u32[]{:S(2)}, u32[]{:S(2)}) collective-permute-start(f32[2,256,128]{2,1,0:T(8,128)S(1)} %gradient_2.1), channel_id=1, source_target_pairs={{0,64},{32,96},{64,0},{96,32},{1,65},{33,97},{65,1},{97,33},{2,66}... | collective-permute-start | bytes 786440 | tf_op jit(solution)/shard_map/ppermute | solution.py:484
  37.5 11.7 %collective-permute-start.9 = (f32[2,256,128]{2,1,0:T(8,128)S(1)}, f32[2,256,128]{2,1,0:T(8,128)S(1)}, u32[]{:S(2)}, u32[]{:S(2)}) collective-permute-start(f32[2,256,128]{2,1,0:T(8,128)S(1)} %gradient_1.1), channel_id=1, source_target_pairs={{0,32},{32,0},{64,96},{96,64},{1,33},{33,1},{65,97},{97,65},{2,34}... | collective-permute-start | bytes 786440 | tf_op jit(solution)/shard_map/ppermute | solution.py:484
  38.5 10.8 %collective-permute-start.10 = (f32[2,256,128]{2,1,0:T(8,128)S(1)}, f32[2,256,128]{2,1,0:T(8,128)S(1)}, u32[]{:S(2)}, u32[]{:S(2)}) collective-permute-start(f32[2,256,128]{2,1,0:T(8,128)S(1)} %gradient_3.1), channel_id=1, source_target_pairs={{0,96},{32,64},{64,32},{96,0},{1,97},{33,65},{65,33},{97,1},{2,98}... | collective-permute-start | bytes 786440 | tf_op jit(solution)/shard_map/ppermute | solution.py:484
  49.3 8.6 %collective-permute-start.11 = (f32[2,256,128]{2,1,0:T(8,128)S(1)}, f32[2,256,128]{2,1,0:T(8,128)S(1)}, u32[]{:S(2)}, u32[]{:S(2)}) collective-permute-start(f32[2,256,128]{2,1,0:T(8,128)S(1)} %add_add_fusion.g0), channel_id=1, source_target_pairs={{0,64},{32,96},{64,0},{96,32},{1,65},{33,97},{65,1},{97,33},{2,66}... | collective-permute-start | bytes 786440 | tf_op jit(solution)/shard_map/ppermute | solution.py:484
  52.6 12.0 %collective-permute-start.12 = (f32[2,256,128]{2,1,0:T(8,128)S(1)}, f32[2,256,128]{2,1,0:T(8,128)S(1)}, u32[]{:S(2)}, u32[]{:S(2)}) collective-permute-start(f32[2,256,128]{2,1,0:T(8,128)S(1)} %add_add_fusion.g0), channel_id=1, source_target_pairs={{0,32},{32,0},{64,96},{96,64},{1,33},{33,1},{65,97},{97,65},{2,34}... | collective-permute-start | bytes 786440 | tf_op jit(solution)/shard_map/ppermute | solution.py:484
  53.0 11.9 %collective-permute-start.13 = (f32[2,256,128]{2,1,0:T(8,128)S(1)}, f32[2,256,128]{2,1,0:T(8,128)S(1)}, u32[]{:S(2)}, u32[]{:S(2)}) collective-permute-start(f32[2,256,128]{2,1,0:T(8,128)S(1)} %add_add_fusion.g0), channel_id=1, source_target_pairs={{0,96},{32,64},{64,32},{96,0},{1,97},{33,65},{65,33},{97,1},{2,98}... | collective-permute-start | bytes 786440 | tf_op jit(solution)/shard_map/ppermute | solution.py:484

commit v5 on v4

--- a/solution.py
+++ b/solution.py
@@ -10,7 +10,8 @@
 X, Y, CZ = 8, 256, 128
 NN = (((1,), (0,)), ((), ()))
 NT = (((1,), (1,)), ((), ()))
-SLABS = 17
+SLABS = 12
+CORNERS = SLABS - 1
 MIB = 1024 * 1024
 
 
@@ -115,8 +116,8 @@
         for p, q in ((0, 0), (0, CZ - 1), (CZ - 1, CZ - 1))
     ]
     corners = jnp.concatenate(corners + [jnp.zeros((5, CZ), F32)], 0)
-    keep_o[16] = corners
-    send_o[16] = corners
+    keep_o[CORNERS] = corners
+    send_o[CORNERS] = corners
 
     row16 = iota((16, CZ), 0)
     lane16 = iota((16, CZ), 1)
@@ -129,7 +130,7 @@
     z_table = jnp.where(piece < 6, six_table(zs[...], piece), 0.0)
 
     lane = iota((Y, CZ), 1)
-    row_y = iota((16, Y), 0)
+    row8 = iota((8, Y), 0)
     for which in early:
         fetch(which, 0).wait()
     inv_o[0] = inverse_eps(lab_s[0], eps)
@@ -189,18 +190,30 @@
             own = (c16 >= 0) & (c16 < 4)
             pick = jnp.where(
                 own & (row16 < 8) & (lane16 == CZ - 1 - c16), 1.0,
-                jnp.where(own & (row16 >= 8) & (c16 < 2) & (lane16 == 0), 1.0, 0.0),
+                jnp.where(own & (row16 >= 8) & (c16 == i) & (lane16 == 0), 1.0, 0.0),
             )
             acc_tops += mm(jnp.concatenate([pick, pick], 1).astype(BF), in_two(packed), NT)
 
-        acc_tops = jnp.where((row_y >= 8) & (lax.rem(row_y, 4) >= 2), 1.0, acc_tops)
-        for base, acc in ((0, acc_ends), (8, acc_tops)):
-            low, high = acc[:, :CZ], acc[:, CZ:]
-            keep = jnp.where(core == 0, low, high)
-            send = jnp.where(core == 0, high, low)
-            for part in range(2):
-                keep_o[base + 4 * part + i] = keep[8 * part:8 * part + 8]
-                send_o[base + 4 * part + i] = send[8 * part:8 * part + 8]
+        tops, planes = acc_tops[0:8], acc_tops[8:16]
+        outgoing = acc_ends[8:16] + jnp.where(lax.rem(row8, 4) >= 2, tops, 0.0)
+        comp = lax.rem(iota((8, CZ), 0), 4)
+        second = lax.rem(i, 2)
+        tops = jnp.where(second == 0, tops, pltpu.roll(tops, 2, 0))
+        tops_mine = comp // 2 == second
+        planes_mine = comp == i
+
+        def put(ref, low):
+            def half(v):
+                return jnp.where((core == 0) == low, v[:, :CZ], v[:, CZ:])
+
+            ref[i] = half(acc_ends[0:8])
+            ref[4 + i] = half(outgoing)
+            slab = 8 + i // 2
+            ref[slab] = jnp.where(tops_mine, half(tops), ref[slab])
+            ref[10] = jnp.where(planes_mine, half(planes), ref[10])
+
+        put(keep_o, True)
+        put(send_o, False)
         return carry
 
     lax.fori_loop(0, X // 2, one_pair, 0)
@@ -208,18 +221,33 @@
 
 def unpack(ref):
     m = ref[...]
+    comp = lax.rem(iota((8, CZ), 0), 4)
+    tops = [jnp.where(comp < 2, v, 0.0) for p in (m[8], m[9]) for v in (p, pltpu.roll(p, 6, 0))]
+    planes = m[10]
+
+    def plane(q):
+        return jnp.where(
+            comp == 0, pltpu.roll(planes, (8 - q) % 8, 0),
+            jnp.where(comp == 1, pltpu.roll(planes, (9 - q) % 8, 0), 0.0),
+        )
+
     return dict(
-        f=m[0:4], l=m[4:8], t=m[8:12], k=m[12:16],
-        a=m[16, 0:1, :], c=m[16, 1:2, :], z=m[16, 2:3, :],
+        f=m[0:4], l=m[4:8], t=jnp.stack(tops), k=jnp.stack([plane(q) for q in range(4)]),
+        a=m[CORNERS, 0:1, :], c=m[CORNERS, 1:2, :], z=m[CORNERS, 2:3, :],
     )
 
 
 def repack(s, ref):
+    comp = lax.rem(iota((8, CZ), 0), 4)
     ref[0:4] = s["f"]
     ref[4:8] = s["l"]
-    ref[8:12] = s["t"]
-    ref[12:16] = s["k"]
-    ref[16] = jnp.concatenate([s["a"], s["c"], s["z"], jnp.zeros((5, CZ), F32)], 0)
+    for p in range(2):
+        ref[8 + p] = jnp.where(comp < 2, s["t"][2 * p], pltpu.roll(s["t"][2 * p + 1], 2, 0))
+    planes = s["k"][0]
+    for q in range(1, 4):
+        planes = jnp.where(comp == q, pltpu.roll(s["k"][q], q, 0), planes)
+    ref[10] = planes
+    ref[CORNERS] = jnp.concatenate([s["a"], s["c"], s["z"], jnp.zeros((5, CZ), F32)], 0)
 
 
 def order(bit, own, other):

time: 66 us -> 65.5 us (level)
  waiting for transfers between devices: 25 us -> 23.7 us
  starting transfers between devices: 21.3 us -> 22.3 us
    ppermute x14, waiting for transfers between devices: 25 us -> 23.7 us  [swap(): lax.ppermute(block, axis, [(i, i ^ mask) for i in range(lax.axis_size(axi...]
    ppermute x14, starting transfers between devices: 21.3 us -> 22.3 us  [swap(): lax.ppermute(block, axis, [(i, i ^ mask) for i in range(lax.axis_size(axi...]
where the time goes in v5:
time: 65.5 us; the launch traced here: 65.4 us
  waiting for transfers between devices  23.7 us (36%)
  starting transfers between devices  22.3 us (34%)
  Pallas kernels  17.9 us (27%)
  between operations  1.39 us (2%)
    ppermute x14, waiting for transfers between devices, swap(): lax.ppermute(block, axis, [(i, i ^ mask) for i in range(lax.axis_size(axi...  23.7 us
    ppermute x14, starting transfers between devices, swap(): lax.ppermute(block, axis, [(i, i ^ mask) for i in range(lax.axis_size(axi...  22.3 us
    pallas_call x1, Pallas kernels, body(): call(rhs_kernel, 'right_hand_sides', [SMEM, SMEM] + [HBM] * 9, [slab] * 8...  7.31 us
    pallas_call x1, Pallas kernels, body(): call(output_kernel, 'outputs', [VMEM] * 8, [shape(3, X, Y, CZ)] * 2, 6, 1...  3.4 us
    pallas_call x1, Pallas kernels, body(): call(primal_kernel, 'primal_products', [VMEM] * 7 + [ANY], [slab] * 3, 4, 8)  2.25 us
    pallas_call x1, Pallas kernels, body(): call(adjoint_kernel, 'adjoint_products', [VMEM] * 5 + [HBM, ANY], [slab]...  1.84 us
    pallas_call x4, Pallas kernels, gradient(): call(lambda *refs: gradient_kernel(k, *refs), f'gradient_{k}', [VMEM] * 8...  1.84 us
  transfers between devices with their start and end apart: 14, of which 11 were waited for; matrix products, arithmetic and copies ran while one was open for 0% of the time, Pallas kernels for 14%

profile of v5, /device:TPU:1, one launch (start us, length us, event | category | flops | bytes accessed | tf_op | source)
XLA Modules:
  0.0 65.4 jit_solution(14774044151342825629)
XLA Ops:
  1.3 7.3 %right_hand_sides.1 = (f32[8,256,128]{2,1,0:T(8,128)S(1)}, f32[8,256,128]{2,1,0:T(8,128)S(1)}, f32[8,256,128]{2,1,0:T(8,128)S(1)}, f32[8,256,128]{2,1,0:T(8,128)...) custom-call(s32[1]{0:T(128)S(6)} %copy.14.angle, ...), custom_call_target="tpu_custom_call" | custom-call | flops 1000 | bytes 18000000 | tf_op jit(solution)/shard_map/right_hand_sides/pallas_call | solution.py:554
  8.6 1.5 %collective-permute-start = (f32[12,8,128]{2,1,0:T(8,128)S(1)}, f32[12,8,128]{2,1,0:T(8,128)S(1)}, u32[]{:S(2)}, u32[]{:S(2)}) collective-permute-start(f32[12,8,128]{2,1,0:T(8,128)S(1)} %get-tuple-element.33), channel_id=1, source_target_pairs={{0,1},{1,0},{2,3},{3,2},{4,5},{5,4},{6,7},{7,6},{8,9},{9,8},{10,11... | collective-permute-start | bytes 147464 | tf_op jit(solution)/shard_map/ppermute | solution.py:512
  10.1 0.9 %collective-permute-done.other.a1 = f32[12,8,128]{2,1,0:T(8,128)S(1)} collective-permute-done((f32[12,8,128]{2,1,0:T(8,128)S(1)}, f32[12,8,128]{2,1,0:T(8,128)S(1)}, u32[]{:S(2)}, u32[]{:S(2)}) %collective-permute-start) | collective-permute-done | bytes 49184 | tf_op jit(solution)/shard_map/ppermute | solution.py:512
  11.0 1.8 %collective-permute-start.1 = (f32[12,8,128]{2,1,0:T(8,128)S(1)}, f32[12,8,128]{2,1,0:T(8,128)S(1)}, u32[]{:S(2)}, u32[]{:S(2)}) collective-permute-start(f32[12,8,128]{2,1,0:T(8,128)S(1)} %chip.1.after.m0), channel_id=1, source_target_pairs={{0,2},{1,3},{2,0},{3,1},{4,6},{5,7},{6,4},{7,5},{8,10},{9,11},{10,... | collective-permute-start | bytes 147464 | tf_op jit(solution)/shard_map/ppermute | solution.py:512
  12.8 3.3 %collective-permute-start.2 = (f32[12,8,128]{2,1,0:T(8,128)S(1)}, f32[12,8,128]{2,1,0:T(8,128)S(1)}, u32[]{:S(2)}, u32[]{:S(2)}) collective-permute-start(f32[12,8,128]{2,1,0:T(8,128)S(1)} %chip.1.after.m0), channel_id=1, source_target_pairs={{0,4},{1,5},{2,6},{3,7},{4,0},{5,1},{6,2},{7,3},{8,12},{9,13},{10,... | collective-permute-start | bytes 147464 | tf_op jit(solution)/shard_map/ppermute | solution.py:512
  16.1 1.8 %adjoint_products.1 = (f32[8,256,128]{2,1,0:T(8,128)S(1)}, f32[8,256,128]{2,1,0:T(8,128)S(1)}) custom-call(f32[8,256,128]{2,1,0:T(8,128)S(1)} %get-tuple-element.27.ax, f32[8,256,128]{2,1,0:T(8,128)S(1)} %get-tuple-element.28.ay, f32[8,256,128]{2,1,0:T(8,128)S(1)} %get-tuple-element.29.psx.refs_1_, f32[8,256,128]{2,1,0:T(8,128)S(1)} %get-tuple-element.30.psy.refs_2_, ...), custom_call_target="tpu_custom_call" | custom-call | flops 1000 | bytes 9000000 | tf_op jit(solution)/shard_map/adjoint_products/pallas_call | solution.py:570
  18.4 1.9 %collective-permute-done.3.m3 = f32[12,8,128]{2,1,0:T(8,128)S(1)} collective-permute-done((f32[12,8,128]{2,1,0:T(8,128)S(1)}, f32[12,8,128]{2,1,0:T(8,128)S(1)}, u32[]{:S(2)}, u32[]{:S(2)}) %collective-permute-start.3) | collective-permute-done | bytes 49184 | tf_op jit(solution)/shard_map/ppermute | solution.py:512
  20.3 1.3 %collective-permute-start.4 = (f32[12,8,128]{2,1,0:T(8,128)S(1)}, f32[12,8,128]{2,1,0:T(8,128)S(1)}, u32[]{:S(2)}, u32[]{:S(2)}) collective-permute-start(f32[12,8,128]{2,1,0:T(8,128)S(1)} %group.1.after.n0), channel_id=1, source_target_pairs={{0,8},{1,9},{2,10},{3,11},{4,12},{5,13},{6,14},{7,15},{8,0},{9,1},... | collective-permute-start | bytes 147464 | tf_op jit(solution)/shard_map/ppermute | solution.py:512
  21.6 2.5 %collective-permute-start.5 = (f32[12,8,128]{2,1,0:T(8,128)S(1)}, f32[12,8,128]{2,1,0:T(8,128)S(1)}, u32[]{:S(2)}, u32[]{:S(2)}) collective-permute-start(f32[12,8,128]{2,1,0:T(8,128)S(1)} %group.1.after.n0), channel_id=1, source_target_pairs={{0,16},{1,17},{2,18},{3,19},{4,20},{5,21},{6,22},{7,23},{8,24},{9,... | collective-permute-start | bytes 147464 | tf_op jit(solution)/shard_map/ppermute | solution.py:512
  24.3 2.3 %primal_products.1 = (f32[8,256,128]{2,1,0:T(8,128)S(1)}, f32[8,256,128]{2,1,0:T(8,128)S(1)}, f32[8,256,128]{2,1,0:T(8,128)S(1)}) custom-call(f32[8,256,128]{2,1,0:T(8,128)S(1)} %get-tuple-element.24.rx, f32[8,256,128]{2,1,0:T(8,128)S(1)} %get-tuple-element.25.ry, f32[3,8,256,128]{3,2,1,0:T(8,128)S(1)} %get-tuple-element.26.h, ...), custom_call_target="tpu_custom_call" | custom-call | flops 1000 | bytes 12000000 | tf_op jit(solution)/shard_map/primal_products/pallas_call | solution.py:577
  26.6 1.7 %collective-permute-done.6.n3 = f32[12,8,128]{2,1,0:T(8,128)S(1)} collective-permute-done((f32[12,8,128]{2,1,0:T(8,128)S(1)}, f32[12,8,128]{2,1,0:T(8,128)S(1)}, u32[]{:S(2)}, u32[]{:S(2)}) %collective-permute-start.6) | collective-permute-done | bytes 49184 | tf_op jit(solution)/shard_map/ppermute | solution.py:512
  28.4 3.9 %collective-permute-start.7 = (f32[12,8,128]{2,1,0:T(8,128)S(1)}, f32[12,8,128]{2,1,0:T(8,128)S(1)}, u32[]{:S(2)}, u32[]{:S(2)}) collective-permute-start(f32[12,8,128]{2,1,0:T(8,128)S(1)} %get-tuple-element.41), channel_id=1, source_target_pairs={{0,1},{1,0},{2,3},{3,2},{4,5},{5,4},{6,7},{7,6},{8,9},{9,8},{10,11... | collective-permute-start | bytes 147464 | tf_op jit(solution)/shard_map/ppermute | solution.py:512
  32.3 0.9 %collective-permute-done.7.recv.refs_6_ = f32[12,8,128]{2,1,0:T(8,128)S(1)} collective-permute-done((f32[12,8,128]{2,1,0:T(8,128)S(1)}, f32[12,8,128]{2,1,0:T(8,128)S(1)}, u32[]{:S(2)}, u32[]{:S(2)}) %collective-permute-start.7) | collective-permute-done | bytes 49184 | tf_op jit(solution)/shard_map/ppermute | solution.py:512
  33.6 3.0 %collective-permute-start.8 = (f32[2,256,128]{2,1,0:T(8,128)S(1)}, f32[2,256,128]{2,1,0:T(8,128)S(1)}, u32[]{:S(2)}, u32[]{:S(2)}) collective-permute-start(f32[2,256,128]{2,1,0:T(8,128)S(1)} %gradient_2.1), channel_id=1, source_target_pairs={{0,64},{32,96},{64,0},{96,32},{1,65},{33,97},{65,1},{97,33},{2,66}... | collective-permute-start | bytes 786440 | tf_op jit(solution)/shard_map/ppermute | solution.py:512
  37.1 0.5 collective-permute-start.9
  38.0 0.5 collective-permute-start.10
  38.5 0.5 gradient_0.1
  39.0 3.8 %collective-permute-done.8 = f32[2,256,128]{2,1,0:T(8,128)S(1)} collective-permute-done((f32[2,256,128]{2,1,0:T(8,128)S(1)}, f32[2,256,128]{2,1,0:T(8,128)S(1)}, u32[]{:S(2)}, u32[]{:S(2)}) %collective-permute-start.8) | collective-permute-done | bytes 262176 | tf_op jit(solution)/shard_map/ppermute | solution.py:512
  42.7 6.0 %collective-permute-done.9 = f32[2,256,128]{2,1,0:T(8,128)S(1)} collective-permute-done((f32[2,256,128]{2,1,0:T(8,128)S(1)}, f32[2,256,128]{2,1,0:T(8,128)S(1)}, u32[]{:S(2)}, u32[]{:S(2)}) %collective-permute-start.9) | collective-permute-done | bytes 262176 | tf_op jit(solution)/shard_map/ppermute | solution.py:512
  48.9 3.2 %collective-permute-start.11 = (f32[2,256,128]{2,1,0:T(8,128)S(1)}, f32[2,256,128]{2,1,0:T(8,128)S(1)}, u32[]{:S(2)}, u32[]{:S(2)}) collective-permute-start(f32[2,256,128]{2,1,0:T(8,128)S(1)} %add_add_fusion.g0), channel_id=1, source_target_pairs={{0,64},{32,96},{64,0},{96,32},{1,65},{33,97},{65,1},{97,33},{2,66}... | collective-permute-start | bytes 786440 | tf_op jit(solution)/shard_map/ppermute | solution.py:512
  52.9 3.4 %outputs.1 = (f32[3,8,256,128]{3,2,1,0:T(8,128)}, f32[3,8,256,128]{3,2,1,0:T(8,128)}) custom-call(f32[8,256,128]{2,1,0:T(8,128)S(1)} %get-tuple-element.37.after.ex, f32[8,256,128]{2,1,0:T(8,128)S(1)} %get-tuple-element.38.ey, f32[3,8,256,128]{3,2,1,0:T(8,128)S(1)} %get-tuple-element.26.h, f32[8,256,128]{2,1,0:T(8,128)S(1)} %get-tuple-element.34.ez, ...), custom_call_target="tpu_custom_call" | custom-call | flops 1000 | bytes 18000000 | tf_op jit(solution)/shard_map/outputs/pallas_call | solution.py:594
  56.3 1.2 %collective-permute-done.11.g2 = f32[2,256,128]{2,1,0:T(8,128)S(1)} collective-permute-done((f32[2,256,128]{2,1,0:T(8,128)S(1)}, f32[2,256,128]{2,1,0:T(8,128)S(1)}, u32[]{:S(2)}, u32[]{:S(2)}) %collective-permute-start.11) | collective-permute-done | bytes 262176 | tf_op jit(solution)/shard_map/ppermute | solution.py:512
  57.5 6.6 %collective-permute-done.12.g1 = f32[2,256,128]{2,1,0:T(8,128)S(1)} collective-permute-done((f32[2,256,128]{2,1,0:T(8,128)S(1)}, f32[2,256,128]{2,1,0:T(8,128)S(1)}, u32[]{:S(2)}, u32[]{:S(2)}) %collective-permute-start.12) | collective-permute-done | bytes 262176 | tf_op jit(solution)/shard_map/ppermute | solution.py:512
  64.4 1.0 %place.1 = f32[8,256,128]{2,1,0:T(8,128)} custom-call(f32[2,256,128]{2,1,0:T(8,128)S(1)} %collective-permute-done.11.g2, f32[2,256,128]{2,1,0:T(8,128)S(1)} %collective-permute-done.12.g1, f32[2,256,128]{2,1,0:T(8,128)S(1)} %collective-permute-done.13.g3, f32[2,256,128]{2,1,0:T(8,128)S(1)} %add_add_fusion.g0), custom_call_target="tpu_custom_call" | custom-call | flops 1000 | bytes 3000000 | tf_op jit(solution)/shard_map/place/pallas_call | solution.py:602
  (17 shorter events, 3.5 us)
Async XLA Ops:
  8.6 2.4 %collective-permute-start = (f32[12,8,128]{2,1,0:T(8,128)S(1)}, f32[12,8,128]{2,1,0:T(8,128)S(1)}, u32[]{:S(2)}, u32[]{:S(2)}) collective-permute-start(f32[12,8,128]{2,1,0:T(8,128)S(1)} %get-tuple-element.33), channel_id=1, source_target_pairs={{0,1},{1,0},{2,3},{3,2},{4,5},{5,4},{6,7},{7,6},{8,9},{9,8},{10,11... | collective-permute-start | bytes 147464 | tf_op jit(solution)/shard_map/ppermute | solution.py:512
  11.0 7.0 %collective-permute-start.1 = (f32[12,8,128]{2,1,0:T(8,128)S(1)}, f32[12,8,128]{2,1,0:T(8,128)S(1)}, u32[]{:S(2)}, u32[]{:S(2)}) collective-permute-start(f32[12,8,128]{2,1,0:T(8,128)S(1)} %chip.1.after.m0), channel_id=1, source_target_pairs={{0,2},{1,3},{2,0},{3,1},{4,6},{5,7},{6,4},{7,5},{8,10},{9,11},{10,... | collective-permute-start | bytes 147464 | tf_op jit(solution)/shard_map/ppermute | solution.py:512
  12.8 5.6 %collective-permute-start.2 = (f32[12,8,128]{2,1,0:T(8,128)S(1)}, f32[12,8,128]{2,1,0:T(8,128)S(1)}, u32[]{:S(2)}, u32[]{:S(2)}) collective-permute-start(f32[12,8,128]{2,1,0:T(8,128)S(1)} %chip.1.after.m0), channel_id=1, source_target_pairs={{0,4},{1,5},{2,6},{3,7},{4,0},{5,1},{6,2},{7,3},{8,12},{9,13},{10,... | collective-permute-start | bytes 147464 | tf_op jit(solution)/shard_map/ppermute | solution.py:512
  16.1 4.2 %collective-permute-start.3 = (f32[12,8,128]{2,1,0:T(8,128)S(1)}, f32[12,8,128]{2,1,0:T(8,128)S(1)}, u32[]{:S(2)}, u32[]{:S(2)}) collective-permute-start(f32[12,8,128]{2,1,0:T(8,128)S(1)} %chip.1.after.m0), channel_id=1, source_target_pairs={{0,6},{1,7},{2,4},{3,5},{4,2},{5,3},{6,0},{7,1},{8,14},{9,15},{10,... | collective-permute-start | bytes 147464 | tf_op jit(solution)/shard_map/ppermute | solution.py:512
  20.3 6.2 %collective-permute-start.4 = (f32[12,8,128]{2,1,0:T(8,128)S(1)}, f32[12,8,128]{2,1,0:T(8,128)S(1)}, u32[]{:S(2)}, u32[]{:S(2)}) collective-permute-start(f32[12,8,128]{2,1,0:T(8,128)S(1)} %group.1.after.n0), channel_id=1, source_target_pairs={{0,8},{1,9},{2,10},{3,11},{4,12},{5,13},{6,14},{7,15},{8,0},{9,1},... | collective-permute-start | bytes 147464 | tf_op jit(solution)/shard_map/ppermute | solution.py:512
  21.6 4.9 %collective-permute-start.5 = (f32[12,8,128]{2,1,0:T(8,128)S(1)}, f32[12,8,128]{2,1,0:T(8,128)S(1)}, u32[]{:S(2)}, u32[]{:S(2)}) collective-permute-start(f32[12,8,128]{2,1,0:T(8,128)S(1)} %group.1.after.n0), channel_id=1, source_target_pairs={{0,16},{1,17},{2,18},{3,19},{4,20},{5,21},{6,22},{7,23},{8,24},{9,... | collective-permute-start | bytes 147464 | tf_op jit(solution)/shard_map/ppermute | solution.py:512
  24.1 4.2 %collective-permute-start.6 = (f32[12,8,128]{2,1,0:T(8,128)S(1)}, f32[12,8,128]{2,1,0:T(8,128)S(1)}, u32[]{:S(2)}, u32[]{:S(2)}) collective-permute-start(f32[12,8,128]{2,1,0:T(8,128)S(1)} %group.1.after.n0), channel_id=1, source_target_pairs={{0,24},{1,25},{2,26},{3,27},{4,28},{5,29},{6,30},{7,31},{8,16},{9,... | collective-permute-start | bytes 147464 | tf_op jit(solution)/shard_map/ppermute | solution.py:512
  28.4 4.7 %collective-permute-start.7 = (f32[12,8,128]{2,1,0:T(8,128)S(1)}, f32[12,8,128]{2,1,0:T(8,128)S(1)}, u32[]{:S(2)}, u32[]{:S(2)}) collective-permute-start(f32[12,8,128]{2,1,0:T(8,128)S(1)} %get-tuple-element.41), channel_id=1, source_target_pairs={{0,1},{1,0},{2,3},{3,2},{4,5},{5,4},{6,7},{7,6},{8,9},{9,8},{10,11... | collective-permute-start | bytes 147464 | tf_op jit(solution)/shard_map/ppermute | solution.py:512
  33.6 9.1 %collective-permute-start.8 = (f32[2,256,128]{2,1,0:T(8,128)S(1)}, f32[2,256,128]{2,1,0:T(8,128)S(1)}, u32[]{:S(2)}, u32[]{:S(2)}) collective-permute-start(f32[2,256,128]{2,1,0:T(8,128)S(1)} %gradient_2.1), channel_id=1, source_target_pairs={{0,64},{32,96},{64,0},{96,32},{1,65},{33,97},{65,1},{97,33},{2,66}... | collective-permute-start | bytes 786440 | tf_op jit(solution)/shard_map/ppermute | solution.py:512
  37.1 11.7 %collective-permute-start.9 = (f32[2,256,128]{2,1,0:T(8,128)S(1)}, f32[2,256,128]{2,1,0:T(8,128)S(1)}, u32[]{:S(2)}, u32[]{:S(2)}) collective-permute-start(f32[2,256,128]{2,1,0:T(8,128)S(1)} %gradient_1.1), channel_id=1, source_target_pairs={{0,32},{32,0},{64,96},{96,64},{1,33},{33,1},{65,97},{97,65},{2,34}... | collective-permute-start | bytes 786440 | tf_op jit(solution)/shard_map/ppermute | solution.py:512
  38.0 10.8 %collective-permute-start.10 = (f32[2,256,128]{2,1,0:T(8,128)S(1)}, f32[2,256,128]{2,1,0:T(8,128)S(1)}, u32[]{:S(2)}, u32[]{:S(2)}) collective-permute-start(f32[2,256,128]{2,1,0:T(8,128)S(1)} %gradient_3.1), channel_id=1, source_target_pairs={{0,96},{32,64},{64,32},{96,0},{1,97},{33,65},{65,33},{97,1},{2,98}... | collective-permute-start | bytes 786440 | tf_op jit(solution)/shard_map/ppermute | solution.py:512
  48.9 8.6 %collective-permute-start.11 = (f32[2,256,128]{2,1,0:T(8,128)S(1)}, f32[2,256,128]{2,1,0:T(8,128)S(1)}, u32[]{:S(2)}, u32[]{:S(2)}) collective-permute-start(f32[2,256,128]{2,1,0:T(8,128)S(1)} %add_add_fusion.g0), channel_id=1, source_target_pairs={{0,64},{32,96},{64,0},{96,32},{1,65},{33,97},{65,1},{97,33},{2,66}... | collective-permute-start | bytes 786440 | tf_op jit(solution)/shard_map/ppermute | solution.py:512
  52.1 12.0 %collective-permute-start.12 = (f32[2,256,128]{2,1,0:T(8,128)S(1)}, f32[2,256,128]{2,1,0:T(8,128)S(1)}, u32[]{:S(2)}, u32[]{:S(2)}) collective-permute-start(f32[2,256,128]{2,1,0:T(8,128)S(1)} %add_add_fusion.g0), channel_id=1, source_target_pairs={{0,32},{32,0},{64,96},{96,64},{1,33},{33,1},{65,97},{97,65},{2,34}... | collective-permute-start | bytes 786440 | tf_op jit(solution)/shard_map/ppermute | solution.py:512
  52.5 11.9 %collective-permute-start.13 = (f32[2,256,128]{2,1,0:T(8,128)S(1)}, f32[2,256,128]{2,1,0:T(8,128)S(1)}, u32[]{:S(2)}, u32[]{:S(2)}) collective-permute-start(f32[2,256,128]{2,1,0:T(8,128)S(1)} %add_add_fusion.g0), channel_id=1, source_target_pairs={{0,96},{32,64},{64,32},{96,0},{1,97},{33,65},{65,33},{97,1},{2,98}... | collective-permute-start | bytes 786440 | tf_op jit(solution)/shard_map/ppermute | solution.py:512

commit v6 on v5

--- a/solution.py
+++ b/solution.py
@@ -73,11 +73,9 @@
 
 def rhs_kernel(
     angle, eps, e, h, ge, gh, lab, prof_in, zs_in, lt_in, w_in,
-    rx_o, ry_o, ax_o, ay_o, psx_o, psy_o, gs_o, inv_o, h_o, w, keep_o, send_o,
+    rx_o, ry_o, ax_o, ay_o, psx_o, psy_o, gs_o, inv_o, h_o, w, mine_o,
     e_s, ge_s, gh_s, lab_s, sems, prof_s, prof, zs, lt,
 ):
-    core = lax.rem(lax.axis_index("gz"), 2)
-
     def fetch(which, x):
         at = pl.ds(x, 1)
         return (
@@ -112,12 +110,10 @@
     rows = jnp.concatenate(six_rows(both) + [jnp.zeros((32, Y), F32)], 0)
     prof_s[...] = rows.T.astype(BF)
     corners = [
-        jnp.broadcast_to(w[p:p + 1, q:q + 1], (1, CZ))
+        jnp.broadcast_to(w[p:p + 1, q:q + 1], (1, Y))
         for p, q in ((0, 0), (0, CZ - 1), (CZ - 1, CZ - 1))
     ]
-    corners = jnp.concatenate(corners + [jnp.zeros((5, CZ), F32)], 0)
-    keep_o[CORNERS] = corners
-    send_o[CORNERS] = corners
+    mine_o[CORNERS] = jnp.concatenate(corners + [jnp.zeros((5, Y), F32)], 0)
 
     row16 = iota((16, CZ), 0)
     lane16 = iota((16, CZ), 1)
@@ -195,25 +191,14 @@
             acc_tops += mm(jnp.concatenate([pick, pick], 1).astype(BF), in_two(packed), NT)
 
         tops, planes = acc_tops[0:8], acc_tops[8:16]
-        outgoing = acc_ends[8:16] + jnp.where(lax.rem(row8, 4) >= 2, tops, 0.0)
-        comp = lax.rem(iota((8, CZ), 0), 4)
+        comp = lax.rem(row8, 4)
         second = lax.rem(i, 2)
+        mine_o[i] = acc_ends[0:8]
+        mine_o[4 + i] = acc_ends[8:16] + jnp.where(comp >= 2, tops, 0.0)
         tops = jnp.where(second == 0, tops, pltpu.roll(tops, 2, 0))
-        tops_mine = comp // 2 == second
-        planes_mine = comp == i
-
-        def put(ref, low):
-            def half(v):
-                return jnp.where((core == 0) == low, v[:, :CZ], v[:, CZ:])
-
-            ref[i] = half(acc_ends[0:8])
-            ref[4 + i] = half(outgoing)
-            slab = 8 + i // 2
-            ref[slab] = jnp.where(tops_mine, half(tops), ref[slab])
-            ref[10] = jnp.where(planes_mine, half(planes), ref[10])
-
-        put(keep_o, True)
-        put(send_o, False)
+        slab = 8 + i // 2
+        mine_o[slab] = jnp.where(comp // 2 == second, tops, mine_o[slab])
+        mine_o[10] = jnp.where(comp == i, planes, mine_o[10])
         return carry
 
     lax.fori_loop(0, X // 2, one_pair, 0)
@@ -221,7 +206,7 @@
 
 def unpack(ref):
     m = ref[...]
-    comp = lax.rem(iota((8, CZ), 0), 4)
+    comp = lax.rem(iota((8, Y), 0), 4)
     tops = [jnp.where(comp < 2, v, 0.0) for p in (m[8], m[9]) for v in (p, pltpu.roll(p, 6, 0))]
     planes = m[10]
 
@@ -238,7 +223,7 @@
 
 
 def repack(s, ref):
-    comp = lax.rem(iota((8, CZ), 0), 4)
+    comp = lax.rem(iota((8, Y), 0), 4)
     ref[0:4] = s["f"]
     ref[4:8] = s["l"]
     for p in range(2):
@@ -247,7 +232,7 @@
     for q in range(1, 4):
         planes = jnp.where(comp == q, pltpu.roll(s["k"][q], q, 0), planes)
     ref[10] = planes
-    ref[CORNERS] = jnp.concatenate([s["a"], s["c"], s["z"], jnp.zeros((5, CZ), F32)], 0)
+    ref[CORNERS] = jnp.concatenate([s["a"], s["c"], s["z"], jnp.zeros((5, Y), F32)], 0)
 
 
 def order(bit, own, other):
@@ -293,13 +278,11 @@
 
 def bits():
     gz = lax.axis_index("gz")
-    core, low_z, high_z = lax.rem(gz, 2), lax.rem(gz // 2, 2), lax.rem(gz // 4, 2)
-    return core, low_z, high_z, lax.rem(gz // 8, 2), gz // 16
+    return lax.rem(gz // 2, 2), lax.rem(gz // 4, 2), lax.rem(gz // 8, 2), gz // 16
 
 
 def chip_kernel(own, other, out):
-    core = bits()[0]
-    repack(combine(*order(core, unpack(own), unpack(other))), out)
+    repack(combine(unpack(other), unpack(own)), out)
 
 
 def four(low, high, own, m1, m2, m3):
@@ -309,13 +292,13 @@
 
 
 def group_kernel(m0, m1, m2, m3, after, out):
-    _, low, high, _, _ = bits()
+    low, high, _, _ = bits()
     repack(combine(*four(low, high, *(unpack(m) for m in (m0, m1, m2, m3)))[1]), out)
 
 
 def back_kernel(a0, a1, m0, m1, m2, m3, n0, n1, n2, n3, after, keep_o, send_o):
-    core, zl, zh, xl, xh = bits()
-    chip = order(core, unpack(a0), unpack(a1))
+    zl, zh, xl, xh = bits()
+    chip = unpack(a1), unpack(a0)
     m0, m1, m2, m3 = (unpack(m) for m in (m0, m1, m2, m3))
     n0, n1, n2, n3 = (unpack(n) for n in (n0, n1, n2, n3))
     z_first, z_second = four(zl, zh, m0, m1, m2, m3)
@@ -330,16 +313,13 @@
     t, u = outside(lower, upper, *edge)
     under_x = jnp.where(xl == 1, n1["t"], jnp.where(xh == 1, n3["t"], zero))
     under = jnp.where(zl == 1, m1["t"], jnp.where(zh == 1, m3["t"], under_x))
-    results = []
-    for block, below, above, plane in ((lower, edge[0], t, under), (upper, u, edge[1], lower["t"])):
+    pairs = ((send_o, lower, edge[0], t, under), (keep_o, upper, u, edge[1], lower["t"]))
+    for out, block, below, above, plane in pairs:
         below = below + block["k"] * plane
         first = block["f"] + block["a"] * below + block["c"] * above
-        extra = jnp.stack([first[q] * pltpu.roll(plane[q], 2, 0) for q in range(4)])
-        results.append((below, above, extra))
-    for part in range(3):
-        low, high = results[0][part], results[1][part]
-        keep_o[4 * part:4 * part + 4] = jnp.where(core == 0, low, high)
-        send_o[4 * part:4 * part + 4] = jnp.where(core == 0, high, low)
+        out[0:4] = below
+        out[4:8] = above
+        out[8:12] = jnp.stack([first[q] * pltpu.roll(plane[q], 2, 0) for q in range(4)])
 
 
 def product_tables(w):
@@ -385,9 +365,7 @@
 
 
 def edge_rows(keep, recv, slab):
-    core = lax.rem(lax.axis_index("gz"), 2)
-    a, b = keep[slab], recv[slab]
-    return jnp.concatenate([jnp.where(core == 0, a, b), jnp.where(core == 0, b, a)], 1)
+    return jnp.where(lax.rem(lax.axis_index("gz"), 2) == 0, recv[slab], keep[slab])
 
 
 def columns(below, above):
@@ -512,6 +490,15 @@
     return lax.ppermute(block, axis, [(i, i ^ mask) for i in range(lax.axis_size(axis))])
 
 
+def among_second(block, mask):
+    return lax.ppermute(block, "gz", [(i, i ^ mask) for i in range(1, lax.axis_size("gz"), 2)])
+
+
+def across_chip(block, source):
+    chips = range(0, lax.axis_size("gz"), 2)
+    return lax.ppermute(block, "gz", [(i + source, i + 1 - source) for i in chips])
+
+
 SMEM = pl.BlockSpec(memory_space=pltpu.SMEM)
 VMEM = pl.BlockSpec(memory_space=pltpu.VMEM)
 HBM = pl.BlockSpec(memory_space=pltpu.HBM)
@@ -546,15 +533,15 @@
     e, h, ge, gh = fields_e[0], fields_h[0], cot_e[0], cot_h[0]
     zs, lt = zsheet.reshape(1, CZ), layer_term.reshape(1, CZ)
     slab = shape(X, Y, CZ)
-    message = shape(SLABS, 8, CZ)
+    message = shape(SLABS, 8, Y)
 
     def space(*dims, dtype=F32):
         return pltpu.VMEM(dims, dtype)
 
-    rx, ry, ax, ay, psx, psy, gs, inv, hv, w, keep, send = call(
+    rx, ry, ax, ay, psx, psy, gs, inv, hv, w, mine = call(
         rhs_kernel, "right_hand_sides",
         [SMEM, SMEM] + [HBM] * 9,
-        [slab] * 8 + [shape(3, X, Y, CZ), shape(CZ, CZ)] + [message] * 2,
+        [slab] * 8 + [shape(3, X, Y, CZ), shape(CZ, CZ)] + [message],
         6, 24,
         scratch=[
             space(2, X, Y, CZ), space(3, X, Y, CZ), space(3, X, Y, CZ),
@@ -563,24 +550,24 @@
         ],
     )(angle_index, *map(in_hbm, (region_eps, e, h, ge, gh, labels, profiles, zs, lt, block_inverse)))
 
-    other = swap(send, "gz", 1)
-    (m0,) = call(chip_kernel, "chip", [VMEM] * 2, [message], 0.5, 4)(keep, other)
-    m1, m2, m3 = (swap(m0, "gz", 2 * k) for k in (1, 2, 3))
+    other = across_chip(mine, 0)
+    (m0,) = call(chip_kernel, "chip", [VMEM] * 2, [message], 0.5, 4)(mine, other)
+    m1, m2, m3 = (among_second(m0, 2 * k) for k in (1, 2, 3))
 
     adjoint, ez = call(
         adjoint_kernel, "adjoint_products", [VMEM] * 5 + [HBM, ANY], [slab] * 2, 3, 8,
         scratch=[pltpu.SemaphoreType.DMA],
     )(ax, ay, psx, psy, w, in_hbm(e), m0)
     (n0,) = call(group_kernel, "group", [VMEM] * 4 + [ANY], [message], 0.5, 4)(m0, m1, m2, m3, adjoint)
-    n1, n2, n3 = (swap(n0, "gz", 8 * k) for k in (1, 2, 3))
+    n1, n2, n3 = (among_second(n0, 8 * k) for k in (1, 2, 3))
 
     ex, ey, grad = call(primal_kernel, "primal_products", [VMEM] * 7 + [ANY], [slab] * 3, 4, 8)(
         rx, ry, hv, ez, gs, adjoint, w, n0
     )
     own_edges, send_edges = call(
-        back_kernel, "back", [VMEM] * 10 + [ANY], [shape(12, 8, CZ)] * 2, 0.5, 4
-    )(keep, other, m0, m1, m2, m3, n0, n1, n2, n3, ex)
-    other_edges = swap(send_edges, "gz", 1)
+        back_kernel, "back", [VMEM] * 10 + [ANY], [shape(12, 8, Y)] * 2, 0.5, 4
+    )(mine, other, m0, m1, m2, m3, n0, n1, n2, n3, ex)
+    other_edges = across_chip(send_edges, 1)
 
     def gradient(k):
         return call(

time: 65.5 us -> 77.3 us (1.18)
  starting transfers between devices: 22.3 us -> 31.3 us
  waiting for transfers between devices: 23.7 us -> 26 us
    ppermute x0 -> x8, starting transfers between devices: none -> 23.4 us  [the longest x6 20.8 us: among_second(): lax.ppermute(block, 'gz', [(i, i ^ mask) for i in range(1, lax.axis_size(...]
    ppermute x14 -> x6, starting transfers between devices: 22.3 us -> 7.95 us  [swap(): lax.ppermute(block, axis, [(i, i ^ mask) for i in range(lax.axis_size(axi...]
    ppermute x0 -> x8, waiting for transfers between devices: none -> 8.06 us  [the longest x6 4.95 us: among_second(): lax.ppermute(block, 'gz', [(i, i ^ mask) for i in range(1, lax.axis_size(...]
    ppermute x14 -> x6, waiting for transfers between devices: 23.7 us -> 17.9 us  [swap(): lax.ppermute(block, axis, [(i, i ^ mask) for i in range(lax.axis_size(axi...]
  transfers between devices with their start and end apart: 14 -> 14, of which waited for: 11 -> 10; matrix products, arithmetic and copies ran while one was open for 0% -> 0% of each run, Pallas kernels for 14% -> 12%
where the time goes in v6:
time: 77.3 us; the launch traced here: 77 us
  starting transfers between devices  31.3 us (40%)
  waiting for transfers between devices  26 us (34%)
  Pallas kernels  18.1 us (23%)
  between operations  1.46 us (2%)
    ppermute x6, starting transfers between devices, among_second(): lax.ppermute(block, 'gz', [(i, i ^ mask) for i in range(1, lax.axis_size(...  20.8 us
    ppermute x6, waiting for transfers between devices, swap(): lax.ppermute(block, axis, [(i, i ^ mask) for i in range(lax.axis_size(axi...  17.9 us
    ppermute x6, starting transfers between devices, swap(): lax.ppermute(block, axis, [(i, i ^ mask) for i in range(lax.axis_size(axi...  7.95 us
    pallas_call x1, Pallas kernels, body(): call(rhs_kernel, 'right_hand_sides', [SMEM, SMEM] + [HBM] * 9, [slab] * 8...  7.3 us
    ppermute x6, waiting for transfers between devices, among_second(): lax.ppermute(block, 'gz', [(i, i ^ mask) for i in range(1, lax.axis_size(...  4.95 us
    pallas_call x1, Pallas kernels, body(): call(output_kernel, 'outputs', [VMEM] * 8, [shape(3, X, Y, CZ)] * 2, 6, 1...  3.41 us
    ppermute x2, waiting for transfers between devices, across_chip(): lax.ppermute(block, 'gz', [(i + source, i + 1 - source) for i in chips])  3.11 us
    ppermute x2, starting transfers between devices, across_chip(): lax.ppermute(block, 'gz', [(i + source, i + 1 - source) for i in chips])  2.59 us
  transfers between devices with their start and end apart: 14, of which 10 were waited for; matrix products, arithmetic and copies ran while one was open for 0% of the time, Pallas kernels for 12%

profile of v6, /device:TPU:1, one launch (start us, length us, event | category | flops | bytes accessed | tf_op | source)
XLA Modules:
  0.0 77.0 jit_solution(12648175956103478405)
XLA Ops:
  1.3 7.3 %right_hand_sides.1 = (f32[8,256,128]{2,1,0:T(8,128)S(1)}, f32[8,256,128]{2,1,0:T(8,128)S(1)}, f32[8,256,128]{2,1,0:T(8,128)S(1)}, f32[8,256,128]{2,1,0:T(8,128)...) custom-call(s32[1]{0:T(128)S(6)} %copy.14.angle, ...), custom_call_target="tpu_custom_call" | custom-call | flops 1000 | bytes 18000000 | tf_op jit(solution)/shard_map/right_hand_sides/pallas_call | solution.py:541
  8.6 1.3 %collective-permute-start = (f32[12,8,256]{2,1,0:T(8,128)S(1)}, f32[12,8,256]{2,1,0:T(8,128)S(1)}, u32[]{:S(2)}, u32[]{:S(2)}) collective-permute-start(f32[12,8,256]{2,1,0:T(8,128)S(1)} %get-tuple-element.31.own.a0), channel_id=1, source_target_pairs={{0,1},{2,3},{4,5},{6,7},{8,9},{10,11},{12,13},{14,15},{16,17},{18,... | collective-permute-start | bytes 294920 | tf_op jit(solution)/shard_map/ppermute | solution.py:499
  9.9 2.2 %collective-permute-done.other.a1 = f32[12,8,256]{2,1,0:T(8,128)S(1)} collective-permute-done((f32[12,8,256]{2,1,0:T(8,128)S(1)}, f32[12,8,256]{2,1,0:T(8,128)S(1)}, u32[]{:S(2)}, u32[]{:S(2)}) %collective-permute-start) | collective-permute-done | bytes 98336 | tf_op jit(solution)/shard_map/ppermute | solution.py:499
  12.1 4.1 %collective-permute-start.1 = (f32[12,8,256]{2,1,0:T(8,128)S(1)}, f32[12,8,256]{2,1,0:T(8,128)S(1)}, u32[]{:S(2)}, u32[]{:S(2)}) collective-permute-start(f32[12,8,256]{2,1,0:T(8,128)S(1)} %chip.1.after.m0), channel_id=1, source_target_pairs={{1,3},{3,1},{5,7},{7,5},{9,11},{11,9},{13,15},{15,13},{17,19},{19,... | collective-permute-start | bytes 294920 | tf_op jit(solution)/shard_map/ppermute | solution.py:494
  16.2 5.2 %collective-permute-start.2 = (f32[12,8,256]{2,1,0:T(8,128)S(1)}, f32[12,8,256]{2,1,0:T(8,128)S(1)}, u32[]{:S(2)}, u32[]{:S(2)}) collective-permute-start(f32[12,8,256]{2,1,0:T(8,128)S(1)} %chip.1.after.m0), channel_id=1, source_target_pairs={{1,5},{3,7},{5,1},{7,3},{9,13},{11,15},{13,9},{15,11},{17,21},{19,... | collective-permute-start | bytes 294920 | tf_op jit(solution)/shard_map/ppermute | solution.py:494
  21.4 1.9 %collective-permute-start.3 = (f32[12,8,256]{2,1,0:T(8,128)S(1)}, f32[12,8,256]{2,1,0:T(8,128)S(1)}, u32[]{:S(2)}, u32[]{:S(2)}) collective-permute-start(f32[12,8,256]{2,1,0:T(8,128)S(1)} %chip.1.after.m0), channel_id=1, source_target_pairs={{1,7},{3,5},{5,3},{7,1},{9,15},{11,13},{13,11},{15,9},{17,23},{19,... | collective-permute-start | bytes 294920 | tf_op jit(solution)/shard_map/ppermute | solution.py:494
  23.4 1.9 %adjoint_products.1 = (f32[8,256,128]{2,1,0:T(8,128)S(1)}, f32[8,256,128]{2,1,0:T(8,128)S(1)}) custom-call(f32[8,256,128]{2,1,0:T(8,128)S(1)} %get-tuple-element.26.ax, f32[8,256,128]{2,1,0:T(8,128)S(1)} %get-tuple-element.27.ay, f32[8,256,128]{2,1,0:T(8,128)S(1)} %get-tuple-element.28.psx.refs_1_, f32[8,256,128]{2,1,0:T(8,128)S(1)} %get-tuple-element.29.psy.refs_2_, ...), custom_call_target="tpu_custom_call" | custom-call | flops 1000 | bytes 9000000 | tf_op jit(solution)/shard_map/adjoint_products/pallas_call | solution.py:557
  25.2 2.8 %collective-permute-done.3.m3 = f32[12,8,256]{2,1,0:T(8,128)S(1)} collective-permute-done((f32[12,8,256]{2,1,0:T(8,128)S(1)}, f32[12,8,256]{2,1,0:T(8,128)S(1)}, u32[]{:S(2)}, u32[]{:S(2)}) %collective-permute-start.3) | collective-permute-done | bytes 98336 | tf_op jit(solution)/shard_map/ppermute | solution.py:494
  28.1 3.1 %collective-permute-start.4 = (f32[12,8,256]{2,1,0:T(8,128)S(1)}, f32[12,8,256]{2,1,0:T(8,128)S(1)}, u32[]{:S(2)}, u32[]{:S(2)}) collective-permute-start(f32[12,8,256]{2,1,0:T(8,128)S(1)} %group.1.after.n0), channel_id=1, source_target_pairs={{1,9},{3,11},{5,13},{7,15},{9,1},{11,3},{13,5},{15,7},{17,25},{19,... | collective-permute-start | bytes 294920 | tf_op jit(solution)/shard_map/ppermute | solution.py:494
  31.3 4.4 %collective-permute-start.5 = (f32[12,8,256]{2,1,0:T(8,128)S(1)}, f32[12,8,256]{2,1,0:T(8,128)S(1)}, u32[]{:S(2)}, u32[]{:S(2)}) collective-permute-start(f32[12,8,256]{2,1,0:T(8,128)S(1)} %group.1.after.n0), channel_id=1, source_target_pairs={{1,17},{3,19},{5,21},{7,23},{9,25},{11,27},{13,29},{15,31},{17,1},... | collective-permute-start | bytes 294920 | tf_op jit(solution)/shard_map/ppermute | solution.py:494
  35.6 2.1 %collective-permute-start.6 = (f32[12,8,256]{2,1,0:T(8,128)S(1)}, f32[12,8,256]{2,1,0:T(8,128)S(1)}, u32[]{:S(2)}, u32[]{:S(2)}) collective-permute-start(f32[12,8,256]{2,1,0:T(8,128)S(1)} %group.1.after.n0), channel_id=1, source_target_pairs={{1,25},{3,27},{5,29},{7,31},{9,17},{11,19},{13,21},{15,23},{17,9},... | collective-permute-start | bytes 294920 | tf_op jit(solution)/shard_map/ppermute | solution.py:494
  37.7 2.3 %primal_products.1 = (f32[8,256,128]{2,1,0:T(8,128)S(1)}, f32[8,256,128]{2,1,0:T(8,128)S(1)}, f32[8,256,128]{2,1,0:T(8,128)S(1)}) custom-call(f32[8,256,128]{2,1,0:T(8,128)S(1)} %get-tuple-element.23.rx, f32[8,256,128]{2,1,0:T(8,128)S(1)} %get-tuple-element.24.ry, f32[3,8,256,128]{3,2,1,0:T(8,128)S(1)} %get-tuple-element.25.h, ...), custom_call_target="tpu_custom_call" | custom-call | flops 1000 | bytes 12000000 | tf_op jit(solution)/shard_map/primal_products/pallas_call | solution.py:564
  40.0 2.2 %collective-permute-done.6.n3 = f32[12,8,256]{2,1,0:T(8,128)S(1)} collective-permute-done((f32[12,8,256]{2,1,0:T(8,128)S(1)}, f32[12,8,256]{2,1,0:T(8,128)S(1)}, u32[]{:S(2)}, u32[]{:S(2)}) %collective-permute-start.6) | collective-permute-done | bytes 98336 | tf_op jit(solution)/shard_map/ppermute | solution.py:494
  42.5 1.3 %collective-permute-start.7 = (f32[12,8,256]{2,1,0:T(8,128)S(1)}, f32[12,8,256]{2,1,0:T(8,128)S(1)}, u32[]{:S(2)}, u32[]{:S(2)}) collective-permute-start(f32[12,8,256]{2,1,0:T(8,128)S(1)} %get-tuple-element.39), channel_id=1, source_target_pairs={{1,0},{3,2},{5,4},{7,6},{9,8},{11,10},{13,12},{15,14},{17,16},{19,... | collective-permute-start | bytes 294920 | tf_op jit(solution)/shard_map/ppermute | solution.py:499
  43.8 0.9 %collective-permute-done.7.recv.refs_6_ = f32[12,8,256]{2,1,0:T(8,128)S(1)} collective-permute-done((f32[12,8,256]{2,1,0:T(8,128)S(1)}, f32[12,8,256]{2,1,0:T(8,128)S(1)}, u32[]{:S(2)}, u32[]{:S(2)}) %collective-permute-start.7) | collective-permute-done | bytes 98336 | tf_op jit(solution)/shard_map/ppermute | solution.py:499
  45.2 3.0 %collective-permute-start.8 = (f32[2,256,128]{2,1,0:T(8,128)S(1)}, f32[2,256,128]{2,1,0:T(8,128)S(1)}, u32[]{:S(2)}, u32[]{:S(2)}) collective-permute-start(f32[2,256,128]{2,1,0:T(8,128)S(1)} %gradient_2.1), channel_id=1, source_target_pairs={{0,64},{32,96},{64,0},{96,32},{1,65},{33,97},{65,1},{97,33},{2,66}... | collective-permute-start | bytes 786440 | tf_op jit(solution)/shard_map/ppermute | solution.py:490
  48.7 0.5 collective-permute-start.9
  50.5 3.8 %collective-permute-done.8 = f32[2,256,128]{2,1,0:T(8,128)S(1)} collective-permute-done((f32[2,256,128]{2,1,0:T(8,128)S(1)}, f32[2,256,128]{2,1,0:T(8,128)S(1)}, u32[]{:S(2)}, u32[]{:S(2)}) %collective-permute-start.8) | collective-permute-done | bytes 262176 | tf_op jit(solution)/shard_map/ppermute | solution.py:490
  54.3 6.0 %collective-permute-done.9 = f32[2,256,128]{2,1,0:T(8,128)S(1)} collective-permute-done((f32[2,256,128]{2,1,0:T(8,128)S(1)}, f32[2,256,128]{2,1,0:T(8,128)S(1)}, u32[]{:S(2)}, u32[]{:S(2)}) %collective-permute-start.9) | collective-permute-done | bytes 262176 | tf_op jit(solution)/shard_map/ppermute | solution.py:490
  60.5 3.2 %collective-permute-start.11 = (f32[2,256,128]{2,1,0:T(8,128)S(1)}, f32[2,256,128]{2,1,0:T(8,128)S(1)}, u32[]{:S(2)}, u32[]{:S(2)}) collective-permute-start(f32[2,256,128]{2,1,0:T(8,128)S(1)} %add_add_fusion.g0), channel_id=1, source_target_pairs={{0,64},{32,96},{64,0},{96,32},{1,65},{33,97},{65,1},{97,33},{2,66}... | collective-permute-start | bytes 786440 | tf_op jit(solution)/shard_map/ppermute | solution.py:490
  64.5 3.4 %outputs.1 = (f32[3,8,256,128]{3,2,1,0:T(8,128)}, f32[3,8,256,128]{3,2,1,0:T(8,128)}) custom-call(f32[8,256,128]{2,1,0:T(8,128)S(1)} %get-tuple-element.35.after.ex, f32[8,256,128]{2,1,0:T(8,128)S(1)} %get-tuple-element.36.ey, f32[3,8,256,128]{3,2,1,0:T(8,128)S(1)} %get-tuple-element.25.h, f32[8,256,128]{2,1,0:T(8,128)S(1)} %get-tuple-element.32.ez, ...), custom_call_target="tpu_custom_call" | custom-call | flops 1000 | bytes 18000000 | tf_op jit(solution)/shard_map/outputs/pallas_call | solution.py:581
  67.9 1.2 %collective-permute-done.11.g2 = f32[2,256,128]{2,1,0:T(8,128)S(1)} collective-permute-done((f32[2,256,128]{2,1,0:T(8,128)S(1)}, f32[2,256,128]{2,1,0:T(8,128)S(1)}, u32[]{:S(2)}, u32[]{:S(2)}) %collective-permute-start.11) | collective-permute-done | bytes 262176 | tf_op jit(solution)/shard_map/ppermute | solution.py:490
  69.1 6.6 %collective-permute-done.12.g1 = f32[2,256,128]{2,1,0:T(8,128)S(1)} collective-permute-done((f32[2,256,128]{2,1,0:T(8,128)S(1)}, f32[2,256,128]{2,1,0:T(8,128)S(1)}, u32[]{:S(2)}, u32[]{:S(2)}) %collective-permute-start.12) | collective-permute-done | bytes 262176 | tf_op jit(solution)/shard_map/ppermute | solution.py:490
  76.0 1.0 %place.1 = f32[8,256,128]{2,1,0:T(8,128)} custom-call(f32[2,256,128]{2,1,0:T(8,128)S(1)} %collective-permute-done.11.g2, f32[2,256,128]{2,1,0:T(8,128)S(1)} %collective-permute-done.12.g1, f32[2,256,128]{2,1,0:T(8,128)S(1)} %collective-permute-done.13.g3, f32[2,256,128]{2,1,0:T(8,128)S(1)} %add_add_fusion.g0), custom_call_target="tpu_custom_call" | custom-call | flops 1000 | bytes 3000000 | tf_op jit(solution)/shard_map/place/pallas_call | solution.py:589
  (17 shorter events, 4.0 us)
Async XLA Ops:
  8.6 3.5 %collective-permute-start = (f32[12,8,256]{2,1,0:T(8,128)S(1)}, f32[12,8,256]{2,1,0:T(8,128)S(1)}, u32[]{:S(2)}, u32[]{:S(2)}) collective-permute-start(f32[12,8,256]{2,1,0:T(8,128)S(1)} %get-tuple-element.31.own.a0), channel_id=1, source_target_pairs={{0,1},{2,3},{4,5},{6,7},{8,9},{10,11},{12,13},{14,15},{16,17},{18,... | collective-permute-start | bytes 294920 | tf_op jit(solution)/shard_map/ppermute | solution.py:499
  12.1 13.1 %collective-permute-start.1 = (f32[12,8,256]{2,1,0:T(8,128)S(1)}, f32[12,8,256]{2,1,0:T(8,128)S(1)}, u32[]{:S(2)}, u32[]{:S(2)}) collective-permute-start(f32[12,8,256]{2,1,0:T(8,128)S(1)} %chip.1.after.m0), channel_id=1, source_target_pairs={{1,3},{3,1},{5,7},{7,5},{9,11},{11,9},{13,15},{15,13},{17,19},{19,... | collective-permute-start | bytes 294920 | tf_op jit(solution)/shard_map/ppermute | solution.py:494
  16.2 9.0 %collective-permute-start.2 = (f32[12,8,256]{2,1,0:T(8,128)S(1)}, f32[12,8,256]{2,1,0:T(8,128)S(1)}, u32[]{:S(2)}, u32[]{:S(2)}) collective-permute-start(f32[12,8,256]{2,1,0:T(8,128)S(1)} %chip.1.after.m0), channel_id=1, source_target_pairs={{1,5},{3,7},{5,1},{7,3},{9,13},{11,15},{13,9},{15,11},{17,21},{19,... | collective-permute-start | bytes 294920 | tf_op jit(solution)/shard_map/ppermute | solution.py:494
  21.4 6.6 %collective-permute-start.3 = (f32[12,8,256]{2,1,0:T(8,128)S(1)}, f32[12,8,256]{2,1,0:T(8,128)S(1)}, u32[]{:S(2)}, u32[]{:S(2)}) collective-permute-start(f32[12,8,256]{2,1,0:T(8,128)S(1)} %chip.1.after.m0), channel_id=1, source_target_pairs={{1,7},{3,5},{5,3},{7,1},{9,15},{11,13},{13,11},{15,9},{17,23},{19,... | collective-permute-start | bytes 294920 | tf_op jit(solution)/shard_map/ppermute | solution.py:494
  28.1 11.9 %collective-permute-start.4 = (f32[12,8,256]{2,1,0:T(8,128)S(1)}, f32[12,8,256]{2,1,0:T(8,128)S(1)}, u32[]{:S(2)}, u32[]{:S(2)}) collective-permute-start(f32[12,8,256]{2,1,0:T(8,128)S(1)} %group.1.after.n0), channel_id=1, source_target_pairs={{1,9},{3,11},{5,13},{7,15},{9,1},{11,3},{13,5},{15,7},{17,25},{19,... | collective-permute-start | bytes 294920 | tf_op jit(solution)/shard_map/ppermute | solution.py:494
  31.3 8.8 %collective-permute-start.5 = (f32[12,8,256]{2,1,0:T(8,128)S(1)}, f32[12,8,256]{2,1,0:T(8,128)S(1)}, u32[]{:S(2)}, u32[]{:S(2)}) collective-permute-start(f32[12,8,256]{2,1,0:T(8,128)S(1)} %group.1.after.n0), channel_id=1, source_target_pairs={{1,17},{3,19},{5,21},{7,23},{9,25},{11,27},{13,29},{15,31},{17,1},... | collective-permute-start | bytes 294920 | tf_op jit(solution)/shard_map/ppermute | solution.py:494
  35.6 6.6 %collective-permute-start.6 = (f32[12,8,256]{2,1,0:T(8,128)S(1)}, f32[12,8,256]{2,1,0:T(8,128)S(1)}, u32[]{:S(2)}, u32[]{:S(2)}) collective-permute-start(f32[12,8,256]{2,1,0:T(8,128)S(1)} %group.1.after.n0), channel_id=1, source_target_pairs={{1,25},{3,27},{5,29},{7,31},{9,17},{11,19},{13,21},{15,23},{17,9},... | collective-permute-start | bytes 294920 | tf_op jit(solution)/shard_map/ppermute | solution.py:494
  42.5 2.2 %collective-permute-start.7 = (f32[12,8,256]{2,1,0:T(8,128)S(1)}, f32[12,8,256]{2,1,0:T(8,128)S(1)}, u32[]{:S(2)}, u32[]{:S(2)}) collective-permute-start(f32[12,8,256]{2,1,0:T(8,128)S(1)} %get-tuple-element.39), channel_id=1, source_target_pairs={{1,0},{3,2},{5,4},{7,6},{9,8},{11,10},{13,12},{15,14},{17,16},{19,... | collective-permute-start | bytes 294920 | tf_op jit(solution)/shard_map/ppermute | solution.py:499
  45.2 9.1 %collective-permute-start.8 = (f32[2,256,128]{2,1,0:T(8,128)S(1)}, f32[2,256,128]{2,1,0:T(8,128)S(1)}, u32[]{:S(2)}, u32[]{:S(2)}) collective-permute-start(f32[2,256,128]{2,1,0:T(8,128)S(1)} %gradient_2.1), channel_id=1, source_target_pairs={{0,64},{32,96},{64,0},{96,32},{1,65},{33,97},{65,1},{97,33},{2,66}... | collective-permute-start | bytes 786440 | tf_op jit(solution)/shard_map/ppermute | solution.py:490
  48.7 11.7 %collective-permute-start.9 = (f32[2,256,128]{2,1,0:T(8,128)S(1)}, f32[2,256,128]{2,1,0:T(8,128)S(1)}, u32[]{:S(2)}, u32[]{:S(2)}) collective-permute-start(f32[2,256,128]{2,1,0:T(8,128)S(1)} %gradient_1.1), channel_id=1, source_target_pairs={{0,32},{32,0},{64,96},{96,64},{1,33},{33,1},{65,97},{97,65},{2,34}... | collective-permute-start | bytes 786440 | tf_op jit(solution)/shard_map/ppermute | solution.py:490
  49.6 10.8 %collective-permute-start.10 = (f32[2,256,128]{2,1,0:T(8,128)S(1)}, f32[2,256,128]{2,1,0:T(8,128)S(1)}, u32[]{:S(2)}, u32[]{:S(2)}) collective-permute-start(f32[2,256,128]{2,1,0:T(8,128)S(1)} %gradient_3.1), channel_id=1, source_target_pairs={{0,96},{32,64},{64,32},{96,0},{1,97},{33,65},{65,33},{97,1},{2,98}... | collective-permute-start | bytes 786440 | tf_op jit(solution)/shard_map/ppermute | solution.py:490
  60.5 8.6 %collective-permute-start.11 = (f32[2,256,128]{2,1,0:T(8,128)S(1)}, f32[2,256,128]{2,1,0:T(8,128)S(1)}, u32[]{:S(2)}, u32[]{:S(2)}) collective-permute-start(f32[2,256,128]{2,1,0:T(8,128)S(1)} %add_add_fusion.g0), channel_id=1, source_target_pairs={{0,64},{32,96},{64,0},{96,32},{1,65},{33,97},{65,1},{97,33},{2,66}... | collective-permute-start | bytes 786440 | tf_op jit(solution)/shard_map/ppermute | solution.py:490
  63.7 12.0 %collective-permute-start.12 = (f32[2,256,128]{2,1,0:T(8,128)S(1)}, f32[2,256,128]{2,1,0:T(8,128)S(1)}, u32[]{:S(2)}, u32[]{:S(2)}) collective-permute-start(f32[2,256,128]{2,1,0:T(8,128)S(1)} %add_add_fusion.g0), channel_id=1, source_target_pairs={{0,32},{32,0},{64,96},{96,64},{1,33},{33,1},{65,97},{97,65},{2,34}... | collective-permute-start | bytes 786440 | tf_op jit(solution)/shard_map/ppermute | solution.py:490
  64.1 11.9 %collective-permute-start.13 = (f32[2,256,128]{2,1,0:T(8,128)S(1)}, f32[2,256,128]{2,1,0:T(8,128)S(1)}, u32[]{:S(2)}, u32[]{:S(2)}) collective-permute-start(f32[2,256,128]{2,1,0:T(8,128)S(1)} %add_add_fusion.g0), channel_id=1, source_target_pairs={{0,96},{32,64},{64,32},{96,0},{1,97},{33,65},{65,33},{97,1},{2,98}... | collective-permute-start | bytes 786440 | tf_op jit(solution)/shard_map/ppermute | solution.py:490

commit v7 on v6

--- a/solution.py
+++ b/solution.py
@@ -491,12 +491,8 @@
 
 
 def among_second(block, mask):
-    return lax.ppermute(block, "gz", [(i, i ^ mask) for i in range(1, lax.axis_size("gz"), 2)])
-
-
-def across_chip(block, source):
-    chips = range(0, lax.axis_size("gz"), 2)
-    return lax.ppermute(block, "gz", [(i + source, i + 1 - source) for i in chips])
+    pairs = [(i, i ^ mask if i % 2 else i) for i in range(lax.axis_size("gz"))]
+    return lax.ppermute(block, "gz", pairs)
 
 
 SMEM = pl.BlockSpec(memory_space=pltpu.SMEM)
@@ -550,7 +546,7 @@
         ],
     )(angle_index, *map(in_hbm, (region_eps, e, h, ge, gh, labels, profiles, zs, lt, block_inverse)))
 
-    other = across_chip(mine, 0)
+    other = swap(mine, "gz", 1)
     (m0,) = call(chip_kernel, "chip", [VMEM] * 2, [message], 0.5, 4)(mine, other)
     m1, m2, m3 = (among_second(m0, 2 * k) for k in (1, 2, 3))
 
@@ -567,7 +563,7 @@
     own_edges, send_edges = call(
         back_kernel, "back", [VMEM] * 10 + [ANY], [shape(12, 8, Y)] * 2, 0.5, 4
     )(mine, other, m0, m1, m2, m3, n0, n1, n2, n3, ex)
-    other_edges = across_chip(send_edges, 1)
+    other_edges = swap(send_edges, "gz", 1)
 
     def gradient(k):
         return call(

time: 77.3 us -> 75 us (0.970)
  starting transfers between devices: 31.3 us -> 29.7 us
    ppermute x8 -> x6, waiting for transfers between devices: 8.06 us -> 4.95 us  [among_second(): return lax.ppermute(block, 'gz', pairs)]
    ppermute x8 -> x6, starting transfers between devices: 23.4 us -> 20.3 us  [among_second(): return lax.ppermute(block, 'gz', pairs)]
    ppermute x6 -> x8, waiting for transfers between devices: 17.9 us -> 20.4 us  [swap(): lax.ppermute(block, axis, [(i, i ^ mask) for i in range(lax.axis_size(axi...]
    ppermute x6 -> x8, starting transfers between devices: 7.95 us -> 9.33 us  [swap(): lax.ppermute(block, axis, [(i, i ^ mask) for i in range(lax.axis_size(axi...]
where the time goes in v7:
time: 75 us; the launch traced here: 74.7 us
  starting transfers between devices  29.7 us (40%)
  waiting for transfers between devices  25.4 us (34%)
  Pallas kernels  18.1 us (24%)
  between operations  1.45 us (2%)
    ppermute x8, waiting for transfers between devices, swap(): lax.ppermute(block, axis, [(i, i ^ mask) for i in range(lax.axis_size(axi...  20.4 us
    ppermute x6, starting transfers between devices, among_second(): return lax.ppermute(block, 'gz', pairs)  20.3 us
    ppermute x8, starting transfers between devices, swap(): lax.ppermute(block, axis, [(i, i ^ mask) for i in range(lax.axis_size(axi...  9.33 us
    pallas_call x1, Pallas kernels, body(): call(rhs_kernel, 'right_hand_sides', [SMEM, SMEM] + [HBM] * 9, [slab] * 8...  7.3 us
    ppermute x6, waiting for transfers between devices, among_second(): return lax.ppermute(block, 'gz', pairs)  4.95 us
    pallas_call x1, Pallas kernels, body(): call(output_kernel, 'outputs', [VMEM] * 8, [shape(3, X, Y, CZ)] * 2, 6, 1...  3.41 us
    pallas_call x1, Pallas kernels, body(): call(primal_kernel, 'primal_products', [VMEM] * 7 + [ANY], [slab] * 3, 4, 8)  2.26 us
    pallas_call x1, Pallas kernels, body(): call(adjoint_kernel, 'adjoint_products', [VMEM] * 5 + [HBM, ANY], [slab]...  1.85 us
  transfers between devices with their start and end apart: 14, of which 10 were waited for; matrix products, arithmetic and copies ran while one was open for 0% of the time, Pallas kernels for 12%

profile of v7, /device:TPU:1, one launch (start us, length us, event | category | flops | bytes accessed | tf_op | source)
XLA Modules:
  0.0 74.7 jit_solution(11881222464430539885)
XLA Ops:
  1.3 7.3 %right_hand_sides.1 = (f32[8,256,128]{2,1,0:T(8,128)S(1)}, f32[8,256,128]{2,1,0:T(8,128)S(1)}, f32[8,256,128]{2,1,0:T(8,128)S(1)}, f32[8,256,128]{2,1,0:T(8,128)...) custom-call(s32[1]{0:T(128)S(6)} %copy.14.angle, ...), custom_call_target="tpu_custom_call" | custom-call | flops 1000 | bytes 18000000 | tf_op jit(solution)/shard_map/right_hand_sides/pallas_call | solution.py:537
  8.6 1.5 %collective-permute-start = (f32[12,8,256]{2,1,0:T(8,128)S(1)}, f32[12,8,256]{2,1,0:T(8,128)S(1)}, u32[]{:S(2)}, u32[]{:S(2)}) collective-permute-start(f32[12,8,256]{2,1,0:T(8,128)S(1)} %get-tuple-element.31.own.a0), channel_id=1, source_target_pairs={{0,1},{1,0},{2,3},{3,2},{4,5},{5,4},{6,7},{7,6},{8,9},{9,8},{10,11... | collective-permute-start | bytes 294920 | tf_op jit(solution)/shard_map/ppermute | solution.py:490
  10.1 0.9 %collective-permute-done.other.a1 = f32[12,8,256]{2,1,0:T(8,128)S(1)} collective-permute-done((f32[12,8,256]{2,1,0:T(8,128)S(1)}, f32[12,8,256]{2,1,0:T(8,128)S(1)}, u32[]{:S(2)}, u32[]{:S(2)}) %collective-permute-start) | collective-permute-done | bytes 98336 | tf_op jit(solution)/shard_map/ppermute | solution.py:490
  11.1 3.6 %collective-permute-start.1 = (f32[12,8,256]{2,1,0:T(8,128)S(1)}, f32[12,8,256]{2,1,0:T(8,128)S(1)}, u32[]{:S(2)}, u32[]{:S(2)}) collective-permute-start(f32[12,8,256]{2,1,0:T(8,128)S(1)} %chip.1.after.m0), channel_id=1, source_target_pairs={{0,0},{1,3},{2,2},{3,1},{4,4},{5,7},{6,6},{7,5},{8,8},{9,11},{10,1... | collective-permute-start | bytes 294920 | tf_op jit(solution)/shard_map/ppermute | solution.py:495
  14.7 5.2 %collective-permute-start.2 = (f32[12,8,256]{2,1,0:T(8,128)S(1)}, f32[12,8,256]{2,1,0:T(8,128)S(1)}, u32[]{:S(2)}, u32[]{:S(2)}) collective-permute-start(f32[12,8,256]{2,1,0:T(8,128)S(1)} %chip.1.after.m0), channel_id=1, source_target_pairs={{0,0},{1,5},{2,2},{3,7},{4,4},{5,1},{6,6},{7,3},{8,8},{9,13},{10,1... | collective-permute-start | bytes 294920 | tf_op jit(solution)/shard_map/ppermute | solution.py:495
  19.9 1.9 %collective-permute-start.3 = (f32[12,8,256]{2,1,0:T(8,128)S(1)}, f32[12,8,256]{2,1,0:T(8,128)S(1)}, u32[]{:S(2)}, u32[]{:S(2)}) collective-permute-start(f32[12,8,256]{2,1,0:T(8,128)S(1)} %chip.1.after.m0), channel_id=1, source_target_pairs={{0,0},{1,7},{2,2},{3,5},{4,4},{5,3},{6,6},{7,1},{8,8},{9,15},{10,1... | collective-permute-start | bytes 294920 | tf_op jit(solution)/shard_map/ppermute | solution.py:495
  21.9 1.9 %adjoint_products.1 = (f32[8,256,128]{2,1,0:T(8,128)S(1)}, f32[8,256,128]{2,1,0:T(8,128)S(1)}) custom-call(f32[8,256,128]{2,1,0:T(8,128)S(1)} %get-tuple-element.26.ax, f32[8,256,128]{2,1,0:T(8,128)S(1)} %get-tuple-element.27.ay, f32[8,256,128]{2,1,0:T(8,128)S(1)} %get-tuple-element.28.psx.refs_1_, f32[8,256,128]{2,1,0:T(8,128)S(1)} %get-tuple-element.29.psy.refs_2_, ...), custom_call_target="tpu_custom_call" | custom-call | flops 1000 | bytes 9000000 | tf_op jit(solution)/shard_map/adjoint_products/pallas_call | solution.py:553
  23.7 2.8 %collective-permute-done.3.m3 = f32[12,8,256]{2,1,0:T(8,128)S(1)} collective-permute-done((f32[12,8,256]{2,1,0:T(8,128)S(1)}, f32[12,8,256]{2,1,0:T(8,128)S(1)}, u32[]{:S(2)}, u32[]{:S(2)}) %collective-permute-start.3) | collective-permute-done | bytes 98336 | tf_op jit(solution)/shard_map/ppermute | solution.py:495
  26.6 3.1 %collective-permute-start.4 = (f32[12,8,256]{2,1,0:T(8,128)S(1)}, f32[12,8,256]{2,1,0:T(8,128)S(1)}, u32[]{:S(2)}, u32[]{:S(2)}) collective-permute-start(f32[12,8,256]{2,1,0:T(8,128)S(1)} %group.1.after.n0), channel_id=1, source_target_pairs={{0,0},{1,9},{2,2},{3,11},{4,4},{5,13},{6,6},{7,15},{8,8},{9,1},{10... | collective-permute-start | bytes 294920 | tf_op jit(solution)/shard_map/ppermute | solution.py:495
  29.8 4.4 %collective-permute-start.5 = (f32[12,8,256]{2,1,0:T(8,128)S(1)}, f32[12,8,256]{2,1,0:T(8,128)S(1)}, u32[]{:S(2)}, u32[]{:S(2)}) collective-permute-start(f32[12,8,256]{2,1,0:T(8,128)S(1)} %group.1.after.n0), channel_id=1, source_target_pairs={{0,0},{1,17},{2,2},{3,19},{4,4},{5,21},{6,6},{7,23},{8,8},{9,25},{... | collective-permute-start | bytes 294920 | tf_op jit(solution)/shard_map/ppermute | solution.py:495
  34.1 2.1 %collective-permute-start.6 = (f32[12,8,256]{2,1,0:T(8,128)S(1)}, f32[12,8,256]{2,1,0:T(8,128)S(1)}, u32[]{:S(2)}, u32[]{:S(2)}) collective-permute-start(f32[12,8,256]{2,1,0:T(8,128)S(1)} %group.1.after.n0), channel_id=1, source_target_pairs={{0,0},{1,25},{2,2},{3,27},{4,4},{5,29},{6,6},{7,31},{8,8},{9,17},{... | collective-permute-start | bytes 294920 | tf_op jit(solution)/shard_map/ppermute | solution.py:495
  36.2 2.3 %primal_products.1 = (f32[8,256,128]{2,1,0:T(8,128)S(1)}, f32[8,256,128]{2,1,0:T(8,128)S(1)}, f32[8,256,128]{2,1,0:T(8,128)S(1)}) custom-call(f32[8,256,128]{2,1,0:T(8,128)S(1)} %get-tuple-element.23.rx, f32[8,256,128]{2,1,0:T(8,128)S(1)} %get-tuple-element.24.ry, f32[3,8,256,128]{3,2,1,0:T(8,128)S(1)} %get-tuple-element.25.h, ...), custom_call_target="tpu_custom_call" | custom-call | flops 1000 | bytes 12000000 | tf_op jit(solution)/shard_map/primal_products/pallas_call | solution.py:560
  38.5 2.2 %collective-permute-done.6.n3 = f32[12,8,256]{2,1,0:T(8,128)S(1)} collective-permute-done((f32[12,8,256]{2,1,0:T(8,128)S(1)}, f32[12,8,256]{2,1,0:T(8,128)S(1)}, u32[]{:S(2)}, u32[]{:S(2)}) %collective-permute-start.6) | collective-permute-done | bytes 98336 | tf_op jit(solution)/shard_map/ppermute | solution.py:495
  41.1 1.3 %collective-permute-done.7.recv.refs_6_ = f32[12,8,256]{2,1,0:T(8,128)S(1)} collective-permute-done((f32[12,8,256]{2,1,0:T(8,128)S(1)}, f32[12,8,256]{2,1,0:T(8,128)S(1)}, u32[]{:S(2)}, u32[]{:S(2)}) %collective-permute-start.7) | collective-permute-done | bytes 98336 | tf_op jit(solution)/shard_map/ppermute | solution.py:490
  42.9 3.0 %collective-permute-start.8 = (f32[2,256,128]{2,1,0:T(8,128)S(1)}, f32[2,256,128]{2,1,0:T(8,128)S(1)}, u32[]{:S(2)}, u32[]{:S(2)}) collective-permute-start(f32[2,256,128]{2,1,0:T(8,128)S(1)} %gradient_2.1), channel_id=1, source_target_pairs={{0,64},{32,96},{64,0},{96,32},{1,65},{33,97},{65,1},{97,33},{2,66}... | collective-permute-start | bytes 786440 | tf_op jit(solution)/shard_map/ppermute | solution.py:490
  46.3 0.5 collective-permute-start.9
  47.3 0.5 collective-permute-start.10
  48.2 4.0 %collective-permute-done.8 = f32[2,256,128]{2,1,0:T(8,128)S(1)} collective-permute-done((f32[2,256,128]{2,1,0:T(8,128)S(1)}, f32[2,256,128]{2,1,0:T(8,128)S(1)}, u32[]{:S(2)}, u32[]{:S(2)}) %collective-permute-start.8) | collective-permute-done | bytes 262176 | tf_op jit(solution)/shard_map/ppermute | solution.py:490
  52.2 6.0 %collective-permute-done.9 = f32[2,256,128]{2,1,0:T(8,128)S(1)} collective-permute-done((f32[2,256,128]{2,1,0:T(8,128)S(1)}, f32[2,256,128]{2,1,0:T(8,128)S(1)}, u32[]{:S(2)}, u32[]{:S(2)}) %collective-permute-start.9) | collective-permute-done | bytes 262176 | tf_op jit(solution)/shard_map/ppermute | solution.py:490
  58.3 3.0 %collective-permute-start.11 = (f32[2,256,128]{2,1,0:T(8,128)S(1)}, f32[2,256,128]{2,1,0:T(8,128)S(1)}, u32[]{:S(2)}, u32[]{:S(2)}) collective-permute-start(f32[2,256,128]{2,1,0:T(8,128)S(1)} %add_add_fusion.g0), channel_id=1, source_target_pairs={{0,64},{32,96},{64,0},{96,32},{1,65},{33,97},{65,1},{97,33},{2,66}... | collective-permute-start | bytes 786440 | tf_op jit(solution)/shard_map/ppermute | solution.py:490
  62.1 3.4 %outputs.1 = (f32[3,8,256,128]{3,2,1,0:T(8,128)}, f32[3,8,256,128]{3,2,1,0:T(8,128)}) custom-call(f32[8,256,128]{2,1,0:T(8,128)S(1)} %get-tuple-element.35.after.ex, f32[8,256,128]{2,1,0:T(8,128)S(1)} %get-tuple-element.36.ey, f32[3,8,256,128]{3,2,1,0:T(8,128)S(1)} %get-tuple-element.25.h, f32[8,256,128]{2,1,0:T(8,128)S(1)} %get-tuple-element.32.ez, ...), custom_call_target="tpu_custom_call" | custom-call | flops 1000 | bytes 18000000 | tf_op jit(solution)/shard_map/outputs/pallas_call | solution.py:577
  65.5 1.3 %collective-permute-done.11.g2 = f32[2,256,128]{2,1,0:T(8,128)S(1)} collective-permute-done((f32[2,256,128]{2,1,0:T(8,128)S(1)}, f32[2,256,128]{2,1,0:T(8,128)S(1)}, u32[]{:S(2)}, u32[]{:S(2)}) %collective-permute-start.11) | collective-permute-done | bytes 262176 | tf_op jit(solution)/shard_map/ppermute | solution.py:490
  66.8 6.5 %collective-permute-done.12.g1 = f32[2,256,128]{2,1,0:T(8,128)S(1)} collective-permute-done((f32[2,256,128]{2,1,0:T(8,128)S(1)}, f32[2,256,128]{2,1,0:T(8,128)S(1)}, u32[]{:S(2)}, u32[]{:S(2)}) %collective-permute-start.12) | collective-permute-done | bytes 262176 | tf_op jit(solution)/shard_map/ppermute | solution.py:490
  73.7 1.0 %place.1 = f32[8,256,128]{2,1,0:T(8,128)} custom-call(f32[2,256,128]{2,1,0:T(8,128)S(1)} %collective-permute-done.11.g2, f32[2,256,128]{2,1,0:T(8,128)S(1)} %collective-permute-done.12.g1, f32[2,256,128]{2,1,0:T(8,128)S(1)} %collective-permute-done.13.g3, f32[2,256,128]{2,1,0:T(8,128)S(1)} %add_add_fusion.g0), custom_call_target="tpu_custom_call" | custom-call | flops 1000 | bytes 3000000 | tf_op jit(solution)/shard_map/place/pallas_call | solution.py:585
  (17 shorter events, 3.6 us)
Async XLA Ops:
  8.6 2.4 %collective-permute-start = (f32[12,8,256]{2,1,0:T(8,128)S(1)}, f32[12,8,256]{2,1,0:T(8,128)S(1)}, u32[]{:S(2)}, u32[]{:S(2)}) collective-permute-start(f32[12,8,256]{2,1,0:T(8,128)S(1)} %get-tuple-element.31.own.a0), channel_id=1, source_target_pairs={{0,1},{1,0},{2,3},{3,2},{4,5},{5,4},{6,7},{7,6},{8,9},{9,8},{10,11... | collective-permute-start | bytes 294920 | tf_op jit(solution)/shard_map/ppermute | solution.py:490
  11.1 12.6 %collective-permute-start.1 = (f32[12,8,256]{2,1,0:T(8,128)S(1)}, f32[12,8,256]{2,1,0:T(8,128)S(1)}, u32[]{:S(2)}, u32[]{:S(2)}) collective-permute-start(f32[12,8,256]{2,1,0:T(8,128)S(1)} %chip.1.after.m0), channel_id=1, source_target_pairs={{0,0},{1,3},{2,2},{3,1},{4,4},{5,7},{6,6},{7,5},{8,8},{9,11},{10,1... | collective-permute-start | bytes 294920 | tf_op jit(solution)/shard_map/ppermute | solution.py:495
  14.7 9.0 %collective-permute-start.2 = (f32[12,8,256]{2,1,0:T(8,128)S(1)}, f32[12,8,256]{2,1,0:T(8,128)S(1)}, u32[]{:S(2)}, u32[]{:S(2)}) collective-permute-start(f32[12,8,256]{2,1,0:T(8,128)S(1)} %chip.1.after.m0), channel_id=1, source_target_pairs={{0,0},{1,5},{2,2},{3,7},{4,4},{5,1},{6,6},{7,3},{8,8},{9,13},{10,1... | collective-permute-start | bytes 294920 | tf_op jit(solution)/shard_map/ppermute | solution.py:495
  19.9 6.6 %collective-permute-start.3 = (f32[12,8,256]{2,1,0:T(8,128)S(1)}, f32[12,8,256]{2,1,0:T(8,128)S(1)}, u32[]{:S(2)}, u32[]{:S(2)}) collective-permute-start(f32[12,8,256]{2,1,0:T(8,128)S(1)} %chip.1.after.m0), channel_id=1, source_target_pairs={{0,0},{1,7},{2,2},{3,5},{4,4},{5,3},{6,6},{7,1},{8,8},{9,15},{10,1... | collective-permute-start | bytes 294920 | tf_op jit(solution)/shard_map/ppermute | solution.py:495
  26.6 11.9 %collective-permute-start.4 = (f32[12,8,256]{2,1,0:T(8,128)S(1)}, f32[12,8,256]{2,1,0:T(8,128)S(1)}, u32[]{:S(2)}, u32[]{:S(2)}) collective-permute-start(f32[12,8,256]{2,1,0:T(8,128)S(1)} %group.1.after.n0), channel_id=1, source_target_pairs={{0,0},{1,9},{2,2},{3,11},{4,4},{5,13},{6,6},{7,15},{8,8},{9,1},{10... | collective-permute-start | bytes 294920 | tf_op jit(solution)/shard_map/ppermute | solution.py:495
  29.8 8.8 %collective-permute-start.5 = (f32[12,8,256]{2,1,0:T(8,128)S(1)}, f32[12,8,256]{2,1,0:T(8,128)S(1)}, u32[]{:S(2)}, u32[]{:S(2)}) collective-permute-start(f32[12,8,256]{2,1,0:T(8,128)S(1)} %group.1.after.n0), channel_id=1, source_target_pairs={{0,0},{1,17},{2,2},{3,19},{4,4},{5,21},{6,6},{7,23},{8,8},{9,25},{... | collective-permute-start | bytes 294920 | tf_op jit(solution)/shard_map/ppermute | solution.py:495
  34.1 6.6 %collective-permute-start.6 = (f32[12,8,256]{2,1,0:T(8,128)S(1)}, f32[12,8,256]{2,1,0:T(8,128)S(1)}, u32[]{:S(2)}, u32[]{:S(2)}) collective-permute-start(f32[12,8,256]{2,1,0:T(8,128)S(1)} %group.1.after.n0), channel_id=1, source_target_pairs={{0,0},{1,25},{2,2},{3,27},{4,4},{5,29},{6,6},{7,31},{8,8},{9,17},{... | collective-permute-start | bytes 294920 | tf_op jit(solution)/shard_map/ppermute | solution.py:495
  41.0 1.4 %collective-permute-start.7 = (f32[12,8,256]{2,1,0:T(8,128)S(1)}, f32[12,8,256]{2,1,0:T(8,128)S(1)}, u32[]{:S(2)}, u32[]{:S(2)}) collective-permute-start(f32[12,8,256]{2,1,0:T(8,128)S(1)} %get-tuple-element.39), channel_id=1, source_target_pairs={{0,1},{1,0},{2,3},{3,2},{4,5},{5,4},{6,7},{7,6},{8,9},{9,8},{10,11... | collective-permute-start | bytes 294920 | tf_op jit(solution)/shard_map/ppermute | solution.py:490
  42.9 9.3 %collective-permute-start.8 = (f32[2,256,128]{2,1,0:T(8,128)S(1)}, f32[2,256,128]{2,1,0:T(8,128)S(1)}, u32[]{:S(2)}, u32[]{:S(2)}) collective-permute-start(f32[2,256,128]{2,1,0:T(8,128)S(1)} %gradient_2.1), channel_id=1, source_target_pairs={{0,64},{32,96},{64,0},{96,32},{1,65},{33,97},{65,1},{97,33},{2,66}... | collective-permute-start | bytes 786440 | tf_op jit(solution)/shard_map/ppermute | solution.py:490
  46.3 11.9 %collective-permute-start.9 = (f32[2,256,128]{2,1,0:T(8,128)S(1)}, f32[2,256,128]{2,1,0:T(8,128)S(1)}, u32[]{:S(2)}, u32[]{:S(2)}) collective-permute-start(f32[2,256,128]{2,1,0:T(8,128)S(1)} %gradient_1.1), channel_id=1, source_target_pairs={{0,32},{32,0},{64,96},{96,64},{1,33},{33,1},{65,97},{97,65},{2,34}... | collective-permute-start | bytes 786440 | tf_op jit(solution)/shard_map/ppermute | solution.py:490
  47.3 11.0 %collective-permute-start.10 = (f32[2,256,128]{2,1,0:T(8,128)S(1)}, f32[2,256,128]{2,1,0:T(8,128)S(1)}, u32[]{:S(2)}, u32[]{:S(2)}) collective-permute-start(f32[2,256,128]{2,1,0:T(8,128)S(1)} %gradient_3.1), channel_id=1, source_target_pairs={{0,96},{32,64},{64,32},{96,0},{1,97},{33,65},{65,33},{97,1},{2,98}... | collective-permute-start | bytes 786440 | tf_op jit(solution)/shard_map/ppermute | solution.py:490
  58.3 8.5 %collective-permute-start.11 = (f32[2,256,128]{2,1,0:T(8,128)S(1)}, f32[2,256,128]{2,1,0:T(8,128)S(1)}, u32[]{:S(2)}, u32[]{:S(2)}) collective-permute-start(f32[2,256,128]{2,1,0:T(8,128)S(1)} %add_add_fusion.g0), channel_id=1, source_target_pairs={{0,64},{32,96},{64,0},{96,32},{1,65},{33,97},{65,1},{97,33},{2,66}... | collective-permute-start | bytes 786440 | tf_op jit(solution)/shard_map/ppermute | solution.py:490
  61.3 12.0 %collective-permute-start.12 = (f32[2,256,128]{2,1,0:T(8,128)S(1)}, f32[2,256,128]{2,1,0:T(8,128)S(1)}, u32[]{:S(2)}, u32[]{:S(2)}) collective-permute-start(f32[2,256,128]{2,1,0:T(8,128)S(1)} %add_add_fusion.g0), channel_id=1, source_target_pairs={{0,32},{32,0},{64,96},{96,64},{1,33},{33,1},{65,97},{97,65},{2,34}... | collective-permute-start | bytes 786440 | tf_op jit(solution)/shard_map/ppermute | solution.py:490
  61.7 11.9 %collective-permute-start.13 = (f32[2,256,128]{2,1,0:T(8,128)S(1)}, f32[2,256,128]{2,1,0:T(8,128)S(1)}, u32[]{:S(2)}, u32[]{:S(2)}) collective-permute-start(f32[2,256,128]{2,1,0:T(8,128)S(1)} %add_add_fusion.g0), channel_id=1, source_target_pairs={{0,96},{32,64},{64,32},{96,0},{1,97},{33,65},{65,33},{97,1},{2,98}... | collective-permute-start | bytes 786440 | tf_op jit(solution)/shard_map/ppermute | solution.py:490

commit v8 on v5

--- a/solution.py
+++ b/solution.py
@@ -308,12 +308,12 @@
     return first, order(high, pair, combine(*order(low, m2, m3)))
 
 
-def group_kernel(m0, m1, m2, m3, after, out):
+def group_kernel(m3, m2, m1, m0, after, out):
     _, low, high, _, _ = bits()
     repack(combine(*four(low, high, *(unpack(m) for m in (m0, m1, m2, m3)))[1]), out)
 
 
-def back_kernel(a0, a1, m0, m1, m2, m3, n0, n1, n2, n3, after, keep_o, send_o):
+def back_kernel(n3, n2, n1, n0, m3, m2, m1, m0, a0, a1, after, keep_o, send_o):
     core, zl, zh, xl, xh = bits()
     chip = order(core, unpack(a0), unpack(a1))
     m0, m1, m2, m3 = (unpack(m) for m in (m0, m1, m2, m3))
@@ -565,21 +565,21 @@
 
     other = swap(send, "gz", 1)
     (m0,) = call(chip_kernel, "chip", [VMEM] * 2, [message], 0.5, 4)(keep, other)
-    m1, m2, m3 = (swap(m0, "gz", 2 * k) for k in (1, 2, 3))
+    m3, m2, m1 = (swap(m0, "gz", 2 * k) for k in (3, 2, 1))
 
     adjoint, ez = call(
         adjoint_kernel, "adjoint_products", [VMEM] * 5 + [HBM, ANY], [slab] * 2, 3, 8,
         scratch=[pltpu.SemaphoreType.DMA],
     )(ax, ay, psx, psy, w, in_hbm(e), m0)
-    (n0,) = call(group_kernel, "group", [VMEM] * 4 + [ANY], [message], 0.5, 4)(m0, m1, m2, m3, adjoint)
-    n1, n2, n3 = (swap(n0, "gz", 8 * k) for k in (1, 2, 3))
+    (n0,) = call(group_kernel, "group", [VMEM] * 4 + [ANY], [message], 0.5, 4)(m3, m2, m1, m0, adjoint)
+    n3, n2, n1 = (swap(n0, "gz", 8 * k) for k in (3, 2, 1))
 
     ex, ey, grad = call(primal_kernel, "primal_products", [VMEM] * 7 + [ANY], [slab] * 3, 4, 8)(
         rx, ry, hv, ez, gs, adjoint, w, n0
     )
     own_edges, send_edges = call(
         back_kernel, "back", [VMEM] * 10 + [ANY], [shape(12, 8, CZ)] * 2, 0.5, 4
-    )(keep, other, m0, m1, m2, m3, n0, n1, n2, n3, ex)
+    )(n3, n2, n1, n0, m3, m2, m1, m0, keep, other, ex)
     other_edges = swap(send_edges, "gz", 1)
 
     def gradient(k):

time: 65.5 us -> 63.2 us (0.965)
  starting transfers between devices: 22.3 us -> 20.7 us
  waiting for transfers between devices: 23.7 us -> 23 us
    ppermute x14, starting transfers between devices: 22.3 us -> 20.7 us  [swap(): lax.ppermute(block, axis, [(i, i ^ mask) for i in range(lax.axis_size(axi...]
  transfers between devices with their start and end apart: 14 -> 14, of which waited for: 11 -> 10; matrix products, arithmetic and copies ran while one was open for 0% -> 0% of each run, Pallas kernels for 14% -> 14%
where the time goes in v8:
time: 63.2 us; the launch traced here: 63 us
  waiting for transfers between devices  23 us (36%)
  starting transfers between devices  20.7 us (33%)
  Pallas kernels  17.9 us (28%)
  between operations  1.38 us (2%)
    ppermute x14, waiting for transfers between devices, swap(): lax.ppermute(block, axis, [(i, i ^ mask) for i in range(lax.axis_size(axi...  23 us
    ppermute x14, starting transfers between devices, swap(): lax.ppermute(block, axis, [(i, i ^ mask) for i in range(lax.axis_size(axi...  20.7 us
    pallas_call x1, Pallas kernels, body(): call(rhs_kernel, 'right_hand_sides', [SMEM, SMEM] + [HBM] * 9, [slab] * 8...  7.31 us
    pallas_call x1, Pallas kernels, body(): call(output_kernel, 'outputs', [VMEM] * 8, [shape(3, X, Y, CZ)] * 2, 6, 1...  3.4 us
    pallas_call x1, Pallas kernels, body(): call(primal_kernel, 'primal_products', [VMEM] * 7 + [ANY], [slab] * 3, 4, 8)  2.25 us
    pallas_call x1, Pallas kernels, body(): call(adjoint_kernel, 'adjoint_products', [VMEM] * 5 + [HBM, ANY], [slab]...  1.84 us
    pallas_call x4, Pallas kernels, gradient(): call(lambda *refs: gradient_kernel(k, *refs), f'gradient_{k}', [VMEM] * 8...  1.84 us
  transfers between devices with their start and end apart: 14, of which 10 were waited for; matrix products, arithmetic and copies ran while one was open for 0% of the time, Pallas kernels for 14%

profile of v8, /device:TPU:1, one launch (start us, length us, event | category | flops | bytes accessed | tf_op | source)
XLA Modules:
  0.0 63.0 jit_solution(10102241102572971657)
XLA Ops:
  1.3 7.3 %right_hand_sides.1 = (f32[8,256,128]{2,1,0:T(8,128)S(1)}, f32[8,256,128]{2,1,0:T(8,128)S(1)}, f32[8,256,128]{2,1,0:T(8,128)S(1)}, f32[8,256,128]{2,1,0:T(8,128)...) custom-call(s32[1]{0:T(128)S(6)} %copy.14.angle, ...), custom_call_target="tpu_custom_call" | custom-call | flops 1000 | bytes 18000000 | tf_op jit(solution)/shard_map/right_hand_sides/pallas_call | solution.py:554
  8.6 1.5 %collective-permute-start = (f32[12,8,128]{2,1,0:T(8,128)S(1)}, f32[12,8,128]{2,1,0:T(8,128)S(1)}, u32[]{:S(2)}, u32[]{:S(2)}) collective-permute-start(f32[12,8,128]{2,1,0:T(8,128)S(1)} %get-tuple-element.33), channel_id=1, source_target_pairs={{0,1},{1,0},{2,3},{3,2},{4,5},{5,4},{6,7},{7,6},{8,9},{9,8},{10,11... | collective-permute-start | bytes 147464 | tf_op jit(solution)/shard_map/ppermute | solution.py:512
  10.1 0.9 %collective-permute-done.other.a1 = f32[12,8,128]{2,1,0:T(8,128)S(1)} collective-permute-done((f32[12,8,128]{2,1,0:T(8,128)S(1)}, f32[12,8,128]{2,1,0:T(8,128)S(1)}, u32[]{:S(2)}, u32[]{:S(2)}) %collective-permute-start) | collective-permute-done | bytes 49184 | tf_op jit(solution)/shard_map/ppermute | solution.py:512
  11.0 3.9 %collective-permute-start.1 = (f32[12,8,128]{2,1,0:T(8,128)S(1)}, f32[12,8,128]{2,1,0:T(8,128)S(1)}, u32[]{:S(2)}, u32[]{:S(2)}) collective-permute-start(f32[12,8,128]{2,1,0:T(8,128)S(1)} %chip.1.after.m0), channel_id=1, source_target_pairs={{0,6},{1,7},{2,4},{3,5},{4,2},{5,3},{6,0},{7,1},{8,14},{9,15},{10,... | collective-permute-start | bytes 147464 | tf_op jit(solution)/shard_map/ppermute | solution.py:512
  14.9 0.7 %collective-permute-start.3 = (f32[12,8,128]{2,1,0:T(8,128)S(1)}, f32[12,8,128]{2,1,0:T(8,128)S(1)}, u32[]{:S(2)}, u32[]{:S(2)}) collective-permute-start(f32[12,8,128]{2,1,0:T(8,128)S(1)} %chip.1.after.m0), channel_id=1, source_target_pairs={{0,2},{1,3},{2,0},{3,1},{4,6},{5,7},{6,4},{7,5},{8,10},{9,11},{10,... | collective-permute-start | bytes 147464 | tf_op jit(solution)/shard_map/ppermute | solution.py:512
  15.6 1.8 %adjoint_products.1 = (f32[8,256,128]{2,1,0:T(8,128)S(1)}, f32[8,256,128]{2,1,0:T(8,128)S(1)}) custom-call(f32[8,256,128]{2,1,0:T(8,128)S(1)} %get-tuple-element.27.ax, f32[8,256,128]{2,1,0:T(8,128)S(1)} %get-tuple-element.28.ay, f32[8,256,128]{2,1,0:T(8,128)S(1)} %get-tuple-element.29.psx.refs_1_, f32[8,256,128]{2,1,0:T(8,128)S(1)} %get-tuple-element.30.psy.refs_2_, ...), custom_call_target="tpu_custom_call" | custom-call | flops 1000 | bytes 9000000 | tf_op jit(solution)/shard_map/adjoint_products/pallas_call | solution.py:570
  17.5 1.9 %collective-permute-done.2.m2 = f32[12,8,128]{2,1,0:T(8,128)S(1)} collective-permute-done((f32[12,8,128]{2,1,0:T(8,128)S(1)}, f32[12,8,128]{2,1,0:T(8,128)S(1)}, u32[]{:S(2)}, u32[]{:S(2)}) %collective-permute-start.2) | collective-permute-done | bytes 49184 | tf_op jit(solution)/shard_map/ppermute | solution.py:512
  19.5 2.6 %collective-permute-start.4 = (f32[12,8,128]{2,1,0:T(8,128)S(1)}, f32[12,8,128]{2,1,0:T(8,128)S(1)}, u32[]{:S(2)}, u32[]{:S(2)}) collective-permute-start(f32[12,8,128]{2,1,0:T(8,128)S(1)} %group.1.after.n0), channel_id=1, source_target_pairs={{0,24},{1,25},{2,26},{3,27},{4,28},{5,29},{6,30},{7,31},{8,16},{9,... | collective-permute-start | bytes 147464 | tf_op jit(solution)/shard_map/ppermute | solution.py:512
  22.0 0.5 collective-permute-start.5
  22.8 2.3 %primal_products.1 = (f32[8,256,128]{2,1,0:T(8,128)S(1)}, f32[8,256,128]{2,1,0:T(8,128)S(1)}, f32[8,256,128]{2,1,0:T(8,128)S(1)}) custom-call(f32[8,256,128]{2,1,0:T(8,128)S(1)} %get-tuple-element.24.rx, f32[8,256,128]{2,1,0:T(8,128)S(1)} %get-tuple-element.25.ry, f32[3,8,256,128]{3,2,1,0:T(8,128)S(1)} %get-tuple-element.26.h, ...), custom_call_target="tpu_custom_call" | custom-call | flops 1000 | bytes 12000000 | tf_op jit(solution)/shard_map/primal_products/pallas_call | solution.py:577
  25.1 1.4 %collective-permute-done.5.n2 = f32[12,8,128]{2,1,0:T(8,128)S(1)} collective-permute-done((f32[12,8,128]{2,1,0:T(8,128)S(1)}, f32[12,8,128]{2,1,0:T(8,128)S(1)}, u32[]{:S(2)}, u32[]{:S(2)}) %collective-permute-start.5) | collective-permute-done | bytes 49184 | tf_op jit(solution)/shard_map/ppermute | solution.py:512
  26.6 3.3 %collective-permute-start.7 = (f32[12,8,128]{2,1,0:T(8,128)S(1)}, f32[12,8,128]{2,1,0:T(8,128)S(1)}, u32[]{:S(2)}, u32[]{:S(2)}) collective-permute-start(f32[12,8,128]{2,1,0:T(8,128)S(1)} %get-tuple-element.41), channel_id=1, source_target_pairs={{0,1},{1,0},{2,3},{3,2},{4,5},{5,4},{6,7},{7,6},{8,9},{9,8},{10,11... | collective-permute-start | bytes 147464 | tf_op jit(solution)/shard_map/ppermute | solution.py:512
  29.9 0.9 %collective-permute-done.7.recv.refs_6_ = f32[12,8,128]{2,1,0:T(8,128)S(1)} collective-permute-done((f32[12,8,128]{2,1,0:T(8,128)S(1)}, f32[12,8,128]{2,1,0:T(8,128)S(1)}, u32[]{:S(2)}, u32[]{:S(2)}) %collective-permute-start.7) | collective-permute-done | bytes 49184 | tf_op jit(solution)/shard_map/ppermute | solution.py:512
  31.3 3.0 %collective-permute-start.8 = (f32[2,256,128]{2,1,0:T(8,128)S(1)}, f32[2,256,128]{2,1,0:T(8,128)S(1)}, u32[]{:S(2)}, u32[]{:S(2)}) collective-permute-start(f32[2,256,128]{2,1,0:T(8,128)S(1)} %gradient_2.1), channel_id=1, source_target_pairs={{0,64},{32,96},{64,0},{96,32},{1,65},{33,97},{65,1},{97,33},{2,66}... | collective-permute-start | bytes 786440 | tf_op jit(solution)/shard_map/ppermute | solution.py:512
  34.7 0.5 collective-permute-start.9
  35.7 0.5 collective-permute-start.10
  36.2 0.5 gradient_0.1
  36.6 3.8 %collective-permute-done.8 = f32[2,256,128]{2,1,0:T(8,128)S(1)} collective-permute-done((f32[2,256,128]{2,1,0:T(8,128)S(1)}, f32[2,256,128]{2,1,0:T(8,128)S(1)}, u32[]{:S(2)}, u32[]{:S(2)}) %collective-permute-start.8) | collective-permute-done | bytes 262176 | tf_op jit(solution)/shard_map/ppermute | solution.py:512
  40.4 6.0 %collective-permute-done.9 = f32[2,256,128]{2,1,0:T(8,128)S(1)} collective-permute-done((f32[2,256,128]{2,1,0:T(8,128)S(1)}, f32[2,256,128]{2,1,0:T(8,128)S(1)}, u32[]{:S(2)}, u32[]{:S(2)}) %collective-permute-start.9) | collective-permute-done | bytes 262176 | tf_op jit(solution)/shard_map/ppermute | solution.py:512
  46.5 3.2 %collective-permute-start.11 = (f32[2,256,128]{2,1,0:T(8,128)S(1)}, f32[2,256,128]{2,1,0:T(8,128)S(1)}, u32[]{:S(2)}, u32[]{:S(2)}) collective-permute-start(f32[2,256,128]{2,1,0:T(8,128)S(1)} %add_add_fusion.g0), channel_id=1, source_target_pairs={{0,64},{32,96},{64,0},{96,32},{1,65},{33,97},{65,1},{97,33},{2,66}... | collective-permute-start | bytes 786440 | tf_op jit(solution)/shard_map/ppermute | solution.py:512
  50.5 3.4 %outputs.1 = (f32[3,8,256,128]{3,2,1,0:T(8,128)}, f32[3,8,256,128]{3,2,1,0:T(8,128)}) custom-call(f32[8,256,128]{2,1,0:T(8,128)S(1)} %get-tuple-element.37.after.ex, f32[8,256,128]{2,1,0:T(8,128)S(1)} %get-tuple-element.38.ey, f32[3,8,256,128]{3,2,1,0:T(8,128)S(1)} %get-tuple-element.26.h, f32[8,256,128]{2,1,0:T(8,128)S(1)} %get-tuple-element.34.ez, ...), custom_call_target="tpu_custom_call" | custom-call | flops 1000 | bytes 18000000 | tf_op jit(solution)/shard_map/outputs/pallas_call | solution.py:594
  53.9 1.2 %collective-permute-done.11.g2 = f32[2,256,128]{2,1,0:T(8,128)S(1)} collective-permute-done((f32[2,256,128]{2,1,0:T(8,128)S(1)}, f32[2,256,128]{2,1,0:T(8,128)S(1)}, u32[]{:S(2)}, u32[]{:S(2)}) %collective-permute-start.11) | collective-permute-done | bytes 262176 | tf_op jit(solution)/shard_map/ppermute | solution.py:512
  55.2 6.6 %collective-permute-done.12.g1 = f32[2,256,128]{2,1,0:T(8,128)S(1)} collective-permute-done((f32[2,256,128]{2,1,0:T(8,128)S(1)}, f32[2,256,128]{2,1,0:T(8,128)S(1)}, u32[]{:S(2)}, u32[]{:S(2)}) %collective-permute-start.12) | collective-permute-done | bytes 262176 | tf_op jit(solution)/shard_map/ppermute | solution.py:512
  62.0 1.0 %place.1 = f32[8,256,128]{2,1,0:T(8,128)} custom-call(f32[2,256,128]{2,1,0:T(8,128)S(1)} %collective-permute-done.11.g2, f32[2,256,128]{2,1,0:T(8,128)S(1)} %collective-permute-done.12.g1, f32[2,256,128]{2,1,0:T(8,128)S(1)} %collective-permute-done.13.g3, f32[2,256,128]{2,1,0:T(8,128)S(1)} %add_add_fusion.g0), custom_call_target="tpu_custom_call" | custom-call | flops 1000 | bytes 3000000 | tf_op jit(solution)/shard_map/place/pallas_call | solution.py:602
  (17 shorter events, 3.1 us)
Async XLA Ops:
  8.6 2.4 %collective-permute-start = (f32[12,8,128]{2,1,0:T(8,128)S(1)}, f32[12,8,128]{2,1,0:T(8,128)S(1)}, u32[]{:S(2)}, u32[]{:S(2)}) collective-permute-start(f32[12,8,128]{2,1,0:T(8,128)S(1)} %get-tuple-element.33), channel_id=1, source_target_pairs={{0,1},{1,0},{2,3},{3,2},{4,5},{5,4},{6,7},{7,6},{8,9},{9,8},{10,11... | collective-permute-start | bytes 147464 | tf_op jit(solution)/shard_map/ppermute | solution.py:512
  11.0 6.4 %collective-permute-start.1 = (f32[12,8,128]{2,1,0:T(8,128)S(1)}, f32[12,8,128]{2,1,0:T(8,128)S(1)}, u32[]{:S(2)}, u32[]{:S(2)}) collective-permute-start(f32[12,8,128]{2,1,0:T(8,128)S(1)} %chip.1.after.m0), channel_id=1, source_target_pairs={{0,6},{1,7},{2,4},{3,5},{4,2},{5,3},{6,0},{7,1},{8,14},{9,15},{10,... | collective-permute-start | bytes 147464 | tf_op jit(solution)/shard_map/ppermute | solution.py:512
  14.9 4.4 %collective-permute-start.2 = (f32[12,8,128]{2,1,0:T(8,128)S(1)}, f32[12,8,128]{2,1,0:T(8,128)S(1)}, u32[]{:S(2)}, u32[]{:S(2)}) collective-permute-start(f32[12,8,128]{2,1,0:T(8,128)S(1)} %chip.1.after.m0), channel_id=1, source_target_pairs={{0,4},{1,5},{2,6},{3,7},{4,0},{5,1},{6,2},{7,3},{8,12},{9,13},{10,... | collective-permute-start | bytes 147464 | tf_op jit(solution)/shard_map/ppermute | solution.py:512
  14.9 4.4 %collective-permute-start.3 = (f32[12,8,128]{2,1,0:T(8,128)S(1)}, f32[12,8,128]{2,1,0:T(8,128)S(1)}, u32[]{:S(2)}, u32[]{:S(2)}) collective-permute-start(f32[12,8,128]{2,1,0:T(8,128)S(1)} %chip.1.after.m0), channel_id=1, source_target_pairs={{0,2},{1,3},{2,0},{3,1},{4,6},{5,7},{6,4},{7,5},{8,10},{9,11},{10,... | collective-permute-start | bytes 147464 | tf_op jit(solution)/shard_map/ppermute | solution.py:512
  19.5 5.6 %collective-permute-start.4 = (f32[12,8,128]{2,1,0:T(8,128)S(1)}, f32[12,8,128]{2,1,0:T(8,128)S(1)}, u32[]{:S(2)}, u32[]{:S(2)}) collective-permute-start(f32[12,8,128]{2,1,0:T(8,128)S(1)} %group.1.after.n0), channel_id=1, source_target_pairs={{0,24},{1,25},{2,26},{3,27},{4,28},{5,29},{6,30},{7,31},{8,16},{9,... | collective-permute-start | bytes 147464 | tf_op jit(solution)/shard_map/ppermute | solution.py:512
  22.0 4.4 %collective-permute-start.5 = (f32[12,8,128]{2,1,0:T(8,128)S(1)}, f32[12,8,128]{2,1,0:T(8,128)S(1)}, u32[]{:S(2)}, u32[]{:S(2)}) collective-permute-start(f32[12,8,128]{2,1,0:T(8,128)S(1)} %group.1.after.n0), channel_id=1, source_target_pairs={{0,16},{1,17},{2,18},{3,19},{4,20},{5,21},{6,22},{7,23},{8,24},{9,... | collective-permute-start | bytes 147464 | tf_op jit(solution)/shard_map/ppermute | solution.py:512
  22.5 3.9 %collective-permute-start.6 = (f32[12,8,128]{2,1,0:T(8,128)S(1)}, f32[12,8,128]{2,1,0:T(8,128)S(1)}, u32[]{:S(2)}, u32[]{:S(2)}) collective-permute-start(f32[12,8,128]{2,1,0:T(8,128)S(1)} %group.1.after.n0), channel_id=1, source_target_pairs={{0,8},{1,9},{2,10},{3,11},{4,12},{5,13},{6,14},{7,15},{8,0},{9,1},... | collective-permute-start | bytes 147464 | tf_op jit(solution)/shard_map/ppermute | solution.py:512
  26.6 4.2 %collective-permute-start.7 = (f32[12,8,128]{2,1,0:T(8,128)S(1)}, f32[12,8,128]{2,1,0:T(8,128)S(1)}, u32[]{:S(2)}, u32[]{:S(2)}) collective-permute-start(f32[12,8,128]{2,1,0:T(8,128)S(1)} %get-tuple-element.41), channel_id=1, source_target_pairs={{0,1},{1,0},{2,3},{3,2},{4,5},{5,4},{6,7},{7,6},{8,9},{9,8},{10,11... | collective-permute-start | bytes 147464 | tf_op jit(solution)/shard_map/ppermute | solution.py:512
  31.3 9.1 %collective-permute-start.8 = (f32[2,256,128]{2,1,0:T(8,128)S(1)}, f32[2,256,128]{2,1,0:T(8,128)S(1)}, u32[]{:S(2)}, u32[]{:S(2)}) collective-permute-start(f32[2,256,128]{2,1,0:T(8,128)S(1)} %gradient_2.1), channel_id=1, source_target_pairs={{0,64},{32,96},{64,0},{96,32},{1,65},{33,97},{65,1},{97,33},{2,66}... | collective-permute-start | bytes 786440 | tf_op jit(solution)/shard_map/ppermute | solution.py:512
  34.7 11.7 %collective-permute-start.9 = (f32[2,256,128]{2,1,0:T(8,128)S(1)}, f32[2,256,128]{2,1,0:T(8,128)S(1)}, u32[]{:S(2)}, u32[]{:S(2)}) collective-permute-start(f32[2,256,128]{2,1,0:T(8,128)S(1)} %gradient_1.1), channel_id=1, source_target_pairs={{0,32},{32,0},{64,96},{96,64},{1,33},{33,1},{65,97},{97,65},{2,34}... | collective-permute-start | bytes 786440 | tf_op jit(solution)/shard_map/ppermute | solution.py:512
  35.7 10.8 %collective-permute-start.10 = (f32[2,256,128]{2,1,0:T(8,128)S(1)}, f32[2,256,128]{2,1,0:T(8,128)S(1)}, u32[]{:S(2)}, u32[]{:S(2)}) collective-permute-start(f32[2,256,128]{2,1,0:T(8,128)S(1)} %gradient_3.1), channel_id=1, source_target_pairs={{0,96},{32,64},{64,32},{96,0},{1,97},{33,65},{65,33},{97,1},{2,98}... | collective-permute-start | bytes 786440 | tf_op jit(solution)/shard_map/ppermute | solution.py:512
  46.5 8.6 %collective-permute-start.11 = (f32[2,256,128]{2,1,0:T(8,128)S(1)}, f32[2,256,128]{2,1,0:T(8,128)S(1)}, u32[]{:S(2)}, u32[]{:S(2)}) collective-permute-start(f32[2,256,128]{2,1,0:T(8,128)S(1)} %add_add_fusion.g0), channel_id=1, source_target_pairs={{0,64},{32,96},{64,0},{96,32},{1,65},{33,97},{65,1},{97,33},{2,66}... | collective-permute-start | bytes 786440 | tf_op jit(solution)/shard_map/ppermute | solution.py:512
  49.8 12.0 %collective-permute-start.12 = (f32[2,256,128]{2,1,0:T(8,128)S(1)}, f32[2,256,128]{2,1,0:T(8,128)S(1)}, u32[]{:S(2)}, u32[]{:S(2)}) collective-permute-start(f32[2,256,128]{2,1,0:T(8,128)S(1)} %add_add_fusion.g0), channel_id=1, source_target_pairs={{0,32},{32,0},{64,96},{96,64},{1,33},{33,1},{65,97},{97,65},{2,34}... | collective-permute-start | bytes 786440 | tf_op jit(solution)/shard_map/ppermute | solution.py:512
  50.2 11.9 %collective-permute-start.13 = (f32[2,256,128]{2,1,0:T(8,128)S(1)}, f32[2,256,128]{2,1,0:T(8,128)S(1)}, u32[]{:S(2)}, u32[]{:S(2)}) collective-permute-start(f32[2,256,128]{2,1,0:T(8,128)S(1)} %add_add_fusion.g0), channel_id=1, source_target_pairs={{0,96},{32,64},{64,32},{96,0},{1,97},{33,65},{65,33},{97,1},{2,98}... | collective-permute-start | bytes 786440 | tf_op jit(solution)/shard_map/ppermute | solution.py:512

commit v9 on v8

--- a/solution.py
+++ b/solution.py
@@ -313,7 +313,7 @@
     repack(combine(*four(low, high, *(unpack(m) for m in (m0, m1, m2, m3)))[1]), out)
 
 
-def back_kernel(n3, n2, n1, n0, m3, m2, m1, m0, a0, a1, after, keep_o, send_o):
+def back_kernel(n2, n3, n1, n0, m3, m2, m1, m0, a0, a1, after, keep_o, send_o):
     core, zl, zh, xl, xh = bits()
     chip = order(core, unpack(a0), unpack(a1))
     m0, m1, m2, m3 = (unpack(m) for m in (m0, m1, m2, m3))
@@ -497,7 +497,7 @@
             copy.wait()
 
 
-def place_kernel(g2, g1, g3, g0, out, sems):
+def place_kernel(g2, g3, g1, g0, out, sems):
     src = lax.axis_index("src")
     copies = []
     for k, g in zip((2, 1, 3, 0), (g2, g1, g3, g0)):
@@ -572,14 +572,14 @@
         scratch=[pltpu.SemaphoreType.DMA],
     )(ax, ay, psx, psy, w, in_hbm(e), m0)
     (n0,) = call(group_kernel, "group", [VMEM] * 4 + [ANY], [message], 0.5, 4)(m3, m2, m1, m0, adjoint)
-    n3, n2, n1 = (swap(n0, "gz", 8 * k) for k in (3, 2, 1))
+    n2, n3, n1 = (swap(n0, "gz", 8 * k) for k in (2, 3, 1))
 
     ex, ey, grad = call(primal_kernel, "primal_products", [VMEM] * 7 + [ANY], [slab] * 3, 4, 8)(
         rx, ry, hv, ez, gs, adjoint, w, n0
     )
     own_edges, send_edges = call(
         back_kernel, "back", [VMEM] * 10 + [ANY], [shape(12, 8, CZ)] * 2, 0.5, 4
-    )(n3, n2, n1, n0, m3, m2, m1, m0, keep, other, ex)
+    )(n2, n3, n1, n0, m3, m2, m1, m0, keep, other, ex)
     other_edges = swap(send_edges, "gz", 1)
 
     def gradient(k):
@@ -588,7 +588,7 @@
             [shape(2, Y, CZ)], 1, 8,
         )(grad, psx, psy, gs, inv, own_edges, other_edges, w)[0]
 
-    arrived = [swap(gradient(k), "src", k) for k in (2, 1, 3)]
+    arrived = [swap(gradient(k), "src", k) for k in (2, 3, 1)]
     own = gradient(0)
 
     e_new, h_new = call(
@@ -598,11 +598,11 @@
     )(ex, ey, hv, ez, inv, own_edges, other_edges, w)
 
     total = own + arrived[0] + arrived[1] + arrived[2]
-    two, one, three = (swap(total, "src", k) for k in (2, 1, 3))
+    two, three, one = (swap(total, "src", k) for k in (2, 3, 1))
     (eps_grad,) = call(
         place_kernel, "place", [ANY] * 4, [slab], 1, 4, out_specs=[HBM],
         scratch=[pltpu.SemaphoreType.DMA((4,))],
-    )(two, one, three, total)
+    )(two, three, one, total)
     return (e_new[None], h_new[None], eps_grad)
 
 

time: 63.2 us -> 63.4 us (level)
  transfers between devices with their start and end apart: 14 -> 14, of which waited for: 10 -> 8; matrix products, arithmetic and copies ran while one was open for 0% -> 0% of each run, Pallas kernels for 14% -> 14%
where the time goes in v9:
time: 63.4 us; the launch traced here: 63.2 us
  waiting for transfers between devices  23.4 us (37%)
  starting transfers between devices  20.5 us (32%)
  Pallas kernels  17.9 us (28%)
  between operations  1.39 us (2%)
    ppermute x14, waiting for transfers between devices, swap(): lax.ppermute(block, axis, [(i, i ^ mask) for i in range(lax.axis_size(axi...  23.4 us
    ppermute x14, starting transfers between devices, swap(): lax.ppermute(block, axis, [(i, i ^ mask) for i in range(lax.axis_size(axi...  20.5 us
    pallas_call x1, Pallas kernels, body(): call(rhs_kernel, 'right_hand_sides', [SMEM, SMEM] + [HBM] * 9, [slab] * 8...  7.31 us
    pallas_call x1, Pallas kernels, body(): call(output_kernel, 'outputs', [VMEM] * 8, [shape(3, X, Y, CZ)] * 2, 6, 1...  3.4 us
    pallas_call x1, Pallas kernels, body(): call(primal_kernel, 'primal_products', [VMEM] * 7 + [ANY], [slab] * 3, 4, 8)  2.25 us
    pallas_call x4, Pallas kernels, gradient(): call(lambda *refs: gradient_kernel(k, *refs), f'gradient_{k}', [VMEM] * 8...  1.84 us
    pallas_call x1, Pallas kernels, body(): call(adjoint_kernel, 'adjoint_products', [VMEM] * 5 + [HBM, ANY], [slab]...  1.84 us
  transfers between devices with their start and end apart: 14, of which 8 were waited for; matrix products, arithmetic and copies ran while one was open for 0% of the time, Pallas kernels for 14%

profile of v9, /device:TPU:1, one launch (start us, length us, event | category | flops | bytes accessed | tf_op | source)
XLA Modules:
  0.0 63.2 jit_solution(4650617320040180305)
XLA Ops:
  1.3 7.3 %right_hand_sides.1 = (f32[8,256,128]{2,1,0:T(8,128)S(1)}, f32[8,256,128]{2,1,0:T(8,128)S(1)}, f32[8,256,128]{2,1,0:T(8,128)S(1)}, f32[8,256,128]{2,1,0:T(8,128)...) custom-call(s32[1]{0:T(128)S(6)} %copy.14.angle, ...), custom_call_target="tpu_custom_call" | custom-call | flops 1000 | bytes 18000000 | tf_op jit(solution)/shard_map/right_hand_sides/pallas_call | solution.py:554
  8.6 1.5 %collective-permute-start = (f32[12,8,128]{2,1,0:T(8,128)S(1)}, f32[12,8,128]{2,1,0:T(8,128)S(1)}, u32[]{:S(2)}, u32[]{:S(2)}) collective-permute-start(f32[12,8,128]{2,1,0:T(8,128)S(1)} %get-tuple-element.33), channel_id=1, source_target_pairs={{0,1},{1,0},{2,3},{3,2},{4,5},{5,4},{6,7},{7,6},{8,9},{9,8},{10,11... | collective-permute-start | bytes 147464 | tf_op jit(solution)/shard_map/ppermute | solution.py:512
  10.1 0.9 %collective-permute-done.other.a1 = f32[12,8,128]{2,1,0:T(8,128)S(1)} collective-permute-done((f32[12,8,128]{2,1,0:T(8,128)S(1)}, f32[12,8,128]{2,1,0:T(8,128)S(1)}, u32[]{:S(2)}, u32[]{:S(2)}) %collective-permute-start) | collective-permute-done | bytes 49184 | tf_op jit(solution)/shard_map/ppermute | solution.py:512
  11.0 3.9 %collective-permute-start.1 = (f32[12,8,128]{2,1,0:T(8,128)S(1)}, f32[12,8,128]{2,1,0:T(8,128)S(1)}, u32[]{:S(2)}, u32[]{:S(2)}) collective-permute-start(f32[12,8,128]{2,1,0:T(8,128)S(1)} %chip.1.after.m0), channel_id=1, source_target_pairs={{0,6},{1,7},{2,4},{3,5},{4,2},{5,3},{6,0},{7,1},{8,14},{9,15},{10,... | collective-permute-start | bytes 147464 | tf_op jit(solution)/shard_map/ppermute | solution.py:512
  14.9 0.7 %collective-permute-start.3 = (f32[12,8,128]{2,1,0:T(8,128)S(1)}, f32[12,8,128]{2,1,0:T(8,128)S(1)}, u32[]{:S(2)}, u32[]{:S(2)}) collective-permute-start(f32[12,8,128]{2,1,0:T(8,128)S(1)} %chip.1.after.m0), channel_id=1, source_target_pairs={{0,2},{1,3},{2,0},{3,1},{4,6},{5,7},{6,4},{7,5},{8,10},{9,11},{10,... | collective-permute-start | bytes 147464 | tf_op jit(solution)/shard_map/ppermute | solution.py:512
  15.6 1.8 %adjoint_products.1 = (f32[8,256,128]{2,1,0:T(8,128)S(1)}, f32[8,256,128]{2,1,0:T(8,128)S(1)}) custom-call(f32[8,256,128]{2,1,0:T(8,128)S(1)} %get-tuple-element.27.ax, f32[8,256,128]{2,1,0:T(8,128)S(1)} %get-tuple-element.28.ay, f32[8,256,128]{2,1,0:T(8,128)S(1)} %get-tuple-element.29.psx.refs_1_, f32[8,256,128]{2,1,0:T(8,128)S(1)} %get-tuple-element.30.psy.refs_2_, ...), custom_call_target="tpu_custom_call" | custom-call | flops 1000 | bytes 9000000 | tf_op jit(solution)/shard_map/adjoint_products/pallas_call | solution.py:570
  17.5 1.9 %collective-permute-done.2.m2 = f32[12,8,128]{2,1,0:T(8,128)S(1)} collective-permute-done((f32[12,8,128]{2,1,0:T(8,128)S(1)}, f32[12,8,128]{2,1,0:T(8,128)S(1)}, u32[]{:S(2)}, u32[]{:S(2)}) %collective-permute-start.2) | collective-permute-done | bytes 49184 | tf_op jit(solution)/shard_map/ppermute | solution.py:512
  19.5 2.8 %collective-permute-start.4 = (f32[12,8,128]{2,1,0:T(8,128)S(1)}, f32[12,8,128]{2,1,0:T(8,128)S(1)}, u32[]{:S(2)}, u32[]{:S(2)}) collective-permute-start(f32[12,8,128]{2,1,0:T(8,128)S(1)} %group.1.after.n0), channel_id=1, source_target_pairs={{0,16},{1,17},{2,18},{3,19},{4,20},{5,21},{6,22},{7,23},{8,24},{9,... | collective-permute-start | bytes 147464 | tf_op jit(solution)/shard_map/ppermute | solution.py:512
  22.3 0.9 %collective-permute-start.5 = (f32[12,8,128]{2,1,0:T(8,128)S(1)}, f32[12,8,128]{2,1,0:T(8,128)S(1)}, u32[]{:S(2)}, u32[]{:S(2)}) collective-permute-start(f32[12,8,128]{2,1,0:T(8,128)S(1)} %group.1.after.n0), channel_id=1, source_target_pairs={{0,24},{1,25},{2,26},{3,27},{4,28},{5,29},{6,30},{7,31},{8,16},{9,... | collective-permute-start | bytes 147464 | tf_op jit(solution)/shard_map/ppermute | solution.py:512
  23.1 2.3 %primal_products.1 = (f32[8,256,128]{2,1,0:T(8,128)S(1)}, f32[8,256,128]{2,1,0:T(8,128)S(1)}, f32[8,256,128]{2,1,0:T(8,128)S(1)}) custom-call(f32[8,256,128]{2,1,0:T(8,128)S(1)} %get-tuple-element.24.rx, f32[8,256,128]{2,1,0:T(8,128)S(1)} %get-tuple-element.25.ry, f32[3,8,256,128]{3,2,1,0:T(8,128)S(1)} %get-tuple-element.26.h, ...), custom_call_target="tpu_custom_call" | custom-call | flops 1000 | bytes 12000000 | tf_op jit(solution)/shard_map/primal_products/pallas_call | solution.py:577
  25.4 1.3 %collective-permute-done.5.n3 = f32[12,8,128]{2,1,0:T(8,128)S(1)} collective-permute-done((f32[12,8,128]{2,1,0:T(8,128)S(1)}, f32[12,8,128]{2,1,0:T(8,128)S(1)}, u32[]{:S(2)}, u32[]{:S(2)}) %collective-permute-start.5) | collective-permute-done | bytes 49184 | tf_op jit(solution)/shard_map/ppermute | solution.py:512
  26.9 3.0 %collective-permute-start.7 = (f32[12,8,128]{2,1,0:T(8,128)S(1)}, f32[12,8,128]{2,1,0:T(8,128)S(1)}, u32[]{:S(2)}, u32[]{:S(2)}) collective-permute-start(f32[12,8,128]{2,1,0:T(8,128)S(1)} %get-tuple-element.41), channel_id=1, source_target_pairs={{0,1},{1,0},{2,3},{3,2},{4,5},{5,4},{6,7},{7,6},{8,9},{9,8},{10,11... | collective-permute-start | bytes 147464 | tf_op jit(solution)/shard_map/ppermute | solution.py:512
  29.9 0.9 %collective-permute-done.7.recv.refs_6_ = f32[12,8,128]{2,1,0:T(8,128)S(1)} collective-permute-done((f32[12,8,128]{2,1,0:T(8,128)S(1)}, f32[12,8,128]{2,1,0:T(8,128)S(1)}, u32[]{:S(2)}, u32[]{:S(2)}) %collective-permute-start.7) | collective-permute-done | bytes 49184 | tf_op jit(solution)/shard_map/ppermute | solution.py:512
  31.3 3.0 %collective-permute-start.8 = (f32[2,256,128]{2,1,0:T(8,128)S(1)}, f32[2,256,128]{2,1,0:T(8,128)S(1)}, u32[]{:S(2)}, u32[]{:S(2)}) collective-permute-start(f32[2,256,128]{2,1,0:T(8,128)S(1)} %gradient_2.1), channel_id=1, source_target_pairs={{0,64},{32,96},{64,0},{96,32},{1,65},{33,97},{65,1},{97,33},{2,66}... | collective-permute-start | bytes 786440 | tf_op jit(solution)/shard_map/ppermute | solution.py:512
  34.7 0.9 %collective-permute-start.9 = (f32[2,256,128]{2,1,0:T(8,128)S(1)}, f32[2,256,128]{2,1,0:T(8,128)S(1)}, u32[]{:S(2)}, u32[]{:S(2)}) collective-permute-start(f32[2,256,128]{2,1,0:T(8,128)S(1)} %gradient_3.1), channel_id=1, source_target_pairs={{0,96},{32,64},{64,32},{96,0},{1,97},{33,65},{65,33},{97,1},{2,98}... | collective-permute-start | bytes 786440 | tf_op jit(solution)/shard_map/ppermute | solution.py:512
  36.1 0.5 gradient_0.1
  36.6 3.8 %collective-permute-done.8 = f32[2,256,128]{2,1,0:T(8,128)S(1)} collective-permute-done((f32[2,256,128]{2,1,0:T(8,128)S(1)}, f32[2,256,128]{2,1,0:T(8,128)S(1)}, u32[]{:S(2)}, u32[]{:S(2)}) %collective-permute-start.8) | collective-permute-done | bytes 262176 | tf_op jit(solution)/shard_map/ppermute | solution.py:512
  40.4 6.3 %collective-permute-done.9 = f32[2,256,128]{2,1,0:T(8,128)S(1)} collective-permute-done((f32[2,256,128]{2,1,0:T(8,128)S(1)}, f32[2,256,128]{2,1,0:T(8,128)S(1)}, u32[]{:S(2)}, u32[]{:S(2)}) %collective-permute-start.9) | collective-permute-done | bytes 262176 | tf_op jit(solution)/shard_map/ppermute | solution.py:512
  46.7 2.5 %collective-permute-start.11 = (f32[2,256,128]{2,1,0:T(8,128)S(1)}, f32[2,256,128]{2,1,0:T(8,128)S(1)}, u32[]{:S(2)}, u32[]{:S(2)}) collective-permute-start(f32[2,256,128]{2,1,0:T(8,128)S(1)} %add_add_fusion.g0), channel_id=1, source_target_pairs={{0,64},{32,96},{64,0},{96,32},{1,65},{33,97},{65,1},{97,33},{2,66}... | collective-permute-start | bytes 786440 | tf_op jit(solution)/shard_map/ppermute | solution.py:512
  49.3 1.2 %collective-permute-start.12 = (f32[2,256,128]{2,1,0:T(8,128)S(1)}, f32[2,256,128]{2,1,0:T(8,128)S(1)}, u32[]{:S(2)}, u32[]{:S(2)}) collective-permute-start(f32[2,256,128]{2,1,0:T(8,128)S(1)} %add_add_fusion.g0), channel_id=1, source_target_pairs={{0,96},{32,64},{64,32},{96,0},{1,97},{33,65},{65,33},{97,1},{2,98}... | collective-permute-start | bytes 786440 | tf_op jit(solution)/shard_map/ppermute | solution.py:512
  50.5 3.4 %outputs.1 = (f32[3,8,256,128]{3,2,1,0:T(8,128)}, f32[3,8,256,128]{3,2,1,0:T(8,128)}) custom-call(f32[8,256,128]{2,1,0:T(8,128)S(1)} %get-tuple-element.37.after.ex, f32[8,256,128]{2,1,0:T(8,128)S(1)} %get-tuple-element.38.ey, f32[3,8,256,128]{3,2,1,0:T(8,128)S(1)} %get-tuple-element.26.h, f32[8,256,128]{2,1,0:T(8,128)S(1)} %get-tuple-element.34.ez, ...), custom_call_target="tpu_custom_call" | custom-call | flops 1000 | bytes 18000000 | tf_op jit(solution)/shard_map/outputs/pallas_call | solution.py:594
  53.9 1.4 %collective-permute-done.11.g2 = f32[2,256,128]{2,1,0:T(8,128)S(1)} collective-permute-done((f32[2,256,128]{2,1,0:T(8,128)S(1)}, f32[2,256,128]{2,1,0:T(8,128)S(1)}, u32[]{:S(2)}, u32[]{:S(2)}) %collective-permute-start.11) | collective-permute-done | bytes 262176 | tf_op jit(solution)/shard_map/ppermute | solution.py:512
  55.3 6.9 %collective-permute-done.12.g3 = f32[2,256,128]{2,1,0:T(8,128)S(1)} collective-permute-done((f32[2,256,128]{2,1,0:T(8,128)S(1)}, f32[2,256,128]{2,1,0:T(8,128)S(1)}, u32[]{:S(2)}, u32[]{:S(2)}) %collective-permute-start.12) | collective-permute-done | bytes 262176 | tf_op jit(solution)/shard_map/ppermute | solution.py:512
  62.2 1.0 %place.1 = f32[8,256,128]{2,1,0:T(8,128)} custom-call(f32[2,256,128]{2,1,0:T(8,128)S(1)} %collective-permute-done.11.g2, f32[2,256,128]{2,1,0:T(8,128)S(1)} %collective-permute-done.12.g3, f32[2,256,128]{2,1,0:T(8,128)S(1)} %collective-permute-done.13.g1, f32[2,256,128]{2,1,0:T(8,128)S(1)} %add_add_fusion.g0), custom_call_target="tpu_custom_call" | custom-call | flops 1000 | bytes 3000000 | tf_op jit(solution)/shard_map/place/pallas_call | solution.py:602
  (17 shorter events, 1.8 us)
Async XLA Ops:
  8.6 2.4 %collective-permute-start = (f32[12,8,128]{2,1,0:T(8,128)S(1)}, f32[12,8,128]{2,1,0:T(8,128)S(1)}, u32[]{:S(2)}, u32[]{:S(2)}) collective-permute-start(f32[12,8,128]{2,1,0:T(8,128)S(1)} %get-tuple-element.33), channel_id=1, source_target_pairs={{0,1},{1,0},{2,3},{3,2},{4,5},{5,4},{6,7},{7,6},{8,9},{9,8},{10,11... | collective-permute-start | bytes 147464 | tf_op jit(solution)/shard_map/ppermute | solution.py:512
  11.0 6.4 %collective-permute-start.1 = (f32[12,8,128]{2,1,0:T(8,128)S(1)}, f32[12,8,128]{2,1,0:T(8,128)S(1)}, u32[]{:S(2)}, u32[]{:S(2)}) collective-permute-start(f32[12,8,128]{2,1,0:T(8,128)S(1)} %chip.1.after.m0), channel_id=1, source_target_pairs={{0,6},{1,7},{2,4},{3,5},{4,2},{5,3},{6,0},{7,1},{8,14},{9,15},{10,... | collective-permute-start | bytes 147464 | tf_op jit(solution)/shard_map/ppermute | solution.py:512
  14.9 4.4 %collective-permute-start.2 = (f32[12,8,128]{2,1,0:T(8,128)S(1)}, f32[12,8,128]{2,1,0:T(8,128)S(1)}, u32[]{:S(2)}, u32[]{:S(2)}) collective-permute-start(f32[12,8,128]{2,1,0:T(8,128)S(1)} %chip.1.after.m0), channel_id=1, source_target_pairs={{0,4},{1,5},{2,6},{3,7},{4,0},{5,1},{6,2},{7,3},{8,12},{9,13},{10,... | collective-permute-start | bytes 147464 | tf_op jit(solution)/shard_map/ppermute | solution.py:512
  14.9 4.4 %collective-permute-start.3 = (f32[12,8,128]{2,1,0:T(8,128)S(1)}, f32[12,8,128]{2,1,0:T(8,128)S(1)}, u32[]{:S(2)}, u32[]{:S(2)}) collective-permute-start(f32[12,8,128]{2,1,0:T(8,128)S(1)} %chip.1.after.m0), channel_id=1, source_target_pairs={{0,2},{1,3},{2,0},{3,1},{4,6},{5,7},{6,4},{7,5},{8,10},{9,11},{10,... | collective-permute-start | bytes 147464 | tf_op jit(solution)/shard_map/ppermute | solution.py:512
  19.5 5.9 %collective-permute-start.4 = (f32[12,8,128]{2,1,0:T(8,128)S(1)}, f32[12,8,128]{2,1,0:T(8,128)S(1)}, u32[]{:S(2)}, u32[]{:S(2)}) collective-permute-start(f32[12,8,128]{2,1,0:T(8,128)S(1)} %group.1.after.n0), channel_id=1, source_target_pairs={{0,16},{1,17},{2,18},{3,19},{4,20},{5,21},{6,22},{7,23},{8,24},{9,... | collective-permute-start | bytes 147464 | tf_op jit(solution)/shard_map/ppermute | solution.py:512
  22.3 4.5 %collective-permute-start.5 = (f32[12,8,128]{2,1,0:T(8,128)S(1)}, f32[12,8,128]{2,1,0:T(8,128)S(1)}, u32[]{:S(2)}, u32[]{:S(2)}) collective-permute-start(f32[12,8,128]{2,1,0:T(8,128)S(1)} %group.1.after.n0), channel_id=1, source_target_pairs={{0,24},{1,25},{2,26},{3,27},{4,28},{5,29},{6,30},{7,31},{8,16},{9,... | collective-permute-start | bytes 147464 | tf_op jit(solution)/shard_map/ppermute | solution.py:512
  23.1 3.6 %collective-permute-start.6 = (f32[12,8,128]{2,1,0:T(8,128)S(1)}, f32[12,8,128]{2,1,0:T(8,128)S(1)}, u32[]{:S(2)}, u32[]{:S(2)}) collective-permute-start(f32[12,8,128]{2,1,0:T(8,128)S(1)} %group.1.after.n0), channel_id=1, source_target_pairs={{0,8},{1,9},{2,10},{3,11},{4,12},{5,13},{6,14},{7,15},{8,0},{9,1},... | collective-permute-start | bytes 147464 | tf_op jit(solution)/shard_map/ppermute | solution.py:512
  26.9 3.9 %collective-permute-start.7 = (f32[12,8,128]{2,1,0:T(8,128)S(1)}, f32[12,8,128]{2,1,0:T(8,128)S(1)}, u32[]{:S(2)}, u32[]{:S(2)}) collective-permute-start(f32[12,8,128]{2,1,0:T(8,128)S(1)} %get-tuple-element.41), channel_id=1, source_target_pairs={{0,1},{1,0},{2,3},{3,2},{4,5},{5,4},{6,7},{7,6},{8,9},{9,8},{10,11... | collective-permute-start | bytes 147464 | tf_op jit(solution)/shard_map/ppermute | solution.py:512
  31.3 9.1 %collective-permute-start.8 = (f32[2,256,128]{2,1,0:T(8,128)S(1)}, f32[2,256,128]{2,1,0:T(8,128)S(1)}, u32[]{:S(2)}, u32[]{:S(2)}) collective-permute-start(f32[2,256,128]{2,1,0:T(8,128)S(1)} %gradient_2.1), channel_id=1, source_target_pairs={{0,64},{32,96},{64,0},{96,32},{1,65},{33,97},{65,1},{97,33},{2,66}... | collective-permute-start | bytes 786440 | tf_op jit(solution)/shard_map/ppermute | solution.py:512
  34.7 12.0 %collective-permute-start.9 = (f32[2,256,128]{2,1,0:T(8,128)S(1)}, f32[2,256,128]{2,1,0:T(8,128)S(1)}, u32[]{:S(2)}, u32[]{:S(2)}) collective-permute-start(f32[2,256,128]{2,1,0:T(8,128)S(1)} %gradient_3.1), channel_id=1, source_target_pairs={{0,96},{32,64},{64,32},{96,0},{1,97},{33,65},{65,33},{97,1},{2,98}... | collective-permute-start | bytes 786440 | tf_op jit(solution)/shard_map/ppermute | solution.py:512
  36.0 10.6 %collective-permute-start.10 = (f32[2,256,128]{2,1,0:T(8,128)S(1)}, f32[2,256,128]{2,1,0:T(8,128)S(1)}, u32[]{:S(2)}, u32[]{:S(2)}) collective-permute-start(f32[2,256,128]{2,1,0:T(8,128)S(1)} %gradient_1.1), channel_id=1, source_target_pairs={{0,32},{32,0},{64,96},{96,64},{1,33},{33,1},{65,97},{97,65},{2,34}... | collective-permute-start | bytes 786440 | tf_op jit(solution)/shard_map/ppermute | solution.py:512
  46.7 8.6 %collective-permute-start.11 = (f32[2,256,128]{2,1,0:T(8,128)S(1)}, f32[2,256,128]{2,1,0:T(8,128)S(1)}, u32[]{:S(2)}, u32[]{:S(2)}) collective-permute-start(f32[2,256,128]{2,1,0:T(8,128)S(1)} %add_add_fusion.g0), channel_id=1, source_target_pairs={{0,64},{32,96},{64,0},{96,32},{1,65},{33,97},{65,1},{97,33},{2,66}... | collective-permute-start | bytes 786440 | tf_op jit(solution)/shard_map/ppermute | solution.py:512
  49.3 12.9 %collective-permute-start.12 = (f32[2,256,128]{2,1,0:T(8,128)S(1)}, f32[2,256,128]{2,1,0:T(8,128)S(1)}, u32[]{:S(2)}, u32[]{:S(2)}) collective-permute-start(f32[2,256,128]{2,1,0:T(8,128)S(1)} %add_add_fusion.g0), channel_id=1, source_target_pairs={{0,96},{32,64},{64,32},{96,0},{1,97},{33,65},{65,33},{97,1},{2,98}... | collective-permute-start | bytes 786440 | tf_op jit(solution)/shard_map/ppermute | solution.py:512
  50.5 11.7 %collective-permute-start.13 = (f32[2,256,128]{2,1,0:T(8,128)S(1)}, f32[2,256,128]{2,1,0:T(8,128)S(1)}, u32[]{:S(2)}, u32[]{:S(2)}) collective-permute-start(f32[2,256,128]{2,1,0:T(8,128)S(1)} %add_add_fusion.g0), channel_id=1, source_target_pairs={{0,32},{32,0},{64,96},{96,64},{1,33},{33,1},{65,97},{97,65},{2,34}... | collective-permute-start | bytes 786440 | tf_op jit(solution)/shard_map/ppermute | solution.py:512

commit v10 on v9

--- a/solution.py
+++ b/solution.py
@@ -216,7 +216,7 @@
         put(send_o, False)
         return carry
 
-    lax.fori_loop(0, X // 2, one_pair, 0)
+    lax.fori_loop(0, X // 2, one_pair, 0, unroll=True)
 
 
 def unpack(ref):
@@ -497,10 +497,10 @@
             copy.wait()
 
 
-def place_kernel(g2, g3, g1, g0, out, sems):
+def place_kernel(g1, g2, g3, g0, out, sems):
     src = lax.axis_index("src")
     copies = []
-    for k, g in zip((2, 1, 3, 0), (g2, g1, g3, g0)):
+    for k, g in zip((1, 2, 3, 0), (g1, g2, g3, g0)):
         copies.append(pltpu.make_async_copy(g, out.at[pl.ds(2 * (src ^ k), 2)], sems.at[k]))
     for copy in copies:
         copy.start()
@@ -588,7 +588,7 @@
             [shape(2, Y, CZ)], 1, 8,
         )(grad, psx, psy, gs, inv, own_edges, other_edges, w)[0]
 
-    arrived = [swap(gradient(k), "src", k) for k in (2, 3, 1)]
+    arrived = [swap(gradient(k), "src", k) for k in (1, 2, 3)]
     own = gradient(0)
 
     e_new, h_new = call(
@@ -598,11 +598,11 @@
     )(ex, ey, hv, ez, inv, own_edges, other_edges, w)
 
     total = own + arrived[0] + arrived[1] + arrived[2]
-    two, three, one = (swap(total, "src", k) for k in (2, 3, 1))
+    one, two, three = (swap(total, "src", k) for k in (1, 2, 3))
     (eps_grad,) = call(
         place_kernel, "place", [ANY] * 4, [slab], 1, 4, out_specs=[HBM],
         scratch=[pltpu.SemaphoreType.DMA((4,))],
-    )(two, three, one, total)
+    )(one, two, three, total)
     return (e_new[None], h_new[None], eps_grad)
 
 

time: 63.4 us -> 66.7 us (1.052); the launches traced: 63.2 us -> 65.8 us
  waiting for transfers between devices: 23.4 us -> 25.8 us
    ppermute x14, waiting for transfers between devices: 23.4 us -> 25.8 us  [swap(): lax.ppermute(block, axis, [(i, i ^ mask) for i in range(lax.axis_size(axi...]
  transfers between devices with their start and end apart: 14 -> 14, of which waited for: 8 -> 9; matrix products, arithmetic and copies ran while one was open for 0% -> 0% of each run, Pallas kernels for 14% -> 13%
where the time goes in v10:
time: 66.7 us; the launch traced here: 65.8 us
  waiting for transfers between devices  25.8 us (39%)
  starting transfers between devices  20.8 us (31%)
  Pallas kernels  17.7 us (27%)
  between operations  1.41 us (2%)
    ppermute x14, waiting for transfers between devices, swap(): lax.ppermute(block, axis, [(i, i ^ mask) for i in range(lax.axis_size(axi...  25.8 us
    ppermute x14, starting transfers between devices, swap(): lax.ppermute(block, axis, [(i, i ^ mask) for i in range(lax.axis_size(axi...  20.8 us
    pallas_call x1, Pallas kernels, body(): call(rhs_kernel, 'right_hand_sides', [SMEM, SMEM] + [HBM] * 9, [slab] * 8...  7.11 us
    pallas_call x1, Pallas kernels, body(): call(output_kernel, 'outputs', [VMEM] * 8, [shape(3, X, Y, CZ)] * 2, 6, 1...  3.4 us
    pallas_call x1, Pallas kernels, body(): call(primal_kernel, 'primal_products', [VMEM] * 7 + [ANY], [slab] * 3, 4, 8)  2.25 us
    pallas_call x4, Pallas kernels, gradient(): call(lambda *refs: gradient_kernel(k, *refs), f'gradient_{k}', [VMEM] * 8...  1.84 us
    pallas_call x1, Pallas kernels, body(): call(adjoint_kernel, 'adjoint_products', [VMEM] * 5 + [HBM, ANY], [slab]...  1.84 us
  transfers between devices with their start and end apart: 14, of which 9 were waited for; matrix products, arithmetic and copies ran while one was open for 0% of the time, Pallas kernels for 13%

profile of v10, /device:TPU:1, one launch (start us, length us, event | category | flops | bytes accessed | tf_op | source)
XLA Modules:
  0.0 65.8 jit_solution(6630189653619259123)
XLA Ops:
  1.3 7.1 %right_hand_sides.1 = (f32[8,256,128]{2,1,0:T(8,128)S(1)}, f32[8,256,128]{2,1,0:T(8,128)S(1)}, f32[8,256,128]{2,1,0:T(8,128)S(1)}, f32[8,256,128]{2,1,0:T(8,128)...) custom-call(s32[1]{0:T(128)S(6)} %copy.14.angle, ...), custom_call_target="tpu_custom_call" | custom-call | flops 1000 | bytes 18000000 | tf_op jit(solution)/shard_map/right_hand_sides/pallas_call | solution.py:554
  8.4 1.5 %collective-permute-start = (f32[12,8,128]{2,1,0:T(8,128)S(1)}, f32[12,8,128]{2,1,0:T(8,128)S(1)}, u32[]{:S(2)}, u32[]{:S(2)}) collective-permute-start(f32[12,8,128]{2,1,0:T(8,128)S(1)} %get-tuple-element.33), channel_id=1, source_target_pairs={{0,1},{1,0},{2,3},{3,2},{4,5},{5,4},{6,7},{7,6},{8,9},{9,8},{10,11... | collective-permute-start | bytes 147464 | tf_op jit(solution)/shard_map/ppermute | solution.py:512
  9.9 0.9 %collective-permute-done.other.a1 = f32[12,8,128]{2,1,0:T(8,128)S(1)} collective-permute-done((f32[12,8,128]{2,1,0:T(8,128)S(1)}, f32[12,8,128]{2,1,0:T(8,128)S(1)}, u32[]{:S(2)}, u32[]{:S(2)}) %collective-permute-start) | collective-permute-done | bytes 49184 | tf_op jit(solution)/shard_map/ppermute | solution.py:512
  10.8 3.9 %collective-permute-start.1 = (f32[12,8,128]{2,1,0:T(8,128)S(1)}, f32[12,8,128]{2,1,0:T(8,128)S(1)}, u32[]{:S(2)}, u32[]{:S(2)}) collective-permute-start(f32[12,8,128]{2,1,0:T(8,128)S(1)} %chip.1.after.m0), channel_id=1, source_target_pairs={{0,6},{1,7},{2,4},{3,5},{4,2},{5,3},{6,0},{7,1},{8,14},{9,15},{10,... | collective-permute-start | bytes 147464 | tf_op jit(solution)/shard_map/ppermute | solution.py:512
  14.7 0.7 %collective-permute-start.3 = (f32[12,8,128]{2,1,0:T(8,128)S(1)}, f32[12,8,128]{2,1,0:T(8,128)S(1)}, u32[]{:S(2)}, u32[]{:S(2)}) collective-permute-start(f32[12,8,128]{2,1,0:T(8,128)S(1)} %chip.1.after.m0), channel_id=1, source_target_pairs={{0,2},{1,3},{2,0},{3,1},{4,6},{5,7},{6,4},{7,5},{8,10},{9,11},{10,... | collective-permute-start | bytes 147464 | tf_op jit(solution)/shard_map/ppermute | solution.py:512
  15.4 1.8 %adjoint_products.1 = (f32[8,256,128]{2,1,0:T(8,128)S(1)}, f32[8,256,128]{2,1,0:T(8,128)S(1)}) custom-call(f32[8,256,128]{2,1,0:T(8,128)S(1)} %get-tuple-element.27.ax, f32[8,256,128]{2,1,0:T(8,128)S(1)} %get-tuple-element.28.ay, f32[8,256,128]{2,1,0:T(8,128)S(1)} %get-tuple-element.29.psx.refs_1_, f32[8,256,128]{2,1,0:T(8,128)S(1)} %get-tuple-element.30.psy.refs_2_, ...), custom_call_target="tpu_custom_call" | custom-call | flops 1000 | bytes 9000000 | tf_op jit(solution)/shard_map/adjoint_products/pallas_call | solution.py:570
  17.3 1.9 %collective-permute-done.2.m2 = f32[12,8,128]{2,1,0:T(8,128)S(1)} collective-permute-done((f32[12,8,128]{2,1,0:T(8,128)S(1)}, f32[12,8,128]{2,1,0:T(8,128)S(1)}, u32[]{:S(2)}, u32[]{:S(2)}) %collective-permute-start.2) | collective-permute-done | bytes 49184 | tf_op jit(solution)/shard_map/ppermute | solution.py:512
  19.3 2.8 %collective-permute-start.4 = (f32[12,8,128]{2,1,0:T(8,128)S(1)}, f32[12,8,128]{2,1,0:T(8,128)S(1)}, u32[]{:S(2)}, u32[]{:S(2)}) collective-permute-start(f32[12,8,128]{2,1,0:T(8,128)S(1)} %group.1.after.n0), channel_id=1, source_target_pairs={{0,16},{1,17},{2,18},{3,19},{4,20},{5,21},{6,22},{7,23},{8,24},{9,... | collective-permute-start | bytes 147464 | tf_op jit(solution)/shard_map/ppermute | solution.py:512
  22.1 0.9 %collective-permute-start.5 = (f32[12,8,128]{2,1,0:T(8,128)S(1)}, f32[12,8,128]{2,1,0:T(8,128)S(1)}, u32[]{:S(2)}, u32[]{:S(2)}) collective-permute-start(f32[12,8,128]{2,1,0:T(8,128)S(1)} %group.1.after.n0), channel_id=1, source_target_pairs={{0,24},{1,25},{2,26},{3,27},{4,28},{5,29},{6,30},{7,31},{8,16},{9,... | collective-permute-start | bytes 147464 | tf_op jit(solution)/shard_map/ppermute | solution.py:512
  22.9 2.3 %primal_products.1 = (f32[8,256,128]{2,1,0:T(8,128)S(1)}, f32[8,256,128]{2,1,0:T(8,128)S(1)}, f32[8,256,128]{2,1,0:T(8,128)S(1)}) custom-call(f32[8,256,128]{2,1,0:T(8,128)S(1)} %get-tuple-element.24.rx, f32[8,256,128]{2,1,0:T(8,128)S(1)} %get-tuple-element.25.ry, f32[3,8,256,128]{3,2,1,0:T(8,128)S(1)} %get-tuple-element.26.h, ...), custom_call_target="tpu_custom_call" | custom-call | flops 1000 | bytes 12000000 | tf_op jit(solution)/shard_map/primal_products/pallas_call | solution.py:577
  25.2 1.3 %collective-permute-done.5.n3 = f32[12,8,128]{2,1,0:T(8,128)S(1)} collective-permute-done((f32[12,8,128]{2,1,0:T(8,128)S(1)}, f32[12,8,128]{2,1,0:T(8,128)S(1)}, u32[]{:S(2)}, u32[]{:S(2)}) %collective-permute-start.5) | collective-permute-done | bytes 49184 | tf_op jit(solution)/shard_map/ppermute | solution.py:512
  26.7 3.0 %collective-permute-start.7 = (f32[12,8,128]{2,1,0:T(8,128)S(1)}, f32[12,8,128]{2,1,0:T(8,128)S(1)}, u32[]{:S(2)}, u32[]{:S(2)}) collective-permute-start(f32[12,8,128]{2,1,0:T(8,128)S(1)} %get-tuple-element.41), channel_id=1, source_target_pairs={{0,1},{1,0},{2,3},{3,2},{4,5},{5,4},{6,7},{7,6},{8,9},{9,8},{10,11... | collective-permute-start | bytes 147464 | tf_op jit(solution)/shard_map/ppermute | solution.py:512
  29.7 0.9 %collective-permute-done.7.recv.refs_6_ = f32[12,8,128]{2,1,0:T(8,128)S(1)} collective-permute-done((f32[12,8,128]{2,1,0:T(8,128)S(1)}, f32[12,8,128]{2,1,0:T(8,128)S(1)}, u32[]{:S(2)}, u32[]{:S(2)}) %collective-permute-start.7) | collective-permute-done | bytes 49184 | tf_op jit(solution)/shard_map/ppermute | solution.py:512
  31.1 1.4 %collective-permute-start.8 = (f32[2,256,128]{2,1,0:T(8,128)S(1)}, f32[2,256,128]{2,1,0:T(8,128)S(1)}, u32[]{:S(2)}, u32[]{:S(2)}) collective-permute-start(f32[2,256,128]{2,1,0:T(8,128)S(1)} %gradient_1.1), channel_id=1, source_target_pairs={{0,32},{32,0},{64,96},{96,64},{1,33},{33,1},{65,97},{97,65},{2,34}... | collective-permute-start | bytes 786440 | tf_op jit(solution)/shard_map/ppermute | solution.py:512
  32.9 2.7 %collective-permute-start.9 = (f32[2,256,128]{2,1,0:T(8,128)S(1)}, f32[2,256,128]{2,1,0:T(8,128)S(1)}, u32[]{:S(2)}, u32[]{:S(2)}) collective-permute-start(f32[2,256,128]{2,1,0:T(8,128)S(1)} %gradient_2.1), channel_id=1, source_target_pairs={{0,64},{32,96},{64,0},{96,32},{1,65},{33,97},{65,1},{97,33},{2,66}... | collective-permute-start | bytes 786440 | tf_op jit(solution)/shard_map/ppermute | solution.py:512
  36.6 2.0 %collective-permute-done.8 = f32[2,256,128]{2,1,0:T(8,128)S(1)} collective-permute-done((f32[2,256,128]{2,1,0:T(8,128)S(1)}, f32[2,256,128]{2,1,0:T(8,128)S(1)}, u32[]{:S(2)}, u32[]{:S(2)}) %collective-permute-start.8) | collective-permute-done | bytes 262176 | tf_op jit(solution)/shard_map/ppermute | solution.py:512
  38.7 8.1 %collective-permute-done.9 = f32[2,256,128]{2,1,0:T(8,128)S(1)} collective-permute-done((f32[2,256,128]{2,1,0:T(8,128)S(1)}, f32[2,256,128]{2,1,0:T(8,128)S(1)}, u32[]{:S(2)}, u32[]{:S(2)}) %collective-permute-start.9) | collective-permute-done | bytes 262176 | tf_op jit(solution)/shard_map/ppermute | solution.py:512
  46.8 3.2 %collective-permute-done.10 = f32[2,256,128]{2,1,0:T(8,128)S(1)} collective-permute-done((f32[2,256,128]{2,1,0:T(8,128)S(1)}, f32[2,256,128]{2,1,0:T(8,128)S(1)}, u32[]{:S(2)}, u32[]{:S(2)}) %collective-permute-start.10) | collective-permute-done | bytes 262176 | tf_op jit(solution)/shard_map/ppermute | solution.py:512
  50.2 1.3 %collective-permute-start.12 = (f32[2,256,128]{2,1,0:T(8,128)S(1)}, f32[2,256,128]{2,1,0:T(8,128)S(1)}, u32[]{:S(2)}, u32[]{:S(2)}) collective-permute-start(f32[2,256,128]{2,1,0:T(8,128)S(1)} %add_add_fusion.g0), channel_id=1, source_target_pairs={{0,64},{32,96},{64,0},{96,32},{1,65},{33,97},{65,1},{97,33},{2,66}... | collective-permute-start | bytes 786440 | tf_op jit(solution)/shard_map/ppermute | solution.py:512
  51.4 2.6 %collective-permute-start.13 = (f32[2,256,128]{2,1,0:T(8,128)S(1)}, f32[2,256,128]{2,1,0:T(8,128)S(1)}, u32[]{:S(2)}, u32[]{:S(2)}) collective-permute-start(f32[2,256,128]{2,1,0:T(8,128)S(1)} %add_add_fusion.g0), channel_id=1, source_target_pairs={{0,96},{32,64},{64,32},{96,0},{1,97},{33,65},{65,33},{97,1},{2,98}... | collective-permute-start | bytes 786440 | tf_op jit(solution)/shard_map/ppermute | solution.py:512
  54.0 3.4 %outputs.1 = (f32[3,8,256,128]{3,2,1,0:T(8,128)}, f32[3,8,256,128]{3,2,1,0:T(8,128)}) custom-call(f32[8,256,128]{2,1,0:T(8,128)S(1)} %get-tuple-element.37.after.ex, f32[8,256,128]{2,1,0:T(8,128)S(1)} %get-tuple-element.38.ey, f32[3,8,256,128]{3,2,1,0:T(8,128)S(1)} %get-tuple-element.26.h, f32[8,256,128]{2,1,0:T(8,128)S(1)} %get-tuple-element.34.ez, ...), custom_call_target="tpu_custom_call" | custom-call | flops 1000 | bytes 18000000 | tf_op jit(solution)/shard_map/outputs/pallas_call | solution.py:594
  57.4 4.4 %collective-permute-done.12.g2 = f32[2,256,128]{2,1,0:T(8,128)S(1)} collective-permute-done((f32[2,256,128]{2,1,0:T(8,128)S(1)}, f32[2,256,128]{2,1,0:T(8,128)S(1)}, u32[]{:S(2)}, u32[]{:S(2)}) %collective-permute-start.12) | collective-permute-done | bytes 262176 | tf_op jit(solution)/shard_map/ppermute | solution.py:512
  61.8 3.0 %collective-permute-done.13.g3 = f32[2,256,128]{2,1,0:T(8,128)S(1)} collective-permute-done((f32[2,256,128]{2,1,0:T(8,128)S(1)}, f32[2,256,128]{2,1,0:T(8,128)S(1)}, u32[]{:S(2)}, u32[]{:S(2)}) %collective-permute-start.13) | collective-permute-done | bytes 262176 | tf_op jit(solution)/shard_map/ppermute | solution.py:512
  64.8 1.0 %place.1 = f32[8,256,128]{2,1,0:T(8,128)} custom-call(f32[2,256,128]{2,1,0:T(8,128)S(1)} %collective-permute-done.11.g1, f32[2,256,128]{2,1,0:T(8,128)S(1)} %collective-permute-done.12.g2, f32[2,256,128]{2,1,0:T(8,128)S(1)} %collective-permute-done.13.g3, f32[2,256,128]{2,1,0:T(8,128)S(1)} %add_add_fusion.g0), custom_call_target="tpu_custom_call" | custom-call | flops 1000 | bytes 3000000 | tf_op jit(solution)/shard_map/place/pallas_call | solution.py:602
  (17 shorter events, 2.4 us)
Async XLA Ops:
  8.4 2.4 %collective-permute-start = (f32[12,8,128]{2,1,0:T(8,128)S(1)}, f32[12,8,128]{2,1,0:T(8,128)S(1)}, u32[]{:S(2)}, u32[]{:S(2)}) collective-permute-start(f32[12,8,128]{2,1,0:T(8,128)S(1)} %get-tuple-element.33), channel_id=1, source_target_pairs={{0,1},{1,0},{2,3},{3,2},{4,5},{5,4},{6,7},{7,6},{8,9},{9,8},{10,11... | collective-permute-start | bytes 147464 | tf_op jit(solution)/shard_map/ppermute | solution.py:512
  10.8 6.4 %collective-permute-start.1 = (f32[12,8,128]{2,1,0:T(8,128)S(1)}, f32[12,8,128]{2,1,0:T(8,128)S(1)}, u32[]{:S(2)}, u32[]{:S(2)}) collective-permute-start(f32[12,8,128]{2,1,0:T(8,128)S(1)} %chip.1.after.m0), channel_id=1, source_target_pairs={{0,6},{1,7},{2,4},{3,5},{4,2},{5,3},{6,0},{7,1},{8,14},{9,15},{10,... | collective-permute-start | bytes 147464 | tf_op jit(solution)/shard_map/ppermute | solution.py:512
  14.7 4.4 %collective-permute-start.2 = (f32[12,8,128]{2,1,0:T(8,128)S(1)}, f32[12,8,128]{2,1,0:T(8,128)S(1)}, u32[]{:S(2)}, u32[]{:S(2)}) collective-permute-start(f32[12,8,128]{2,1,0:T(8,128)S(1)} %chip.1.after.m0), channel_id=1, source_target_pairs={{0,4},{1,5},{2,6},{3,7},{4,0},{5,1},{6,2},{7,3},{8,12},{9,13},{10,... | collective-permute-start | bytes 147464 | tf_op jit(solution)/shard_map/ppermute | solution.py:512
  14.7 4.4 %collective-permute-start.3 = (f32[12,8,128]{2,1,0:T(8,128)S(1)}, f32[12,8,128]{2,1,0:T(8,128)S(1)}, u32[]{:S(2)}, u32[]{:S(2)}) collective-permute-start(f32[12,8,128]{2,1,0:T(8,128)S(1)} %chip.1.after.m0), channel_id=1, source_target_pairs={{0,2},{1,3},{2,0},{3,1},{4,6},{5,7},{6,4},{7,5},{8,10},{9,11},{10,... | collective-permute-start | bytes 147464 | tf_op jit(solution)/shard_map/ppermute | solution.py:512
  19.3 6.0 %collective-permute-start.4 = (f32[12,8,128]{2,1,0:T(8,128)S(1)}, f32[12,8,128]{2,1,0:T(8,128)S(1)}, u32[]{:S(2)}, u32[]{:S(2)}) collective-permute-start(f32[12,8,128]{2,1,0:T(8,128)S(1)} %group.1.after.n0), channel_id=1, source_target_pairs={{0,16},{1,17},{2,18},{3,19},{4,20},{5,21},{6,22},{7,23},{8,24},{9,... | collective-permute-start | bytes 147464 | tf_op jit(solution)/shard_map/ppermute | solution.py:512
  22.1 4.5 %collective-permute-start.5 = (f32[12,8,128]{2,1,0:T(8,128)S(1)}, f32[12,8,128]{2,1,0:T(8,128)S(1)}, u32[]{:S(2)}, u32[]{:S(2)}) collective-permute-start(f32[12,8,128]{2,1,0:T(8,128)S(1)} %group.1.after.n0), channel_id=1, source_target_pairs={{0,24},{1,25},{2,26},{3,27},{4,28},{5,29},{6,30},{7,31},{8,16},{9,... | collective-permute-start | bytes 147464 | tf_op jit(solution)/shard_map/ppermute | solution.py:512
  22.9 3.6 %collective-permute-start.6 = (f32[12,8,128]{2,1,0:T(8,128)S(1)}, f32[12,8,128]{2,1,0:T(8,128)S(1)}, u32[]{:S(2)}, u32[]{:S(2)}) collective-permute-start(f32[12,8,128]{2,1,0:T(8,128)S(1)} %group.1.after.n0), channel_id=1, source_target_pairs={{0,8},{1,9},{2,10},{3,11},{4,12},{5,13},{6,14},{7,15},{8,0},{9,1},... | collective-permute-start | bytes 147464 | tf_op jit(solution)/shard_map/ppermute | solution.py:512
  26.7 3.9 %collective-permute-start.7 = (f32[12,8,128]{2,1,0:T(8,128)S(1)}, f32[12,8,128]{2,1,0:T(8,128)S(1)}, u32[]{:S(2)}, u32[]{:S(2)}) collective-permute-start(f32[12,8,128]{2,1,0:T(8,128)S(1)} %get-tuple-element.41), channel_id=1, source_target_pairs={{0,1},{1,0},{2,3},{3,2},{4,5},{5,4},{6,7},{7,6},{8,9},{9,8},{10,11... | collective-permute-start | bytes 147464 | tf_op jit(solution)/shard_map/ppermute | solution.py:512
  31.1 7.6 %collective-permute-start.8 = (f32[2,256,128]{2,1,0:T(8,128)S(1)}, f32[2,256,128]{2,1,0:T(8,128)S(1)}, u32[]{:S(2)}, u32[]{:S(2)}) collective-permute-start(f32[2,256,128]{2,1,0:T(8,128)S(1)} %gradient_1.1), channel_id=1, source_target_pairs={{0,32},{32,0},{64,96},{96,64},{1,33},{33,1},{65,97},{97,65},{2,34}... | collective-permute-start | bytes 786440 | tf_op jit(solution)/shard_map/ppermute | solution.py:512
  32.9 13.9 %collective-permute-start.9 = (f32[2,256,128]{2,1,0:T(8,128)S(1)}, f32[2,256,128]{2,1,0:T(8,128)S(1)}, u32[]{:S(2)}, u32[]{:S(2)}) collective-permute-start(f32[2,256,128]{2,1,0:T(8,128)S(1)} %gradient_2.1), channel_id=1, source_target_pairs={{0,64},{32,96},{64,0},{96,32},{1,65},{33,97},{65,1},{97,33},{2,66}... | collective-permute-start | bytes 786440 | tf_op jit(solution)/shard_map/ppermute | solution.py:512
  36.1 14.0 %collective-permute-start.10 = (f32[2,256,128]{2,1,0:T(8,128)S(1)}, f32[2,256,128]{2,1,0:T(8,128)S(1)}, u32[]{:S(2)}, u32[]{:S(2)}) collective-permute-start(f32[2,256,128]{2,1,0:T(8,128)S(1)} %gradient_3.1), channel_id=1, source_target_pairs={{0,96},{32,64},{64,32},{96,0},{1,97},{33,65},{65,33},{97,1},{2,98}... | collective-permute-start | bytes 786440 | tf_op jit(solution)/shard_map/ppermute | solution.py:512
  50.1 7.3 %collective-permute-start.11 = (f32[2,256,128]{2,1,0:T(8,128)S(1)}, f32[2,256,128]{2,1,0:T(8,128)S(1)}, u32[]{:S(2)}, u32[]{:S(2)}) collective-permute-start(f32[2,256,128]{2,1,0:T(8,128)S(1)} %add_add_fusion.g0), channel_id=1, source_target_pairs={{0,32},{32,0},{64,96},{96,64},{1,33},{33,1},{65,97},{97,65},{2,34}... | collective-permute-start | bytes 786440 | tf_op jit(solution)/shard_map/ppermute | solution.py:512
  50.2 11.7 %collective-permute-start.12 = (f32[2,256,128]{2,1,0:T(8,128)S(1)}, f32[2,256,128]{2,1,0:T(8,128)S(1)}, u32[]{:S(2)}, u32[]{:S(2)}) collective-permute-start(f32[2,256,128]{2,1,0:T(8,128)S(1)} %add_add_fusion.g0), channel_id=1, source_target_pairs={{0,64},{32,96},{64,0},{96,32},{1,65},{33,97},{65,1},{97,33},{2,66}... | collective-permute-start | bytes 786440 | tf_op jit(solution)/shard_map/ppermute | solution.py:512
  51.4 13.4 %collective-permute-start.13 = (f32[2,256,128]{2,1,0:T(8,128)S(1)}, f32[2,256,128]{2,1,0:T(8,128)S(1)}, u32[]{:S(2)}, u32[]{:S(2)}) collective-permute-start(f32[2,256,128]{2,1,0:T(8,128)S(1)} %add_add_fusion.g0), channel_id=1, source_target_pairs={{0,96},{32,64},{64,32},{96,0},{1,97},{33,65},{65,33},{97,1},{2,98}... | collective-permute-start | bytes 786440 | tf_op jit(solution)/shard_map/ppermute | solution.py:512

commit v11 on v9

--- a/solution.py
+++ b/solution.py
@@ -216,7 +216,7 @@
         put(send_o, False)
         return carry
 
-    lax.fori_loop(0, X // 2, one_pair, 0)
+    lax.fori_loop(0, X // 2, one_pair, 0, unroll=True)
 
 
 def unpack(ref):
@@ -497,17 +497,26 @@
             copy.wait()
 
 
-def place_kernel(g2, g3, g1, g0, out, sems):
+def place(masks, quarters, out, sems):
     src = lax.axis_index("src")
-    copies = []
-    for k, g in zip((2, 1, 3, 0), (g2, g1, g3, g0)):
-        copies.append(pltpu.make_async_copy(g, out.at[pl.ds(2 * (src ^ k), 2)], sems.at[k]))
+    copies = [
+        pltpu.make_async_copy(g, out.at[pl.ds(2 * (src ^ k), 2)], sems.at[n])
+        for n, (k, g) in enumerate(zip(masks, quarters))
+    ]
     for copy in copies:
         copy.start()
     for copy in copies:
         copy.wait()
 
 
+def place_first(g0, g2, out, sems):
+    place((0, 2), (g0, g2), out, sems)
+
+
+def place_rest(g3, g1, partial, out, sems):
+    place((3, 1), (g3, g1), out, sems)
+
+
 def swap(block, axis, mask):
     return lax.ppermute(block, axis, [(i, i ^ mask) for i in range(lax.axis_size(axis))])
 
@@ -522,13 +531,14 @@
     return jax.ShapeDtypeStruct(dims, F32)
 
 
-def call(kernel, name, in_specs, outs, us, mib, out_specs=None, scratch=()):
+def call(kernel, name, in_specs, outs, us, mib, out_specs=None, scratch=(), aliases=None):
     return pl.pallas_call(
         kernel,
         in_specs=in_specs,
         out_specs=out_specs or [VMEM] * len(outs),
         out_shape=outs,
         scratch_shapes=scratch,
+        input_output_aliases=aliases or {},
         compiler_params=pltpu.CompilerParams(vmem_limit_bytes=mib * MIB),
         cost_estimate=pl.CostEstimate(flops=1000, bytes_accessed=int(us * 3.0e6), transcendentals=0),
         name=name,
@@ -599,10 +609,14 @@
 
     total = own + arrived[0] + arrived[1] + arrived[2]
     two, three, one = (swap(total, "src", k) for k in (2, 3, 1))
+    (partial,) = call(
+        place_first, "place_first", [ANY] * 2, [slab], 1, 4, out_specs=[HBM],
+        scratch=[pltpu.SemaphoreType.DMA((2,))],
+    )(total, two)
     (eps_grad,) = call(
-        place_kernel, "place", [ANY] * 4, [slab], 1, 4, out_specs=[HBM],
-        scratch=[pltpu.SemaphoreType.DMA((4,))],
-    )(two, three, one, total)
+        place_rest, "place_rest", [ANY] * 2 + [HBM], [slab], 1, 4, out_specs=[HBM],
+        scratch=[pltpu.SemaphoreType.DMA((2,))], aliases={2: 0},
+    )(three, one, partial)
     return (e_new[None], h_new[None], eps_grad)
 
 

time: 63.4 us -> 63 us (level)
  waiting for transfers between devices: 23.4 us -> 22.5 us
    ppermute x14, waiting for transfers between devices: 23.4 us -> 22.5 us  [swap(): lax.ppermute(block, axis, [(i, i ^ mask) for i in range(lax.axis_size(axi...]
    pallas_call x1 -> x2, Pallas kernels: 1 us -> 1.61 us  [the longest x1 0.81 us: body(): call(place_rest, 'place_rest', [ANY] * 2 + [HBM], [slab], 1, 4, out_specs...]
  transfers between devices with their start and end apart: 14 -> 14, of which waited for: 8 -> 8; matrix products, arithmetic and copies ran while one was open for 0% -> 0% of each run, Pallas kernels for 14% -> 15%
where the time goes in v11:
time: 63 us; the launch traced here: 62.8 us
  waiting for transfers between devices  22.5 us (36%)
  starting transfers between devices  20.5 us (33%)
  Pallas kernels  18.3 us (29%)
  between operations  1.4 us (2%)
    ppermute x14, waiting for transfers between devices, swap(): lax.ppermute(block, axis, [(i, i ^ mask) for i in range(lax.axis_size(axi...  22.5 us
    ppermute x14, starting transfers between devices, swap(): lax.ppermute(block, axis, [(i, i ^ mask) for i in range(lax.axis_size(axi...  20.5 us
    pallas_call x1, Pallas kernels, body(): call(rhs_kernel, 'right_hand_sides', [SMEM, SMEM] + [HBM] * 9, [slab] * 8...  7.11 us
    pallas_call x1, Pallas kernels, body(): call(output_kernel, 'outputs', [VMEM] * 8, [shape(3, X, Y, CZ)] * 2, 6, 1...  3.4 us
    pallas_call x1, Pallas kernels, body(): call(primal_kernel, 'primal_products', [VMEM] * 7 + [ANY], [slab] * 3, 4, 8)  2.25 us
    pallas_call x4, Pallas kernels, gradient(): call(lambda *refs: gradient_kernel(k, *refs), f'gradient_{k}', [VMEM] * 8...  1.84 us
    pallas_call x1, Pallas kernels, body(): call(adjoint_kernel, 'adjoint_products', [VMEM] * 5 + [HBM, ANY], [slab]...  1.84 us
  transfers between devices with their start and end apart: 14, of which 8 were waited for; matrix products, arithmetic and copies ran while one was open for 0% of the time, Pallas kernels for 15%

profile of v11, /device:TPU:1, one launch (start us, length us, event | category | flops | bytes accessed | tf_op | source)
XLA Modules:
  0.0 62.8 jit_solution(14190969007195542826)
XLA Ops:
  1.3 7.1 %right_hand_sides.1 = (f32[8,256,128]{2,1,0:T(8,128)S(1)}, f32[8,256,128]{2,1,0:T(8,128)S(1)}, f32[8,256,128]{2,1,0:T(8,128)S(1)}, f32[8,256,128]{2,1,0:T(8,128)...) custom-call(s32[1]{0:T(128)S(6)} %copy.16.angle, ...), custom_call_target="tpu_custom_call" | custom-call | flops 1000 | bytes 18000000 | tf_op jit(solution)/shard_map/right_hand_sides/pallas_call | solution.py:564
  8.4 1.5 %collective-permute-start = (f32[12,8,128]{2,1,0:T(8,128)S(1)}, f32[12,8,128]{2,1,0:T(8,128)S(1)}, u32[]{:S(2)}, u32[]{:S(2)}) collective-permute-start(f32[12,8,128]{2,1,0:T(8,128)S(1)} %get-tuple-element.33), channel_id=1, source_target_pairs={{0,1},{1,0},{2,3},{3,2},{4,5},{5,4},{6,7},{7,6},{8,9},{9,8},{10,11... | collective-permute-start | bytes 147464 | tf_op jit(solution)/shard_map/ppermute | solution.py:521
  9.9 0.9 %collective-permute-done.other.a1 = f32[12,8,128]{2,1,0:T(8,128)S(1)} collective-permute-done((f32[12,8,128]{2,1,0:T(8,128)S(1)}, f32[12,8,128]{2,1,0:T(8,128)S(1)}, u32[]{:S(2)}, u32[]{:S(2)}) %collective-permute-start) | collective-permute-done | bytes 49184 | tf_op jit(solution)/shard_map/ppermute | solution.py:521
  10.8 3.9 %collective-permute-start.1 = (f32[12,8,128]{2,1,0:T(8,128)S(1)}, f32[12,8,128]{2,1,0:T(8,128)S(1)}, u32[]{:S(2)}, u32[]{:S(2)}) collective-permute-start(f32[12,8,128]{2,1,0:T(8,128)S(1)} %chip.1.after.m0), channel_id=1, source_target_pairs={{0,6},{1,7},{2,4},{3,5},{4,2},{5,3},{6,0},{7,1},{8,14},{9,15},{10,... | collective-permute-start | bytes 147464 | tf_op jit(solution)/shard_map/ppermute | solution.py:521
  14.7 0.7 %collective-permute-start.3 = (f32[12,8,128]{2,1,0:T(8,128)S(1)}, f32[12,8,128]{2,1,0:T(8,128)S(1)}, u32[]{:S(2)}, u32[]{:S(2)}) collective-permute-start(f32[12,8,128]{2,1,0:T(8,128)S(1)} %chip.1.after.m0), channel_id=1, source_target_pairs={{0,2},{1,3},{2,0},{3,1},{4,6},{5,7},{6,4},{7,5},{8,10},{9,11},{10,... | collective-permute-start | bytes 147464 | tf_op jit(solution)/shard_map/ppermute | solution.py:521
  15.4 1.8 %adjoint_products.1 = (f32[8,256,128]{2,1,0:T(8,128)S(1)}, f32[8,256,128]{2,1,0:T(8,128)S(1)}) custom-call(f32[8,256,128]{2,1,0:T(8,128)S(1)} %get-tuple-element.27.ax, f32[8,256,128]{2,1,0:T(8,128)S(1)} %get-tuple-element.28.ay, f32[8,256,128]{2,1,0:T(8,128)S(1)} %get-tuple-element.29.psx.refs_1_, f32[8,256,128]{2,1,0:T(8,128)S(1)} %get-tuple-element.30.psy.refs_2_, ...), custom_call_target="tpu_custom_call" | custom-call | flops 1000 | bytes 9000000 | tf_op jit(solution)/shard_map/adjoint_products/pallas_call | solution.py:580
  17.3 1.9 %collective-permute-done.2.m2 = f32[12,8,128]{2,1,0:T(8,128)S(1)} collective-permute-done((f32[12,8,128]{2,1,0:T(8,128)S(1)}, f32[12,8,128]{2,1,0:T(8,128)S(1)}, u32[]{:S(2)}, u32[]{:S(2)}) %collective-permute-start.2) | collective-permute-done | bytes 49184 | tf_op jit(solution)/shard_map/ppermute | solution.py:521
  19.3 2.8 %collective-permute-start.4 = (f32[12,8,128]{2,1,0:T(8,128)S(1)}, f32[12,8,128]{2,1,0:T(8,128)S(1)}, u32[]{:S(2)}, u32[]{:S(2)}) collective-permute-start(f32[12,8,128]{2,1,0:T(8,128)S(1)} %group.1.after.n0), channel_id=1, source_target_pairs={{0,16},{1,17},{2,18},{3,19},{4,20},{5,21},{6,22},{7,23},{8,24},{9,... | collective-permute-start | bytes 147464 | tf_op jit(solution)/shard_map/ppermute | solution.py:521
  22.1 0.9 %collective-permute-start.5 = (f32[12,8,128]{2,1,0:T(8,128)S(1)}, f32[12,8,128]{2,1,0:T(8,128)S(1)}, u32[]{:S(2)}, u32[]{:S(2)}) collective-permute-start(f32[12,8,128]{2,1,0:T(8,128)S(1)} %group.1.after.n0), channel_id=1, source_target_pairs={{0,24},{1,25},{2,26},{3,27},{4,28},{5,29},{6,30},{7,31},{8,16},{9,... | collective-permute-start | bytes 147464 | tf_op jit(solution)/shard_map/ppermute | solution.py:521
  22.9 2.3 %primal_products.1 = (f32[8,256,128]{2,1,0:T(8,128)S(1)}, f32[8,256,128]{2,1,0:T(8,128)S(1)}, f32[8,256,128]{2,1,0:T(8,128)S(1)}) custom-call(f32[8,256,128]{2,1,0:T(8,128)S(1)} %get-tuple-element.24.rx, f32[8,256,128]{2,1,0:T(8,128)S(1)} %get-tuple-element.25.ry, f32[3,8,256,128]{3,2,1,0:T(8,128)S(1)} %get-tuple-element.26.h, ...), custom_call_target="tpu_custom_call" | custom-call | flops 1000 | bytes 12000000 | tf_op jit(solution)/shard_map/primal_products/pallas_call | solution.py:587
  25.2 1.3 %collective-permute-done.5.n3 = f32[12,8,128]{2,1,0:T(8,128)S(1)} collective-permute-done((f32[12,8,128]{2,1,0:T(8,128)S(1)}, f32[12,8,128]{2,1,0:T(8,128)S(1)}, u32[]{:S(2)}, u32[]{:S(2)}) %collective-permute-start.5) | collective-permute-done | bytes 49184 | tf_op jit(solution)/shard_map/ppermute | solution.py:521
  26.7 3.0 %collective-permute-start.7 = (f32[12,8,128]{2,1,0:T(8,128)S(1)}, f32[12,8,128]{2,1,0:T(8,128)S(1)}, u32[]{:S(2)}, u32[]{:S(2)}) collective-permute-start(f32[12,8,128]{2,1,0:T(8,128)S(1)} %get-tuple-element.41), channel_id=1, source_target_pairs={{0,1},{1,0},{2,3},{3,2},{4,5},{5,4},{6,7},{7,6},{8,9},{9,8},{10,11... | collective-permute-start | bytes 147464 | tf_op jit(solution)/shard_map/ppermute | solution.py:521
  29.7 0.9 %collective-permute-done.7.recv.refs_6_ = f32[12,8,128]{2,1,0:T(8,128)S(1)} collective-permute-done((f32[12,8,128]{2,1,0:T(8,128)S(1)}, f32[12,8,128]{2,1,0:T(8,128)S(1)}, u32[]{:S(2)}, u32[]{:S(2)}) %collective-permute-start.7) | collective-permute-done | bytes 49184 | tf_op jit(solution)/shard_map/ppermute | solution.py:521
  31.1 3.0 %collective-permute-start.8 = (f32[2,256,128]{2,1,0:T(8,128)S(1)}, f32[2,256,128]{2,1,0:T(8,128)S(1)}, u32[]{:S(2)}, u32[]{:S(2)}) collective-permute-start(f32[2,256,128]{2,1,0:T(8,128)S(1)} %gradient_2.1), channel_id=1, source_target_pairs={{0,64},{32,96},{64,0},{96,32},{1,65},{33,97},{65,1},{97,33},{2,66}... | collective-permute-start | bytes 786440 | tf_op jit(solution)/shard_map/ppermute | solution.py:521
  34.5 0.9 %collective-permute-start.9 = (f32[2,256,128]{2,1,0:T(8,128)S(1)}, f32[2,256,128]{2,1,0:T(8,128)S(1)}, u32[]{:S(2)}, u32[]{:S(2)}) collective-permute-start(f32[2,256,128]{2,1,0:T(8,128)S(1)} %gradient_3.1), channel_id=1, source_target_pairs={{0,96},{32,64},{64,32},{96,0},{1,97},{33,65},{65,33},{97,1},{2,98}... | collective-permute-start | bytes 786440 | tf_op jit(solution)/shard_map/ppermute | solution.py:521
  36.4 3.8 %collective-permute-done.8 = f32[2,256,128]{2,1,0:T(8,128)S(1)} collective-permute-done((f32[2,256,128]{2,1,0:T(8,128)S(1)}, f32[2,256,128]{2,1,0:T(8,128)S(1)}, u32[]{:S(2)}, u32[]{:S(2)}) %collective-permute-start.8) | collective-permute-done | bytes 262176 | tf_op jit(solution)/shard_map/ppermute | solution.py:521
  40.2 6.3 %collective-permute-done.9 = f32[2,256,128]{2,1,0:T(8,128)S(1)} collective-permute-done((f32[2,256,128]{2,1,0:T(8,128)S(1)}, f32[2,256,128]{2,1,0:T(8,128)S(1)}, u32[]{:S(2)}, u32[]{:S(2)}) %collective-permute-start.9) | collective-permute-done | bytes 262176 | tf_op jit(solution)/shard_map/ppermute | solution.py:521
  46.5 2.5 %collective-permute-start.13 = (f32[2,256,128]{2,1,0:T(8,128)S(1)}, f32[2,256,128]{2,1,0:T(8,128)S(1)}, u32[]{:S(2)}, u32[]{:S(2)}) collective-permute-start(f32[2,256,128]{2,1,0:T(8,128)S(1)} %add_add_fusion.g0), channel_id=1, source_target_pairs={{0,64},{32,96},{64,0},{96,32},{1,65},{33,97},{65,1},{97,33},{2,66}... | collective-permute-start | bytes 786440 | tf_op jit(solution)/shard_map/ppermute | solution.py:521
  49.1 1.2 %collective-permute-start.11 = (f32[2,256,128]{2,1,0:T(8,128)S(1)}, f32[2,256,128]{2,1,0:T(8,128)S(1)}, u32[]{:S(2)}, u32[]{:S(2)}) collective-permute-start(f32[2,256,128]{2,1,0:T(8,128)S(1)} %add_add_fusion.g0), channel_id=1, source_target_pairs={{0,96},{32,64},{64,32},{96,0},{1,97},{33,65},{65,33},{97,1},{2,98}... | collective-permute-start | bytes 786440 | tf_op jit(solution)/shard_map/ppermute | solution.py:521
  50.3 3.4 %outputs.1 = (f32[3,8,256,128]{3,2,1,0:T(8,128)}, f32[3,8,256,128]{3,2,1,0:T(8,128)}) custom-call(f32[8,256,128]{2,1,0:T(8,128)S(1)} %get-tuple-element.37.after.ex, f32[8,256,128]{2,1,0:T(8,128)S(1)} %get-tuple-element.38.ey, f32[3,8,256,128]{3,2,1,0:T(8,128)S(1)} %get-tuple-element.26.h, f32[8,256,128]{2,1,0:T(8,128)S(1)} %get-tuple-element.34.ez, ...), custom_call_target="tpu_custom_call" | custom-call | flops 1000 | bytes 18000000 | tf_op jit(solution)/shard_map/outputs/pallas_call | solution.py:604
  53.7 1.4 %collective-permute-done.13.g2 = f32[2,256,128]{2,1,0:T(8,128)S(1)} collective-permute-done((f32[2,256,128]{2,1,0:T(8,128)S(1)}, f32[2,256,128]{2,1,0:T(8,128)S(1)}, u32[]{:S(2)}, u32[]{:S(2)}) %collective-permute-start.13) | collective-permute-done | bytes 262176 | tf_op jit(solution)/shard_map/ppermute | solution.py:521
  55.1 0.8 %place_first.1.partial = f32[8,256,128]{2,1,0:T(8,128)} custom-call(f32[2,256,128]{2,1,0:T(8,128)S(1)} %add_add_fusion.g0, f32[2,256,128]{2,1,0:T(8,128)S(1)} %collective-permute-done.13.g2), custom_call_target="tpu_custom_call" | custom-call | flops 1000 | bytes 3000000 | tf_op jit(solution)/shard_map/place_first/pallas_call | solution.py:612
  55.9 6.0 %collective-permute-done.11.g3 = f32[2,256,128]{2,1,0:T(8,128)S(1)} collective-permute-done((f32[2,256,128]{2,1,0:T(8,128)S(1)}, f32[2,256,128]{2,1,0:T(8,128)S(1)}, u32[]{:S(2)}, u32[]{:S(2)}) %collective-permute-start.11) | collective-permute-done | bytes 262176 | tf_op jit(solution)/shard_map/ppermute | solution.py:521
  62.0 0.8 %place_rest.1 = f32[8,256,128]{2,1,0:T(8,128)} custom-call(f32[2,256,128]{2,1,0:T(8,128)S(1)} %collective-permute-done.11.g3, f32[2,256,128]{2,1,0:T(8,128)S(1)} %collective-permute-done.12.g1, f32[8,256,128]{2,1,0:T(8,128)} %place_first.1.partial), custom_call_target="tpu_custom_call", output_to_operand_aliasing={{}: (2, {})} | custom-call | flops 1000 | bytes 3000000 | tf_op jit(solution)/shard_map/place_rest/pallas_call | solution.py:616
  (18 shorter events, 2.3 us)
Async XLA Ops:
  8.4 2.4 %collective-permute-start = (f32[12,8,128]{2,1,0:T(8,128)S(1)}, f32[12,8,128]{2,1,0:T(8,128)S(1)}, u32[]{:S(2)}, u32[]{:S(2)}) collective-permute-start(f32[12,8,128]{2,1,0:T(8,128)S(1)} %get-tuple-element.33), channel_id=1, source_target_pairs={{0,1},{1,0},{2,3},{3,2},{4,5},{5,4},{6,7},{7,6},{8,9},{9,8},{10,11... | collective-permute-start | bytes 147464 | tf_op jit(solution)/shard_map/ppermute | solution.py:521
  10.8 6.4 %collective-permute-start.1 = (f32[12,8,128]{2,1,0:T(8,128)S(1)}, f32[12,8,128]{2,1,0:T(8,128)S(1)}, u32[]{:S(2)}, u32[]{:S(2)}) collective-permute-start(f32[12,8,128]{2,1,0:T(8,128)S(1)} %chip.1.after.m0), channel_id=1, source_target_pairs={{0,6},{1,7},{2,4},{3,5},{4,2},{5,3},{6,0},{7,1},{8,14},{9,15},{10,... | collective-permute-start | bytes 147464 | tf_op jit(solution)/shard_map/ppermute | solution.py:521
  14.7 4.4 %collective-permute-start.2 = (f32[12,8,128]{2,1,0:T(8,128)S(1)}, f32[12,8,128]{2,1,0:T(8,128)S(1)}, u32[]{:S(2)}, u32[]{:S(2)}) collective-permute-start(f32[12,8,128]{2,1,0:T(8,128)S(1)} %chip.1.after.m0), channel_id=1, source_target_pairs={{0,4},{1,5},{2,6},{3,7},{4,0},{5,1},{6,2},{7,3},{8,12},{9,13},{10,... | collective-permute-start | bytes 147464 | tf_op jit(solution)/shard_map/ppermute | solution.py:521
  14.7 4.4 %collective-permute-start.3 = (f32[12,8,128]{2,1,0:T(8,128)S(1)}, f32[12,8,128]{2,1,0:T(8,128)S(1)}, u32[]{:S(2)}, u32[]{:S(2)}) collective-permute-start(f32[12,8,128]{2,1,0:T(8,128)S(1)} %chip.1.after.m0), channel_id=1, source_target_pairs={{0,2},{1,3},{2,0},{3,1},{4,6},{5,7},{6,4},{7,5},{8,10},{9,11},{10,... | collective-permute-start | bytes 147464 | tf_op jit(solution)/shard_map/ppermute | solution.py:521
  19.3 6.0 %collective-permute-start.4 = (f32[12,8,128]{2,1,0:T(8,128)S(1)}, f32[12,8,128]{2,1,0:T(8,128)S(1)}, u32[]{:S(2)}, u32[]{:S(2)}) collective-permute-start(f32[12,8,128]{2,1,0:T(8,128)S(1)} %group.1.after.n0), channel_id=1, source_target_pairs={{0,16},{1,17},{2,18},{3,19},{4,20},{5,21},{6,22},{7,23},{8,24},{9,... | collective-permute-start | bytes 147464 | tf_op jit(solution)/shard_map/ppermute | solution.py:521
  22.1 4.5 %collective-permute-start.5 = (f32[12,8,128]{2,1,0:T(8,128)S(1)}, f32[12,8,128]{2,1,0:T(8,128)S(1)}, u32[]{:S(2)}, u32[]{:S(2)}) collective-permute-start(f32[12,8,128]{2,1,0:T(8,128)S(1)} %group.1.after.n0), channel_id=1, source_target_pairs={{0,24},{1,25},{2,26},{3,27},{4,28},{5,29},{6,30},{7,31},{8,16},{9,... | collective-permute-start | bytes 147464 | tf_op jit(solution)/shard_map/ppermute | solution.py:521
  22.9 3.6 %collective-permute-start.6 = (f32[12,8,128]{2,1,0:T(8,128)S(1)}, f32[12,8,128]{2,1,0:T(8,128)S(1)}, u32[]{:S(2)}, u32[]{:S(2)}) collective-permute-start(f32[12,8,128]{2,1,0:T(8,128)S(1)} %group.1.after.n0), channel_id=1, source_target_pairs={{0,8},{1,9},{2,10},{3,11},{4,12},{5,13},{6,14},{7,15},{8,0},{9,1},... | collective-permute-start | bytes 147464 | tf_op jit(solution)/shard_map/ppermute | solution.py:521
  26.7 3.9 %collective-permute-start.7 = (f32[12,8,128]{2,1,0:T(8,128)S(1)}, f32[12,8,128]{2,1,0:T(8,128)S(1)}, u32[]{:S(2)}, u32[]{:S(2)}) collective-permute-start(f32[12,8,128]{2,1,0:T(8,128)S(1)} %get-tuple-element.41), channel_id=1, source_target_pairs={{0,1},{1,0},{2,3},{3,2},{4,5},{5,4},{6,7},{7,6},{8,9},{9,8},{10,11... | collective-permute-start | bytes 147464 | tf_op jit(solution)/shard_map/ppermute | solution.py:521
  31.1 9.1 %collective-permute-start.8 = (f32[2,256,128]{2,1,0:T(8,128)S(1)}, f32[2,256,128]{2,1,0:T(8,128)S(1)}, u32[]{:S(2)}, u32[]{:S(2)}) collective-permute-start(f32[2,256,128]{2,1,0:T(8,128)S(1)} %gradient_2.1), channel_id=1, source_target_pairs={{0,64},{32,96},{64,0},{96,32},{1,65},{33,97},{65,1},{97,33},{2,66}... | collective-permute-start | bytes 786440 | tf_op jit(solution)/shard_map/ppermute | solution.py:521
  34.5 12.0 %collective-permute-start.9 = (f32[2,256,128]{2,1,0:T(8,128)S(1)}, f32[2,256,128]{2,1,0:T(8,128)S(1)}, u32[]{:S(2)}, u32[]{:S(2)}) collective-permute-start(f32[2,256,128]{2,1,0:T(8,128)S(1)} %gradient_3.1), channel_id=1, source_target_pairs={{0,96},{32,64},{64,32},{96,0},{1,97},{33,65},{65,33},{97,1},{2,98}... | collective-permute-start | bytes 786440 | tf_op jit(solution)/shard_map/ppermute | solution.py:521
  35.8 10.7 %collective-permute-start.10 = (f32[2,256,128]{2,1,0:T(8,128)S(1)}, f32[2,256,128]{2,1,0:T(8,128)S(1)}, u32[]{:S(2)}, u32[]{:S(2)}) collective-permute-start(f32[2,256,128]{2,1,0:T(8,128)S(1)} %gradient_1.1), channel_id=1, source_target_pairs={{0,32},{32,0},{64,96},{96,64},{1,33},{33,1},{65,97},{97,65},{2,34}... | collective-permute-start | bytes 786440 | tf_op jit(solution)/shard_map/ppermute | solution.py:521
  46.5 8.6 %collective-permute-start.13 = (f32[2,256,128]{2,1,0:T(8,128)S(1)}, f32[2,256,128]{2,1,0:T(8,128)S(1)}, u32[]{:S(2)}, u32[]{:S(2)}) collective-permute-start(f32[2,256,128]{2,1,0:T(8,128)S(1)} %add_add_fusion.g0), channel_id=1, source_target_pairs={{0,64},{32,96},{64,0},{96,32},{1,65},{33,97},{65,1},{97,33},{2,66}... | collective-permute-start | bytes 786440 | tf_op jit(solution)/shard_map/ppermute | solution.py:521
  49.1 12.9 %collective-permute-start.11 = (f32[2,256,128]{2,1,0:T(8,128)S(1)}, f32[2,256,128]{2,1,0:T(8,128)S(1)}, u32[]{:S(2)}, u32[]{:S(2)}) collective-permute-start(f32[2,256,128]{2,1,0:T(8,128)S(1)} %add_add_fusion.g0), channel_id=1, source_target_pairs={{0,96},{32,64},{64,32},{96,0},{1,97},{33,65},{65,33},{97,1},{2,98}... | collective-permute-start | bytes 786440 | tf_op jit(solution)/shard_map/ppermute | solution.py:521
  50.3 11.7 %collective-permute-start.12 = (f32[2,256,128]{2,1,0:T(8,128)S(1)}, f32[2,256,128]{2,1,0:T(8,128)S(1)}, u32[]{:S(2)}, u32[]{:S(2)}) collective-permute-start(f32[2,256,128]{2,1,0:T(8,128)S(1)} %add_add_fusion.g0), channel_id=1, source_target_pairs={{0,32},{32,0},{64,96},{96,64},{1,33},{33,1},{65,97},{97,65},{2,34}... | collective-permute-start | bytes 786440 | tf_op jit(solution)/shard_map/ppermute | solution.py:521
